TPU v7x, 32 devices: a whole 2x2x4 slice. The times are simulated.
32 devices in a mesh: segment: 4 (over z), frame: 4 (over y, x), row: 2 (over core).
Axes of the slice: x: 2, y: 2, z: 4, core: 2. Of those that a mesh axis runs over, the one named last changes fastest.
Arguments:
- clip_tokens: bfloat16 [4, 4, 2, 2, 64, 1536], P('segment', 'frame', 'row'), may hold values from -6 to 6
- qkv_weight: bfloat16 [4, 1536, 2304], P('segment'), may hold values from -1 to 1
- out_weight: bfloat16 [4, 768, 1536], P('segment'), may hold values from -0.21875 to 0.21875
- modulation: bfloat16 [4, 8, 3, 1536], P('segment'), may hold values from -4 to 4
- domain_ids: int32 [4], P('segment'), may hold values from 0 to 7
- tile_lists: int32 [4, 2, 2, 6], P('frame', 'row'), may hold values from 0 to 9, as said below
Outputs:
- handed: bfloat16 [4, 4, 2, 2, 64, 1536], P('segment', 'frame', 'row')
Inputs may be any that keep to these rules, and one draw needn't show every extreme that they name: `tile_lists`: each row names 6 different candidates, always the tile's own one, and never a tile outside the grid.
All inputs are finite; a program needn't handle non-finite values.
Results may differ from a plain program's by a relative error of at most 0.0081.
Values may be sent and summed in bfloat16 or wider, within the bound.
No kernel may reach another device: no remote copies, remote signals or barrier semaphores. Data moves between devices by JAX's collectives and lax.ppermute only.
A program may use at most 64 MiB of HBM per device.

v0:
```python
import jax
import jax.numpy as jnp
from jax import lax
from jax.sharding import PartitionSpec as P

HD = 128


epsilon = 1e-06


def extended_2(cells, sides, width):
    for axis, dim in sides:
        count = lax.axis_size(axis)
        ends = count - 1
        head = lax.slice_in_dim(cells, 0, width, axis=dim)
        tail = lax.slice_in_dim(cells, cells.shape[dim] - width, cells.shape[dim], axis=dim)
        cells = jnp.concatenate(
            [
                lax.ppermute(tail, axis, [(i, (i + 1) % count) for i in range(ends)]),
                cells,
                lax.ppermute(head, axis, [((i + 1) % count, i) for i in range(ends)]),
            ],
            axis=dim,
        )
    return cells


def passed_along(x, axis, by):
    size = lax.axis_size(axis)
    return lax.ppermute(x, axis, [(i, (i + by) % size) for i in range(size)])


def normalize(rows, modulate):
    values = rows.astype(jnp.float32)
    row_mean = jnp.mean(values, axis=-1, keepdims=True)
    centered = values - row_mean
    row_var = jnp.mean(centered * centered, axis=-1, keepdims=True)
    scaled = centered * lax.rsqrt(row_var + epsilon)
    return (scaled * (1.0 + modulate[1]) + modulate[0]).astype(jnp.bfloat16)


def nearby(extended):
    return jnp.stack(
        [extended[1, 1], extended[0, 1], extended[2, 1], extended[1, 0], extended[1, 2]]
    )


def body(clip_tokens, qkv_weight, out_weight, modulation, domain_ids, tile_lists):
    col_tiles = clip_tokens.shape[3]
    tile_len = clip_tokens.shape[4]
    model_width = clip_tokens.shape[5]
    inner_width = out_weight.shape[1]
    head_count = inner_width // HD
    own_count = col_tiles * tile_len
    own_rows = clip_tokens.reshape(own_count, model_width)
    domain_count = modulation.shape[1]
    one_hot = (jnp.arange(domain_count, dtype=jnp.int32) == domain_ids[0]).astype(jnp.float32)
    table_rows = modulation[0].reshape(domain_count, 3 * model_width).astype(jnp.float32)
    modulate = jnp.dot(one_hot[None, :], table_rows, precision=lax.Precision.HIGHEST).reshape(
        3, model_width
    )
    weight = qkv_weight[0]
    normed = normalize(own_rows, modulate)
    projected = jnp.dot(normed, weight, preferred_element_type=jnp.float32)
    queries = projected[:, :inner_width].astype(jnp.bfloat16)
    pairs = projected[:, inner_width:].astype(jnp.bfloat16)
    slab = pairs.reshape(1, 1, col_tiles, tile_len, 2 * inner_width)
    extended = extended_2(slab, (("frame", 0), ("row", 1)), 1)
    candidates = nearby(extended).reshape(5 * col_tiles, tile_len, 2 * inner_width)
    chosen = tile_lists[0, 0]
    picked = candidates[chosen].reshape(col_tiles, -1, 2 * inner_width)
    key_count = picked.shape[1]
    key_rows = picked[..., :inner_width].reshape(col_tiles, key_count, head_count, HD)
    value_rows = picked[..., inner_width:].reshape(col_tiles, key_count, head_count, HD)
    query_rows = queries.reshape(col_tiles, tile_len, head_count, HD)
    scores = jnp.einsum(
        "tqhd,tkhd->thqk", query_rows, key_rows, preferred_element_type=jnp.float32
    ) * HD ** (-0.5)
    row_peak = jnp.max(scores, axis=-1, keepdims=True)
    raised = jnp.exp(scores - row_peak)
    attn_weights = (raised / jnp.sum(raised, axis=-1, keepdims=True)).astype(jnp.bfloat16)
    mixed_heads = jnp.einsum(
        "thqk,tkhd->tqhd", attn_weights, value_rows, preferred_element_type=jnp.float32
    )
    mixed_heads = mixed_heads.astype(jnp.bfloat16).reshape(own_count, inner_width)
    branch = jnp.dot(mixed_heads, out_weight[0], preferred_element_type=jnp.float32)
    finished = (
        (own_rows.astype(jnp.float32) + modulate[2] * branch)
        .astype(jnp.bfloat16)
        .reshape(clip_tokens.shape)
    )
    return passed_along(finished, "segment", 1)


def solution(mesh):
    return jax.shard_map(
        body,
        mesh=mesh,
        in_specs=(
            P("segment", "frame", "row", None, None, None),
            P("segment", None, None),
            P("segment", None, None),
            P("segment", None, None, None),
            P("segment"),
            P("frame", "row", None, None),
        ),
        out_specs=P("segment", "frame", "row", None, None, None),
        check_vma=False,
    )
```

profile of v0, /device:TPU:0, one launch (start us, length us, event | category | flops | bytes accessed | tf_op | source)
XLA Modules:
  0.0 74.5 jit_solution(12643842217122067141)
XLA Ops:
  0.0 0.0 copy-start
  0.0 0.0 copy-start.1
  0.8 1.1 %convolution_reduce_fusion = f32[4608]{0:T(1024)S(1)} fusion(bf16[8,4608]{1,0:T(8,128)(2,1)} %bitcast.64, s32[]{:T(128)} %bitcast.52), kind=kOutput, calls=%fused_computation.16 | convolution fusion | flops 73736 | bytes 92164 | tf_op jit(solution)/shard_map/dot_general | solution.py:60
  1.9 1.1 %convert_reduce_fusion = f32[2,64]{1,0:T(2,128)S(1)} fusion(bf16[1,1,1,2,64,1536]{5,4,3,2,1,0:T(8,128)(2,1)} %param.6), kind=kLoop, calls=%fused_computation.19 | loop fusion | flops 393088 | bytes 393728 | tf_op jit(solution)/shard_map/reduce_sum | solution.py:36
  3.1 1.3 %multiply_reduce_fusion = f32[2,64]{1,0:T(2,128)S(1)} fusion(bf16[1,1,1,2,64,1536]{5,4,3,2,1,0:T(8,128)(2,1)} %param.6, f32[2,64]{1,0:T(2,128)S(1)} %broadcast_multiply_fusion), kind=kLoop, calls=%fused_computation.18 | loop fusion | flops 786304 | bytes 394240 | tf_op jit(solution)/shard_map/reduce_sum | solution.py:38
  4.3 0.0 copy-done.1
  4.3 0.3 add_convert_fusion
  4.6 4.1 %fusion.3 = bf16[128,2304]{1,0:T(8,128)(2,1)S(1)} fusion(bf16[128,1536]{1,0:T(8,128)(2,1)S(1)} %bitcast.60, bf16[1,1536,2304]{2,1,0:T(8,128)(2,1)} %param.7), kind=kOutput, calls=%fused_computation.4 | convolution fusion | flops 906264576 | bytes 8060928 | tf_op jit(solution)/shard_map/dot_general | solution.py:65
  8.8 0.0 copy-start.4
  8.8 4.9 %collective-permute-start = (bf16[1,1,2,64,1536]{4,3,2,1,0:T(8,128)(2,1)S(1)}, bf16[1,1,2,64,1536]{4,3,2,1,0:T(8,128)(2,1)S(1)}, u32[]{:S(2)}, u32[]{:S(2)}) collective-permute-start(bf16[1,1,2,64,1536]{4,3,2,1,0:T(8,128)(2,1)S(1)} %bitcast.56), channel_id=1, source_target_pairs={{0,2},{2,4},{4,6},{1,3},{3,5},{5,7},{8,10},{10,12},{12,14},{9,11},... | collective-permute-start | bytes 1179656 | tf_op jit(solution)/shard_map/ppermute | solution.py:20
  13.7 1.3 %collective-permute-start.1 = (bf16[1,1,2,64,1536]{4,3,2,1,0:T(8,128)(2,1)S(1)}, bf16[1,1,2,64,1536]{4,3,2,1,0:T(8,128)(2,1)}, u32[]{:S(2)}, u32[]{:S(2)}) collective-permute-start(bf16[1,1,2,64,1536]{4,3,2,1,0:T(8,128)(2,1)S(1)} %bitcast.57), channel_id=1, source_target_pairs={{2,0},{4,2},{6,4},{3,1},{5,3},{7,5},{10,8},{12,10},{14,12},{11,9},... | collective-permute-start | bytes 1179656 | tf_op jit(solution)/shard_map/ppermute | solution.py:22
  15.0 0.7 slice.50
  15.7 0.0 copy-done.4
  15.7 0.1 reshape.134
  15.8 1.9 %reshape.127 = bf16[2,64,6,128]{3,2,1,0:T(8,128)(2,1)} reshape(bf16[128,768]{1,0:T(8,128)(2,1)} %slice.50) | data formatting | bytes 393216 | tf_op jit(solution)/shard_map/reshape | solution.py:76
  17.6 4.4 %collective-permute-done = bf16[1,1,2,64,1536]{4,3,2,1,0:T(8,128)(2,1)S(1)} collective-permute-done((bf16[1,1,2,64,1536]{4,3,2,1,0:T(8,128)(2,1)S(1)}, bf16[1,1,2,64,1536]{4,3,2,1,0:T(8,128)(2,1)S(1)}, u32[]{:S(2)}, u32[]{:S(2)}) %collective-permute-start) | collective-permute-done | bytes 393248 | tf_op jit(solution)/shard_map/ppermute | solution.py:20
  22.0 10.5 %collective-permute-done.1 = bf16[1,1,2,64,1536]{4,3,2,1,0:T(8,128)(2,1)} collective-permute-done((bf16[1,1,2,64,1536]{4,3,2,1,0:T(8,128)(2,1)S(1)}, bf16[1,1,2,64,1536]{4,3,2,1,0:T(8,128)(2,1)}, u32[]{:S(2)}, u32[]{:S(2)}) %collective-permute-start.1) | collective-permute-done | bytes 393248 | tf_op jit(solution)/shard_map/ppermute | solution.py:22
  32.5 1.1 %pad_maximum_fusion = bf16[3,1,2,64,1536]{4,3,2,1,0:T(8,128)(2,1)S(1)} fusion(bf16[1,1,2,64,1536]{4,3,2,1,0:T(8,128)(2,1)} %collective-permute-done.1, bf16[1,1,2,64,1536]{4,3,2,1,0:T(8,128)(2,1)S(1)} %bitcast.58, bf16[1,1,2,64,1536]{4,3,2,1,0:T(8,128)(2,1)S(1)} %collective-permute-done), kind=kLoop, calls=%fused_computation.12 | loop fusion | flops 1179648 | bytes 2359296 | tf_op jit(solution)/shard_map/concatenate | solution.py:18
  33.6 1.4 %collective-permute-start.2 = (bf16[3,1,2,64,1536]{4,3,2,1,0:T(8,128)(2,1)S(1)}, bf16[3,1,2,64,1536]{4,3,2,1,0:T(8,128)(2,1)S(1)}, u32[]{:S(2)}, u32[]{:S(2)}) collective-permute-start(bf16[3,1,2,64,1536]{4,3,2,1,0:T(8,128)(2,1)S(1)} %pad_maximum_fusion), channel_id=1, source_target_pairs={{0,1},{2,3},{4,5},{6,7},{8,9},{10,11},{12,13},{14,15},{16,17},{18,... | collective-permute-start | bytes 3538952 | tf_op jit(solution)/shard_map/ppermute | solution.py:20
  35.0 0.8 %constant_dynamic-update-slice_fusion = bf16[5,2,64,1536]{3,2,1,0:T(8,128)(2,1)} fusion(bf16[1,2,64,1536]{3,2,1,0:T(8,128)(2,1)S(1)} %bitcast.59), kind=kLoop, calls=%fused_computation.29 | loop fusion | bytes 786432
  35.8 1.3 %collective-permute-start.3 = (bf16[3,1,2,64,1536]{4,3,2,1,0:T(8,128)(2,1)S(1)}, bf16[3,1,2,64,1536]{4,3,2,1,0:T(8,128)(2,1)S(1)}, u32[]{:S(2)}, u32[]{:S(2)}) collective-permute-start(bf16[3,1,2,64,1536]{4,3,2,1,0:T(8,128)(2,1)S(1)} %pad_maximum_fusion), channel_id=1, source_target_pairs={{1,0},{3,2},{5,4},{7,6},{9,8},{11,10},{13,12},{15,14},{17,16},{19,... | collective-permute-start | bytes 3538952 | tf_op jit(solution)/shard_map/ppermute | solution.py:22
  37.0 0.8 %bitcast_dynamic-update-slice_fusion.1 = bf16[5,2,64,1536]{3,2,1,0:T(8,128)(2,1)} fusion(bf16[5,2,64,1536]{3,2,1,0:T(8,128)(2,1)} %constant_dynamic-update-slice_fusion, bf16[1,1,2,64,1536]{4,3,2,1,0:T(8,128)(2,1)S(1)} %collective-permute-done), kind=kLoop, calls=%fused_computation.25 | loop fusion | bytes 786432
  37.8 1.8 %bitcast_dynamic-update-slice_fusion = bf16[5,2,64,1536]{3,2,1,0:T(8,128)(2,1)} fusion(bf16[5,2,64,1536]{3,2,1,0:T(8,128)(2,1)} %bitcast_dynamic-update-slice_fusion.1, bf16[1,1,2,64,1536]{4,3,2,1,0:T(8,128)(2,1)} %collective-permute-done.1), kind=kLoop, calls=%fused_computation.24 | loop fusion | bytes 786432
  39.6 0.0 collective-permute-done.2
  39.6 0.8 %fusion.13 = bf16[5,2,64,1536]{3,2,1,0:T(8,128)(2,1)} fusion(bf16[5,2,64,1536]{3,2,1,0:T(8,128)(2,1)} %bitcast_dynamic-update-slice_fusion, bf16[3,1,2,64,1536]{4,3,2,1,0:T(8,128)(2,1)S(1)} %collective-permute-done.2), kind=kLoop, calls=%fused_computation.23 | loop fusion | bytes 786432
  40.4 0.1 collective-permute-done.3
  40.5 0.8 %fusion.12 = bf16[5,2,64,1536]{3,2,1,0:T(8,128)(2,1)} fusion(bf16[5,2,64,1536]{3,2,1,0:T(8,128)(2,1)} %fusion.13, bf16[3,1,2,64,1536]{4,3,2,1,0:T(8,128)(2,1)S(1)} %collective-permute-done.3), kind=kLoop, calls=%fused_computation.21 | loop fusion | bytes 786432 | tf_op jit(solution)/shard_map/stack | solution.py:44
  41.3 3.7 %gather_fusion = bf16[12,64,1536]{2,1,0:T(8,128)(2,1)} fusion(bf16[10,64,1536]{2,1,0:T(8,128)(2,1)} %bitcast.12, s32[1024]{0:T(1024)S(1)} %pad_clamp_fusion), kind=kCustom, calls=%fused_computation | custom fusion | bytes 4718640 | tf_op jit(solution)/shard_map/gather | solution.py:72
  45.0 3.2 %fusion.22 = (bf16[2,384,768]{2,1,0:T(8,128)(2,1)}, bf16[2,384,768]{2,1,0:T(8,128)(2,1)}) fusion(bf16[2,384,1536]{2,1,0:T(8,128)(2,1)} %bitcast.53), kind=kLoop, calls=%fused_computation.40 | loop fusion | bytes 4718592 | tf_op jit(solution)/shard_map/slice | solution.py:74
  48.2 2.4 %copy.12 = bf16[2,384,768]{1,2,0:T(8,128)(2,1)} copy(bf16[2,384,768]{2,1,0:T(8,128)(2,1)} %get-tuple-element.6) | data formatting | bytes 2359296 | tf_op jit(solution)/shard_map/slice | solution.py:75
  50.5 0.0 copy-start.3
  50.5 2.4 %copy.13 = bf16[2,384,768]{1,2,0:T(8,128)(2,1)} copy(bf16[2,384,768]{2,1,0:T(8,128)(2,1)} %get-tuple-element.5) | data formatting | bytes 2359296 | tf_op jit(solution)/shard_map/slice | solution.py:74
  53.0 0.0 copy-done.3
  53.0 1.6 %convolution_multiply_fusion.1 = f32[2,6,64,384]{3,2,1,0:T(8,128)S(1)} fusion(bf16[2,384,6,128]{1,3,2,0:T(8,128)(2,1)} %bitcast.55, bf16[2,64,6,128]{3,2,1,0:T(8,128)(2,1)S(1)} %copy-done.3), kind=kOutput, calls=%fused_computation.10 | convolution fusion | flops 75792384 | bytes 2555904 | tf_op jit(solution)/shard_map/tqhd,tkhd->thqk/dot_general | solution.py:77
  54.6 0.0 copy-start.2
  54.6 1.0 %copy-done.2 = f32[2,6,64,384]{3,2,1,0:T(8,128)} copy-done((f32[2,6,64,384]{3,2,1,0:T(8,128)}, f32[2,6,64,384]{3,2,1,0:T(8,128)S(1)}, u32[]{:S(2)}) %copy-start.2) | copy-done | bytes 1179672
  55.6 0.4 fusion.23
  56.0 3.4 %fusion.11 = bf16[2,64,6,128]{3,1,2,0:T(8,128)(2,1)S(1)} fusion(bf16[2,384,6,128]{1,3,2,0:T(8,128)(2,1)} %bitcast.61, f32[2,6,64]{2,1,0:T(8,128)S(1)} %fusion.23, f32[2,6,64,384]{3,2,1,0:T(8,128)} %copy-done.2), kind=kOutput, calls=%fused_computation.15 | convolution fusion | flops 76481664 | bytes 2558976 | tf_op jit(solution)/shard_map/thqk,tkhd->tqhd/dot_general | solution.py:83
  59.4 0.2 copy.17
  59.6 0.0 copy-done
  59.6 0.5 fusion.7
  60.1 1.6 %collective-permute-start.4 = (bf16[1,1,1,2,64,1536]{5,4,3,2,1,0:T(8,128)(2,1)S(1)}, bf16[1,1,1,2,64,1536]{5,4,3,2,1,0:T(8,128)(2,1)S(1)}, u32[]{:S(2)}, u32[]{:S(2)}) collective-permute-start(bf16[1,1,1,2,64,1536]{5,4,3,2,1,0:T(8,128)(2,1)S(1)} %bitcast.63), channel_id=1, source_target_pairs={{0,8},{8,16},{16,24},{24,0},{1,9},{9,17},{17,25},{25,1},{2,10},{10... | collective-permute-start | bytes 1179656 | tf_op jit(solution)/shard_map/ppermute | solution.py:31
  61.7 12.0 %collective-permute-done.4 = bf16[1,1,1,2,64,1536]{5,4,3,2,1,0:T(8,128)(2,1)S(1)} collective-permute-done((bf16[1,1,1,2,64,1536]{5,4,3,2,1,0:T(8,128)(2,1)S(1)}, bf16[1,1,1,2,64,1536]{5,4,3,2,1,0:T(8,128)(2,1)S(1)}, u32[]{:S(2)}, u32[]{:S(2)}) %collective-permute-start.4) | collective-permute-done | bytes 393248 | tf_op jit(solution)/shard_map/ppermute | solution.py:31
  73.7 0.7 %copy.33 = bf16[1,1,1,2,64,1536]{5,4,3,2,1,0:T(8,128)(2,1)} copy(bf16[1,1,1,2,64,1536]{5,4,3,2,1,0:T(8,128)(2,1)S(1)} %collective-permute-done.4) | data formatting | bytes 786432
  (6 shorter events, 0.1 us)
Async XLA Ops:
  0.0 59.6 %copy-start = (bf16[1,768,1536]{2,1,0:T(8,128)(2,1)S(1)}, bf16[1,768,1536]{2,1,0:T(8,128)(2,1)}, u32[]{:S(2)}) copy-start(bf16[1,768,1536]{2,1,0:T(8,128)(2,1)} %param.8) | copy-start | bytes 7077892
  0.0 4.3 %copy-start.1 = (bf16[1,1,1,2,64,1536]{5,4,3,2,1,0:T(8,128)(2,1)S(1)}, bf16[1,1,1,2,64,1536]{5,4,3,2,1,0:T(8,128)(2,1)}, u32[]{:S(2)}) copy-start(bf16[1,1,1,2,64,1536]{5,4,3,2,1,0:T(8,128)(2,1)} %param.6) | copy-start | bytes 1179652
  8.8 6.9 %copy-start.4 = (s32[1,1,2,6]{3,2,1,0:T(2,128)S(1)}, s32[1,1,2,6]{3,2,1,0:T(2,128)}, u32[]{:S(2)}) copy-start(s32[1,1,2,6]{3,2,1,0:T(2,128)} %param.11) | copy-start | bytes 148
  8.8 13.2 %collective-permute-start = (bf16[1,1,2,64,1536]{4,3,2,1,0:T(8,128)(2,1)S(1)}, bf16[1,1,2,64,1536]{4,3,2,1,0:T(8,128)(2,1)S(1)}, u32[]{:S(2)}, u32[]{:S(2)}) collective-permute-start(bf16[1,1,2,64,1536]{4,3,2,1,0:T(8,128)(2,1)S(1)} %bitcast.56), channel_id=1, source_target_pairs={{0,2},{2,4},{4,6},{1,3},{3,5},{5,7},{8,10},{10,12},{12,14},{9,11},... | collective-permute-start | bytes 1179656 | tf_op jit(solution)/shard_map/ppermute | solution.py:20
  13.7 18.8 %collective-permute-start.1 = (bf16[1,1,2,64,1536]{4,3,2,1,0:T(8,128)(2,1)S(1)}, bf16[1,1,2,64,1536]{4,3,2,1,0:T(8,128)(2,1)}, u32[]{:S(2)}, u32[]{:S(2)}) collective-permute-start(bf16[1,1,2,64,1536]{4,3,2,1,0:T(8,128)(2,1)S(1)} %bitcast.57), channel_id=1, source_target_pairs={{2,0},{4,2},{6,4},{3,1},{5,3},{7,5},{10,8},{12,10},{14,12},{11,9},... | collective-permute-start | bytes 1179656 | tf_op jit(solution)/shard_map/ppermute | solution.py:22
  33.6 6.0 %collective-permute-start.2 = (bf16[3,1,2,64,1536]{4,3,2,1,0:T(8,128)(2,1)S(1)}, bf16[3,1,2,64,1536]{4,3,2,1,0:T(8,128)(2,1)S(1)}, u32[]{:S(2)}, u32[]{:S(2)}) collective-permute-start(bf16[3,1,2,64,1536]{4,3,2,1,0:T(8,128)(2,1)S(1)} %pad_maximum_fusion), channel_id=1, source_target_pairs={{0,1},{2,3},{4,5},{6,7},{8,9},{10,11},{12,13},{14,15},{16,17},{18,... | collective-permute-start | bytes 3538952 | tf_op jit(solution)/shard_map/ppermute | solution.py:20
  35.8 4.7 %collective-permute-start.3 = (bf16[3,1,2,64,1536]{4,3,2,1,0:T(8,128)(2,1)S(1)}, bf16[3,1,2,64,1536]{4,3,2,1,0:T(8,128)(2,1)S(1)}, u32[]{:S(2)}, u32[]{:S(2)}) collective-permute-start(bf16[3,1,2,64,1536]{4,3,2,1,0:T(8,128)(2,1)S(1)} %pad_maximum_fusion), channel_id=1, source_target_pairs={{1,0},{3,2},{5,4},{7,6},{9,8},{11,10},{13,12},{15,14},{17,16},{19,... | collective-permute-start | bytes 3538952 | tf_op jit(solution)/shard_map/ppermute | solution.py:22
  50.5 2.4 %copy-start.3 = (bf16[2,64,6,128]{3,2,1,0:T(8,128)(2,1)S(1)}, bf16[2,64,6,128]{3,2,1,0:T(8,128)(2,1)}, u32[]{:S(2)}) copy-start(bf16[2,64,6,128]{3,2,1,0:T(8,128)(2,1)} %reshape.127) | copy-start | bytes 589828
  54.6 1.1 %copy-start.2 = (f32[2,6,64,384]{3,2,1,0:T(8,128)}, f32[2,6,64,384]{3,2,1,0:T(8,128)S(1)}, u32[]{:S(2)}) copy-start(f32[2,6,64,384]{3,2,1,0:T(8,128)S(1)} %convolution_multiply_fusion.1) | copy-start | bytes 3538948
  60.1 13.7 %collective-permute-start.4 = (bf16[1,1,1,2,64,1536]{5,4,3,2,1,0:T(8,128)(2,1)S(1)}, bf16[1,1,1,2,64,1536]{5,4,3,2,1,0:T(8,128)(2,1)S(1)}, u32[]{:S(2)}, u32[]{:S(2)}) collective-permute-start(bf16[1,1,1,2,64,1536]{5,4,3,2,1,0:T(8,128)(2,1)S(1)} %bitcast.63), channel_id=1, source_target_pairs={{0,8},{8,16},{16,24},{24,0},{1,9},{9,17},{17,25},{25,1},{2,10},{10... | collective-permute-start | bytes 1179656 | tf_op jit(solution)/shard_map/ppermute | solution.py:31
where the time goes:
time: 75.1 us; the launch traced here: 74.5 us
  waiting for transfers between devices  27 us (36%)
  local copies, waits for them, and re-layouts  21.2 us (28%)
  matrix products  10.7 us (14%)
  starting transfers between devices  10.4 us (14%)
  other arithmetic  4.2 us (6%)
  between operations  0.96 us (1%)
    ppermute x1, waiting for transfers between devices, passed_along(): return lax.ppermute(x, axis, [(i, (i + by) % size) for i in range(size)])  12 us
    ppermute x2, waiting for transfers between devices, extended_2(): lax.ppermute(head, axis, [((i + 1) % count, i) for i in range(ends)])  10.6 us
    ppermute x2, starting transfers between devices, extended_2(): lax.ppermute(tail, axis, [(i, (i + 1) % count) for i in range(ends)])  6.23 us
    unnamed x15, local copies, waits for them, and re-layouts  5.89 us
    slice x2, local copies, waits for them, and re-layouts, body(): picked[..., :inner_width].reshape(col_tiles, key_count, head_count, HD)  5.6 us
    ppermute x2, waiting for transfers between devices, extended_2(): lax.ppermute(tail, axis, [(i, (i + 1) % count) for i in range(ends)])  4.39 us
    dot_general x1, matrix products, body(): projected = jnp.dot(normed, weight, preferred_element_type=jnp.float32)  4.1 us
    gather x1, local copies, waits for them, and re-layouts, body(): picked = candidates[chosen].reshape(col_tiles, -1, 2 * inner_width)  3.73 us
  transfers between devices with their start and end apart: 5, of which 4 were waited for; matrix products, arithmetic and copies ran while one was open for 9% of the time, Pallas kernels for 0%

commit v1 on v0

v1 whole, which is shorter than its diff:
```python
import functools

import jax
import jax.numpy as jnp
from jax import lax
from jax.experimental import pallas as pl
from jax.experimental.pallas import tpu as pltpu
from jax.sharding import PartitionSpec as P

HD = 128
EPSILON = 1e-06
MASKED = -1e30
RELAYED = (2, 2, 2)
DIRECT = 2
F32 = jnp.float32
BF16 = jnp.bfloat16
VMEM = pl.BlockSpec(memory_space=pltpu.VMEM)
SMEM = pl.BlockSpec(memory_space=pltpu.SMEM)
HBM = pl.BlockSpec(memory_space=pltpu.HBM)
PARAMS = pltpu.CompilerParams(vmem_limit_bytes=32 * 1024 * 1024)


def modulate_rows(domain_ref, modulation_ref):
    table = modulation_ref[...].astype(F32)
    row = lax.broadcasted_iota(jnp.int32, table.shape, 1)
    return jnp.sum(jnp.where(row == domain_ref[0], table, 0.0), axis=1)


def normalize(rows, shift, scale):
    values = rows.astype(F32)
    centered = values - jnp.mean(values, axis=-1, keepdims=True)
    row_var = jnp.mean(centered * centered, axis=-1, keepdims=True)
    return (centered * lax.rsqrt(row_var + EPSILON) * (1.0 + scale) + shift).astype(BF16)


def normalized(refs, modulate_ref):
    shift, scale = modulate_ref[0:1, :], modulate_ref[1:2, :]
    return jnp.concatenate([normalize(r[...], shift, scale) for r in refs], axis=0)


def projected(rows, weight_ref):
    return jnp.dot(rows, weight_ref[...], preferred_element_type=F32).astype(BF16)


def own_kernel(n_other, inner, domain_ref, modulation_hbm, weight_hbm, out_weight_hbm, own_hbm, *refs):
    other_refs = refs[:n_other]
    (modulate_ref, pair_weight_ref, out_weight_ref, own_ref, q_ref, kv_ref) = refs[n_other : n_other + 6]
    kv_other_refs = refs[n_other + 6 : 2 * n_other + 6]
    modulation_ref, q_weight_ref, sems = refs[2 * n_other + 6 :]
    first = [
        pltpu.make_async_copy(modulation_hbm, modulation_ref, sems.at[4]),
        pltpu.make_async_copy(own_hbm, own_ref, sems.at[5]),
    ]
    loads = [
        pltpu.make_async_copy(weight_hbm.at[:, pl.ds(inner, inner)], pair_weight_ref.at[:, pl.ds(0, inner)], sems.at[0]),
        pltpu.make_async_copy(weight_hbm.at[:, pl.ds(2 * inner, inner)], pair_weight_ref.at[:, pl.ds(inner, inner)], sems.at[1]),
        pltpu.make_async_copy(weight_hbm.at[:, pl.ds(0, inner)], q_weight_ref, sems.at[2]),
        pltpu.make_async_copy(out_weight_hbm, out_weight_ref, sems.at[3]),
    ]
    for load in first + loads:
        load.start()
    for load in first:
        load.wait()
    modulate_ref[...] = modulate_rows(domain_ref, modulation_ref)
    rows = normalized((own_ref, *other_refs), modulate_ref)
    count = own_ref.shape[0]
    for part in range(2):
        loads[part].wait()
        cols = slice(part * inner, (part + 1) * inner)
        pairs = jnp.dot(rows, pair_weight_ref[:, cols], preferred_element_type=F32).astype(BF16)
        for i, ref in enumerate((kv_ref, *kv_other_refs)):
            ref[:, cols] = pairs[i * count : (i + 1) * count]
    loads[2].wait()
    q_ref[...] = projected(rows[:count], q_weight_ref)
    loads[3].wait()


def pairs_kernel(n_chunks, modulate_ref, weight_ref, *refs):
    chunk_refs, kv_ref = refs[:n_chunks], refs[n_chunks]
    kv_ref[...] = projected(normalized(chunk_refs, modulate_ref), weight_ref)


def picked_bits(lists_ref, tile, count, col_tiles, slots):
    bits = jnp.int32(0)
    for k in range(count):
        number = lists_ref[tile, k]
        direction = number // col_tiles
        slot = jnp.int32(0)
        for d in range(1, 5):
            slot = jnp.where(direction == d, slots[d], slot)
        bits = bits | (jnp.int32(1) << (slot * col_tiles + number % col_tiles))
    return bits


def attend_kernel(
    n_kv, n_chunks, inner, tile_len, slots_of,
    lists_ref, modulate_ref, weight_ref, out_weight_ref, own_ref, q_ref, *refs
):
    kv_refs = refs[:n_kv]
    chunk_refs = refs[n_kv : n_kv + n_chunks]
    finished_ref = refs[n_kv + n_chunks]
    own_count = own_ref.shape[0]
    col_tiles = own_count // tile_len
    pairs = [r[...] for r in kv_refs]
    if n_chunks:
        pairs.append(projected(normalized(chunk_refs, modulate_ref), weight_ref))
    pairs = jnp.concatenate(pairs, axis=0)
    key_count = pairs.shape[0]
    slots = slots_of()
    count = lists_ref.shape[1]
    position = lax.broadcasted_iota(jnp.int32, (tile_len, key_count), 1) // tile_len
    bias = jnp.concatenate(
        [
            jnp.where(
                ((picked_bits(lists_ref, t, count, col_tiles, slots) >> position) & 1) == 1,
                0.0,
                MASKED,
            )
            for t in range(col_tiles)
        ],
        axis=0,
    )
    queries = q_ref[...]
    heads = []
    for h in range(inner // HD):
        cols = slice(h * HD, (h + 1) * HD)
        keys = pairs[:, cols]
        values = pairs[:, inner + h * HD : inner + (h + 1) * HD]
        scores = lax.dot_general(
            queries[:, cols], keys, (((1,), (1,)), ((), ())), preferred_element_type=F32
        )
        scores = scores * HD ** (-0.5) + bias
        raised = jnp.exp(scores - jnp.max(scores, axis=-1, keepdims=True))
        total = jnp.sum(raised, axis=-1, keepdims=True)
        mixed = jnp.dot(raised.astype(BF16), values, preferred_element_type=F32)
        heads.append((mixed / total).astype(BF16))
    mixed_heads = jnp.concatenate(heads, axis=1)
    branch = jnp.dot(mixed_heads, out_weight_ref[...], preferred_element_type=F32)
    finished_ref[...] = (own_ref[...].astype(F32) + modulate_ref[2:3, :] * branch).astype(BF16)


def swap_perm(size):
    return [(i, i ^ 1) for i in range(size)]


def far_perm(size):
    return [(i, i + 1) for i in range(1, size - 1, 2)] + [(i + 1, i) for i in range(1, size - 1, 2)]


def relay_perm(size):
    return [(i, i + 2) for i in range(0, size - 2, 2)] + [(i, i - 2) for i in range(3, size, 2)]


def in_hbm(x):
    return pltpu.with_memory_space_constraint(x, pltpu.HBM)


def body(clip_tokens, qkv_weight, out_weight, modulation, domain_ids, tile_lists):
    col_tiles, tile_len, width = clip_tokens.shape[3:]
    own_count = col_tiles * tile_len
    inner = out_weight.shape[1]
    frames, rows = lax.axis_size("frame"), lax.axis_size("row")
    own = clip_tokens.reshape(own_count, width)
    modulation_table = jnp.transpose(modulation[0], (1, 0, 2))
    lists = tile_lists[0, 0]

    shares = RELAYED + (DIRECT,)
    starts = [own_count * sum(shares[:i]) // sum(shares) for i in range(len(shares) + 1)]
    chunks = [own[a:b] for a, b in zip(starts[:-1], starts[1:])]
    near_chunks = [lax.ppermute(c, "frame", swap_perm(frames)) for c in chunks]
    near_rows = [lax.ppermute(own, "row", swap_perm(rows))]
    if rows > 2:
        near_rows.append(lax.ppermute(near_rows[0], "row", relay_perm(rows)))

    pair_shape = (own_count, 2 * inner)
    modulate, pair_weight, out_w, own_rows, q, *pairs = pl.pallas_call(
        functools.partial(own_kernel, len(near_rows), inner),
        out_shape=[
            pltpu.VMEM((3, width), F32),
            pltpu.VMEM((width, 2 * inner), BF16),
            pltpu.VMEM((inner, width), BF16),
            pltpu.VMEM((own_count, width), BF16),
            pltpu.VMEM((own_count, inner), BF16),
        ]
        + [pltpu.VMEM(pair_shape, BF16)] * (1 + len(near_rows)),
        in_specs=[SMEM] + [HBM] * 4 + [VMEM] * len(near_rows),
        out_specs=[VMEM] * (6 + len(near_rows)),
        scratch_shapes=[
            pltpu.VMEM(modulation_table.shape, BF16),
            pltpu.VMEM((width, inner), BF16),
            pltpu.SemaphoreType.DMA((6,)),
        ],
        compiler_params=PARAMS,
        name="own_pairs",
    )(domain_ids, *map(in_hbm, (modulation_table, qkv_weight[0], out_weight[0], own)), *near_rows)

    far_chunks = []
    if frames > 2:
        *relayed, q = lax.optimization_barrier((*near_chunks[:-1], q))
        far_chunks = [lax.ppermute(c, "frame", relay_perm(frames)) for c in relayed]
        far_chunks.append(lax.ppermute(chunks[-1], "frame", far_perm(frames)))
        near_chunks = [*relayed, near_chunks[-1]]
    pairs.append(
        pl.pallas_call(
            functools.partial(pairs_kernel, len(near_chunks)),
            out_shape=pltpu.VMEM(pair_shape, BF16),
            in_specs=[VMEM] * (2 + len(near_chunks)),
            out_specs=VMEM,
            compiler_params=PARAMS,
            name="near_pairs",
        )(modulate, pair_weight, *near_chunks)
    )

    def slots_of():
        odd_frame = lax.axis_index("frame") % 2
        odd_row = lax.axis_index("row") % 2
        row_slot, frame_slot = 1, 1 + len(near_rows)
        return {
            1: frame_slot + 1 - odd_frame,
            2: frame_slot + odd_frame,
            3: row_slot + 1 - odd_row,
            4: row_slot + odd_row,
        }

    finished = pl.pallas_call(
        functools.partial(
            attend_kernel, len(pairs), len(far_chunks), inner, tile_len, slots_of
        ),
        out_shape=jax.ShapeDtypeStruct((own_count, width), BF16),
        in_specs=[SMEM] + [VMEM] * (5 + len(pairs) + len(far_chunks)),
        out_specs=VMEM,
        compiler_params=PARAMS,
        name="attend",
    )(lists, modulate, pair_weight, out_w, own_rows, q, *pairs, *far_chunks)
    segments = lax.axis_size("segment")
    return lax.ppermute(
        finished.reshape(clip_tokens.shape),
        "segment",
        [(i, (i + 1) % segments) for i in range(segments)],
    )


def solution(mesh):
    return jax.shard_map(
        body,
        mesh=mesh,
        in_specs=(
            P("segment", "frame", "row", None, None, None),
            P("segment", None, None),
            P("segment", None, None),
            P("segment", None, None, None),
            P("segment"),
            P("frame", "row", None, None),
        ),
        out_specs=P("segment", "frame", "row", None, None, None),
        check_vma=False,
    )
```

time: 75.1 us -> 39.9 us (0.53)
  local copies, waits for them, and re-layouts: 21.2 us -> 1.81 us
  waiting for transfers between devices: 27 us -> 12.5 us
  matrix products: 10.7 us -> 0 us
  Pallas kernels: 0 us -> 8.95 us
  starting transfers between devices: 10.4 us -> 15.5 us
  other arithmetic: 4.2 us -> 0 us
    ppermute x5 -> x10, waiting for transfers between devices: 27 us -> 12.5 us  [the longest x1 10.1 us: body(): lax.ppermute(finished.reshape(clip_tokens.shape), 'segment', [(i, (i + 1)...]
    dot_general x5 -> x0, matrix products: 10.7 us -> none  [the longest x1 4.1 us: body(): projected = jnp.dot(normed, weight, preferred_element_type=jnp.float32)]
    pallas_call x0 -> x3, Pallas kernels: none -> 8.95 us  [the longest x1 4.36 us: body(): pl.pallas_call(functools.partial(own_kernel, len(near_rows), inner), out_...]
    slice x5 -> x1, local copies, waits for them, and re-layouts: 8.67 us -> 1.06 us  [body(): chunks = [own[a:b] for a, b in zip(starts[:-1], starts[1:])]]
    unnamed x15 -> x3, local copies, waits for them, and re-layouts: 5.89 us -> 0.75 us
    ppermute x5 -> x10, starting transfers between devices: 10.4 us -> 15.5 us  [the longest x4 8.87 us: body(): near_chunks = [lax.ppermute(c, 'frame', swap_perm(frames)) for c in chunks]]
    gather x1 -> x0, local copies, waits for them, and re-layouts: 3.73 us -> none  [body(): picked = candidates[chosen].reshape(col_tiles, -1, 2 * inner_width)]
    reduce_sum x2 -> x0, other arithmetic: 2.38 us -> none  [the longest x1 1.25 us: normalize(): row_var = jnp.mean(centered * centered, axis=-1, keepdims=True)]
  transfers between devices with their start and end apart: 5 -> 10, of which waited for: 4 -> 3; matrix products, arithmetic and copies ran while one was open for 9% -> 3% of each run, Pallas kernels for 0% -> 14%
where the time goes in v1:
time: 39.9 us; the launch traced here: 39.5 us
  starting transfers between devices  15.5 us (39%)
  waiting for transfers between devices  12.5 us (31%)
  Pallas kernels  8.95 us (22%)
  local copies, waits for them, and re-layouts  1.81 us (5%)
  between operations  0.77 us (2%)
    ppermute x1, waiting for transfers between devices, body(): lax.ppermute(finished.reshape(clip_tokens.shape), 'segment', [(i, (i + 1)...  10.1 us
    ppermute x4, starting transfers between devices, body(): near_chunks = [lax.ppermute(c, 'frame', swap_perm(frames)) for c in chunks]  8.87 us
    pallas_call x1, Pallas kernels, body(): pl.pallas_call(functools.partial(own_kernel, len(near_rows), inner), out_...  4.36 us
    ppermute x3, starting transfers between devices, body(): far_chunks = [lax.ppermute(c, 'frame', relay_perm(frames)) for c in relayed]  3.89 us
    pallas_call x1, Pallas kernels, body(): pl.pallas_call(functools.partial(attend_kernel, len(pairs), len(far_chunk...  3.55 us
    ppermute x3, waiting for transfers between devices, body(): far_chunks = [lax.ppermute(c, 'frame', relay_perm(frames)) for c in relayed]  2.36 us
    ppermute x1, starting transfers between devices, body(): lax.ppermute(finished.reshape(clip_tokens.shape), 'segment', [(i, (i + 1)...  1.61 us
    slice x1, local copies, waits for them, and re-layouts, body(): chunks = [own[a:b] for a, b in zip(starts[:-1], starts[1:])]  1.06 us
  transfers between devices with their start and end apart: 10, of which 3 were waited for; matrix products, arithmetic and copies ran while one was open for 3% of the time, Pallas kernels for 14%

profile of v1, /device:TPU:0, one launch (start us, length us, event | category | flops | bytes accessed | tf_op | source)
XLA Modules:
  0.0 39.5 jit_solution(13620951683480015975)
XLA Ops:
  0.0 0.5 %collective-permute-start = (bf16[128,1536]{1,0:T(8,128)(2,1)}, bf16[128,1536]{1,0:T(8,128)(2,1)S(1)}, u32[]{:S(2)}, u32[]{:S(2)}) collective-permute-start(bf16[128,1536]{1,0:T(8,128)(2,1)} %bitcast.12), channel_id=1, source_target_pairs={{0,1},{1,0},{2,3},{3,2},{4,5},{5,4},{6,7},{7,6},{8,9},{9,8},{10,11... | collective-permute-start | bytes 1179656 | tf_op jit(solution)/shard_map/ppermute | solution.py:171
  0.5 1.1 %fusion = (bf16[32,1536]{1,0:T(8,128)(2,1)S(1)}, bf16[32,1536]{1,0:T(8,128)(2,1)S(1)}, bf16[32,1536]{1,0:T(8,128)(2,1)S(1)}, bf16[32,1536]{1,0:T(8,128)(2,1)S(1)}) fusion(bf16[128,1536]{1,0:T(8,128)(2,1)} %bitcast.13), kind=kLoop, calls=%fused_computation | loop fusion | bytes 786432 | tf_op jit(solution)/shard_map/slice | solution.py:169
  1.5 2.6 %collective-permute-start.3 = (bf16[32,1536]{1,0:T(8,128)(2,1)S(1)}, bf16[32,1536]{1,0:T(8,128)(2,1)S(1)}, u32[]{:S(2)}, u32[]{:S(2)}) collective-permute-start(bf16[32,1536]{1,0:T(8,128)(2,1)S(1)} %get-tuple-element.28), channel_id=1, source_target_pairs={{0,2},{2,0},{4,6},{6,4},{1,3},{3,1},{5,7},{7,5},{8,10},{10,8},{12,... | collective-permute-start | bytes 294920 | tf_op jit(solution)/shard_map/ppermute | solution.py:170
  4.1 0.1 collective-permute-start.2
  4.2 1.9 %collective-permute-start.1 = (bf16[32,1536]{1,0:T(8,128)(2,1)S(1)}, bf16[32,1536]{1,0:T(8,128)(2,1)S(1)}, u32[]{:S(2)}, u32[]{:S(2)}) collective-permute-start(bf16[32,1536]{1,0:T(8,128)(2,1)S(1)} %get-tuple-element.30), channel_id=1, source_target_pairs={{0,2},{2,0},{4,6},{6,4},{1,3},{3,1},{5,7},{7,5},{8,10},{10,8},{12,... | collective-permute-start | bytes 294920 | tf_op jit(solution)/shard_map/ppermute | solution.py:170
  6.1 0.7 %collective-permute-start.8 = (bf16[32,1536]{1,0:T(8,128)(2,1)S(1)}, bf16[32,1536]{1,0:T(8,128)(2,1)S(1)}, u32[]{:S(2)}, u32[]{:S(2)}) collective-permute-start(bf16[32,1536]{1,0:T(8,128)(2,1)S(1)} %get-tuple-element.27), channel_id=1, source_target_pairs={{2,4},{4,2},{3,5},{5,3},{10,12},{12,10},{11,13},{13,11},{18,20},{2... | collective-permute-start | bytes 294920 | tf_op jit(solution)/shard_map/ppermute | solution.py:201
  7.4 0.0 collective-permute-done.refs_0_
  7.4 4.3 %collective-permute-start.4 = (bf16[32,1536]{1,0:T(8,128)(2,1)S(1)}, bf16[32,1536]{1,0:T(8,128)(2,1)S(1)}, u32[]{:S(2)}, u32[]{:S(2)}) collective-permute-start(bf16[32,1536]{1,0:T(8,128)(2,1)S(1)} %get-tuple-element.27), channel_id=1, source_target_pairs={{0,2},{2,0},{4,6},{6,4},{1,3},{3,1},{5,7},{7,5},{8,10},{10,8},{12,... | collective-permute-start | bytes 294920 | tf_op jit(solution)/shard_map/ppermute | solution.py:170
  11.7 4.4 %own_pairs.1 = (f32[3,1536]{1,0:T(4,128)S(1)}, bf16[1536,1536]{1,0:T(8,128)(2,1)S(1)}, bf16[768,1536]{1,0:T(8,128)(2,1)S(1)}, bf16[128,1536]{1,0:T(8,128)(2,1)S(...) custom-call(s32[1]{0:T(128)S(6)} %copy.8.domain_ref, ...), custom_call_target="tpu_custom_call" | custom-call | tf_op jit(solution)/shard_map/own_pairs/pallas_call | solution.py:176
  16.1 0.0 copy-start
  16.1 0.0 collective-permute-done.3.refs_2_
  16.1 0.0 collective-permute-done.2.refs_1_
  16.1 0.0 collective-permute-done.1.refs_0_
  16.1 1.3 %collective-permute-start.5 = (bf16[32,1536]{1,0:T(8,128)(2,1)S(1)}, bf16[32,1536]{1,0:T(8,128)(2,1)S(1)}, u32[]{:S(2)}, u32[]{:S(2)}) collective-permute-start(bf16[32,1536]{1,0:T(8,128)(2,1)S(1)} %collective-permute-done.1.refs_0_), channel_id=1, source_target_pairs={{0,4},{6,2},{1,5},{7,3},{8,12},{14,10},{9,13},{15,11},{16,20},{22,... | collective-permute-start | bytes 294920 | tf_op jit(solution)/shard_map/ppermute | solution.py:200
  17.4 1.3 %collective-permute-start.6 = (bf16[32,1536]{1,0:T(8,128)(2,1)S(1)}, bf16[32,1536]{1,0:T(8,128)(2,1)S(1)}, u32[]{:S(2)}, u32[]{:S(2)}) collective-permute-start(bf16[32,1536]{1,0:T(8,128)(2,1)S(1)} %collective-permute-done.2.refs_1_), channel_id=1, source_target_pairs={{0,4},{6,2},{1,5},{7,3},{8,12},{14,10},{9,13},{15,11},{16,20},{22,... | collective-permute-start | bytes 294920 | tf_op jit(solution)/shard_map/ppermute | solution.py:200
  18.7 1.3 %collective-permute-start.7 = (bf16[32,1536]{1,0:T(8,128)(2,1)S(1)}, bf16[32,1536]{1,0:T(8,128)(2,1)S(1)}, u32[]{:S(2)}, u32[]{:S(2)}) collective-permute-start(bf16[32,1536]{1,0:T(8,128)(2,1)S(1)} %collective-permute-done.3.refs_2_), channel_id=1, source_target_pairs={{0,4},{6,2},{1,5},{7,3},{8,12},{14,10},{9,13},{15,11},{16,20},{22,... | collective-permute-start | bytes 294920 | tf_op jit(solution)/shard_map/ppermute | solution.py:200
  20.0 0.0 collective-permute-done.4.refs_3_
  20.0 1.0 %near_pairs.1.refs_2_ = bf16[128,1536]{1,0:T(8,128)(2,1)S(1)} custom-call(f32[3,1536]{1,0:T(4,128)S(1)} %get-tuple-element.16.modulate_ref, bf16[1536,1536]{1,0:T(8,128)(2,1)S(1)} %get-tuple-element.17.weight_ref, bf16[32,1536]{1,0:T(8,128)(2,1)S(1)} %collective-permute-done.1.refs_0_, bf16[32,1536]{1,0:T(8,128)(2,1)S(1)} %collective-permute-done.2.refs_1_, ...), custom_call_target="tpu_custom_call" | custom-call | tf_op jit(solution)/shard_map/near_pairs/pallas_call | solution.py:204
  21.1 0.0 collective-permute-done.8.refs_6_
  21.1 0.0 collective-permute-done.5.refs_3_
  21.1 1.3 %collective-permute-done.6.refs_4_ = bf16[32,1536]{1,0:T(8,128)(2,1)S(1)} collective-permute-done((bf16[32,1536]{1,0:T(8,128)(2,1)S(1)}, bf16[32,1536]{1,0:T(8,128)(2,1)S(1)}, u32[]{:S(2)}, u32[]{:S(2)}) %collective-permute-start.6) | collective-permute-done | bytes 98336 | tf_op jit(solution)/shard_map/ppermute | solution.py:200
  22.4 1.1 %collective-permute-done.7.refs_5_ = bf16[32,1536]{1,0:T(8,128)(2,1)S(1)} collective-permute-done((bf16[32,1536]{1,0:T(8,128)(2,1)S(1)}, bf16[32,1536]{1,0:T(8,128)(2,1)S(1)}, u32[]{:S(2)}, u32[]{:S(2)}) %collective-permute-start.7) | collective-permute-done | bytes 98336 | tf_op jit(solution)/shard_map/ppermute | solution.py:200
  23.5 0.0 copy-done
  23.5 3.5 %attend.1 = bf16[128,1536]{1,0:T(8,128)(2,1)S(1)} custom-call(s32[2,6]{1,0:T(2,128)S(1)} %bitcast.9, f32[3,1536]{1,0:T(4,128)S(1)} %get-tuple-element.16.modulate_ref, bf16[1536,1536]{1,0:T(8,128)(2,1)S(1)} %get-tuple-element.17.weight_ref, bf16[768,1536]{1,0:T(8,128)(2,1)S(1)} %get-tuple-element.18.out_weight_ref, ...), custom_call_target="tpu_custom_call" | custom-call | tf_op jit(solution)/shard_map/attend/pallas_call | solution.py:225
  27.0 1.6 %collective-permute-start.9 = (bf16[1,1,1,2,64,1536]{5,4,3,2,1,0:T(8,128)(2,1)S(1)}, bf16[1,1,1,2,64,1536]{5,4,3,2,1,0:T(8,128)(2,1)S(1)}, u32[]{:S(2)}, u32[]{:S(2)}) collective-permute-start(bf16[1,1,1,2,64,1536]{5,4,3,2,1,0:T(8,128)(2,1)S(1)} %bitcast.8), channel_id=1, source_target_pairs={{0,8},{8,16},{16,24},{24,0},{1,9},{9,17},{17,25},{25,1},{2,10},{10... | collective-permute-start | bytes 1179656 | tf_op jit(solution)/shard_map/ppermute | solution.py:236
  28.6 10.1 %collective-permute-done.9 = bf16[1,1,1,2,64,1536]{5,4,3,2,1,0:T(8,128)(2,1)S(1)} collective-permute-done((bf16[1,1,1,2,64,1536]{5,4,3,2,1,0:T(8,128)(2,1)S(1)}, bf16[1,1,1,2,64,1536]{5,4,3,2,1,0:T(8,128)(2,1)S(1)}, u32[]{:S(2)}, u32[]{:S(2)}) %collective-permute-start.9) | collective-permute-done | bytes 393248 | tf_op jit(solution)/shard_map/ppermute | solution.py:236
  38.7 0.7 %copy.9 = bf16[1,1,1,2,64,1536]{5,4,3,2,1,0:T(8,128)(2,1)} copy(bf16[1,1,1,2,64,1536]{5,4,3,2,1,0:T(8,128)(2,1)S(1)} %collective-permute-done.9) | data formatting | bytes 786432
Async XLA Ops:
  0.0 7.4 %collective-permute-start = (bf16[128,1536]{1,0:T(8,128)(2,1)}, bf16[128,1536]{1,0:T(8,128)(2,1)S(1)}, u32[]{:S(2)}, u32[]{:S(2)}) collective-permute-start(bf16[128,1536]{1,0:T(8,128)(2,1)} %bitcast.12), channel_id=1, source_target_pairs={{0,1},{1,0},{2,3},{3,2},{4,5},{5,4},{6,7},{7,6},{8,9},{9,8},{10,11... | collective-permute-start | bytes 1179656 | tf_op jit(solution)/shard_map/ppermute | solution.py:171
  1.5 14.6 %collective-permute-start.3 = (bf16[32,1536]{1,0:T(8,128)(2,1)S(1)}, bf16[32,1536]{1,0:T(8,128)(2,1)S(1)}, u32[]{:S(2)}, u32[]{:S(2)}) collective-permute-start(bf16[32,1536]{1,0:T(8,128)(2,1)S(1)} %get-tuple-element.28), channel_id=1, source_target_pairs={{0,2},{2,0},{4,6},{6,4},{1,3},{3,1},{5,7},{7,5},{8,10},{10,8},{12,... | collective-permute-start | bytes 294920 | tf_op jit(solution)/shard_map/ppermute | solution.py:170
  4.1 12.0 %collective-permute-start.2 = (bf16[32,1536]{1,0:T(8,128)(2,1)S(1)}, bf16[32,1536]{1,0:T(8,128)(2,1)S(1)}, u32[]{:S(2)}, u32[]{:S(2)}) collective-permute-start(bf16[32,1536]{1,0:T(8,128)(2,1)S(1)} %get-tuple-element.29), channel_id=1, source_target_pairs={{0,2},{2,0},{4,6},{6,4},{1,3},{3,1},{5,7},{7,5},{8,10},{10,8},{12,... | collective-permute-start | bytes 294920 | tf_op jit(solution)/shard_map/ppermute | solution.py:170
  4.2 12.0 %collective-permute-start.1 = (bf16[32,1536]{1,0:T(8,128)(2,1)S(1)}, bf16[32,1536]{1,0:T(8,128)(2,1)S(1)}, u32[]{:S(2)}, u32[]{:S(2)}) collective-permute-start(bf16[32,1536]{1,0:T(8,128)(2,1)S(1)} %get-tuple-element.30), channel_id=1, source_target_pairs={{0,2},{2,0},{4,6},{6,4},{1,3},{3,1},{5,7},{7,5},{8,10},{10,8},{12,... | collective-permute-start | bytes 294920 | tf_op jit(solution)/shard_map/ppermute | solution.py:170
  6.1 15.0 %collective-permute-start.8 = (bf16[32,1536]{1,0:T(8,128)(2,1)S(1)}, bf16[32,1536]{1,0:T(8,128)(2,1)S(1)}, u32[]{:S(2)}, u32[]{:S(2)}) collective-permute-start(bf16[32,1536]{1,0:T(8,128)(2,1)S(1)} %get-tuple-element.27), channel_id=1, source_target_pairs={{2,4},{4,2},{3,5},{5,3},{10,12},{12,10},{11,13},{13,11},{18,20},{2... | collective-permute-start | bytes 294920 | tf_op jit(solution)/shard_map/ppermute | solution.py:201
  7.4 12.6 %collective-permute-start.4 = (bf16[32,1536]{1,0:T(8,128)(2,1)S(1)}, bf16[32,1536]{1,0:T(8,128)(2,1)S(1)}, u32[]{:S(2)}, u32[]{:S(2)}) collective-permute-start(bf16[32,1536]{1,0:T(8,128)(2,1)S(1)} %get-tuple-element.27), channel_id=1, source_target_pairs={{0,2},{2,0},{4,6},{6,4},{1,3},{3,1},{5,7},{7,5},{8,10},{10,8},{12,... | collective-permute-start | bytes 294920 | tf_op jit(solution)/shard_map/ppermute | solution.py:170
  16.1 7.4 %copy-start = (s32[1,1,2,6]{3,2,1,0:T(2,128)S(1)}, s32[1,1,2,6]{3,2,1,0:T(2,128)}, u32[]{:S(2)}) copy-start(s32[1,1,2,6]{3,2,1,0:T(2,128)} %param.11) | copy-start | bytes 148
  16.1 5.0 %collective-permute-start.5 = (bf16[32,1536]{1,0:T(8,128)(2,1)S(1)}, bf16[32,1536]{1,0:T(8,128)(2,1)S(1)}, u32[]{:S(2)}, u32[]{:S(2)}) collective-permute-start(bf16[32,1536]{1,0:T(8,128)(2,1)S(1)} %collective-permute-done.1.refs_0_), channel_id=1, source_target_pairs={{0,4},{6,2},{1,5},{7,3},{8,12},{14,10},{9,13},{15,11},{16,20},{22,... | collective-permute-start | bytes 294920 | tf_op jit(solution)/shard_map/ppermute | solution.py:200
  17.4 5.0 %collective-permute-start.6 = (bf16[32,1536]{1,0:T(8,128)(2,1)S(1)}, bf16[32,1536]{1,0:T(8,128)(2,1)S(1)}, u32[]{:S(2)}, u32[]{:S(2)}) collective-permute-start(bf16[32,1536]{1,0:T(8,128)(2,1)S(1)} %collective-permute-done.2.refs_1_), channel_id=1, source_target_pairs={{0,4},{6,2},{1,5},{7,3},{8,12},{14,10},{9,13},{15,11},{16,20},{22,... | collective-permute-start | bytes 294920 | tf_op jit(solution)/shard_map/ppermute | solution.py:200
  18.7 4.7 %collective-permute-start.7 = (bf16[32,1536]{1,0:T(8,128)(2,1)S(1)}, bf16[32,1536]{1,0:T(8,128)(2,1)S(1)}, u32[]{:S(2)}, u32[]{:S(2)}) collective-permute-start(bf16[32,1536]{1,0:T(8,128)(2,1)S(1)} %collective-permute-done.3.refs_2_), channel_id=1, source_target_pairs={{0,4},{6,2},{1,5},{7,3},{8,12},{14,10},{9,13},{15,11},{16,20},{22,... | collective-permute-start | bytes 294920 | tf_op jit(solution)/shard_map/ppermute | solution.py:200
  27.0 11.7 %collective-permute-start.9 = (bf16[1,1,1,2,64,1536]{5,4,3,2,1,0:T(8,128)(2,1)S(1)}, bf16[1,1,1,2,64,1536]{5,4,3,2,1,0:T(8,128)(2,1)S(1)}, u32[]{:S(2)}, u32[]{:S(2)}) collective-permute-start(bf16[1,1,1,2,64,1536]{5,4,3,2,1,0:T(8,128)(2,1)S(1)} %bitcast.8), channel_id=1, source_target_pairs={{0,8},{8,16},{16,24},{24,0},{1,9},{9,17},{17,25},{25,1},{2,10},{10... | collective-permute-start | bytes 1179656 | tf_op jit(solution)/shard_map/ppermute | solution.py:236

commit v2 on v0

v2 whole, which is shorter than its diff:
```python
import functools

import jax
import jax.numpy as jnp
from jax import lax
from jax.experimental import pallas as pl
from jax.experimental.pallas import tpu as pltpu
from jax.sharding import PartitionSpec as P

HD = 128
EPSILON = 1e-06
MASKED = -1e30
F32 = jnp.float32
BF16 = jnp.bfloat16
VMEM = pl.BlockSpec(memory_space=pltpu.VMEM)
SMEM = pl.BlockSpec(memory_space=pltpu.SMEM)
HBM = pl.BlockSpec(memory_space=pltpu.HBM)
PARAMS = pltpu.CompilerParams(vmem_limit_bytes=32 * 1024 * 1024)


def modulate_rows(domain_ref, modulation_ref):
    table = modulation_ref[...].astype(F32)
    row = lax.broadcasted_iota(jnp.int32, table.shape, 1)
    return jnp.sum(jnp.where(row == domain_ref[0], table, 0.0), axis=1)


def normalize(rows, shift, scale):
    values = rows.astype(F32)
    centered = values - jnp.mean(values, axis=-1, keepdims=True)
    row_var = jnp.mean(centered * centered, axis=-1, keepdims=True)
    return (centered * lax.rsqrt(row_var + EPSILON) * (1.0 + scale) + shift).astype(BF16)


def normalized(refs, modulate_ref):
    shift, scale = modulate_ref[0:1, :], modulate_ref[1:2, :]
    return jnp.concatenate([normalize(r[...], shift, scale) for r in refs], axis=0)


def projected(rows, weight):
    return jnp.dot(rows, weight, preferred_element_type=F32).astype(BF16)


def load_kernel(
    inner, domain_hbm, modulation_hbm, weight_hbm, out_weight_hbm, own_hbm,
    modulate_ref, q_weight_ref, pair_weight_ref, out_weight_ref, kv_ref, domain_ref, modulation_ref, own_ref, sems
):
    first = [
        pltpu.make_async_copy(modulation_hbm, modulation_ref, sems.at[0]),
        pltpu.make_async_copy(own_hbm, own_ref, sems.at[1]),
        pltpu.make_async_copy(domain_hbm, domain_ref, sems.at[6]),
    ]
    loads = [
        pltpu.make_async_copy(
            weight_hbm.at[:, pl.ds((i + 1) * inner, inner)],
            pair_weight_ref.at[:, pl.ds(i * inner, inner)],
            sems.at[2 + i],
        )
        for i in range(2)
    ]
    rest = [
        pltpu.make_async_copy(weight_hbm.at[:, pl.ds(0, inner)], q_weight_ref, sems.at[4]),
        pltpu.make_async_copy(out_weight_hbm, out_weight_ref, sems.at[5]),
    ]
    for load in first + loads + rest:
        load.start()
    for load in first:
        load.wait()
    modulate_ref[...] = modulate_rows(domain_ref, modulation_ref)
    rows = normalized((own_ref,), modulate_ref)
    for i, load in enumerate(loads):
        load.wait()
        cols = slice(i * inner, (i + 1) * inner)
        kv_ref[:, cols] = projected(rows, pair_weight_ref[:, cols])
    for load in rest:
        load.wait()


def pair_kernel(modulate_ref, weight_ref, rows_ref, kv_ref, *normed_ref):
    rows = normalized((rows_ref,), modulate_ref)
    kv_ref[...] = projected(rows, weight_ref[...])
    for ref in normed_ref:
        ref[...] = rows


def masking(lists_ref, slots, tile_len, first, key_count, query_count):
    col_tiles = query_count // tile_len
    numbers = lists_ref[...]
    slot = jnp.full(numbers.shape, slots[0], jnp.int32)
    for d in range(1, 5):
        slot = jnp.where(numbers // col_tiles == d, slots[d], slot)
    bits = jnp.sum(
        jnp.int32(1) << (slot * col_tiles + numbers % col_tiles), axis=1, keepdims=True
    )
    tile = lax.broadcasted_iota(jnp.int32, (1, query_count), 1) // tile_len
    row = jnp.zeros((1, query_count), jnp.int32)
    for t in range(col_tiles):
        row = jnp.where(tile == t, bits[t : t + 1, :], row)
    return jnp.concatenate(
        [
            jnp.broadcast_to(
                jnp.where((row >> (first + p)) & 1 == 1, 0.0, MASKED), (tile_len, query_count)
            )
            for p in range(key_count // tile_len)
        ],
        axis=0,
    )


def head_cols(h, offset=0):
    return slice(offset + h * HD, offset + (h + 1) * HD)


def scores_of(q_ref, kv_refs, bias):
    return [
        lax.dot_general(
            jnp.concatenate([r[:, head_cols(h)] for r in kv_refs], axis=0),
            q_ref[:, head_cols(h)],
            (((1,), (1,)), ((), ())),
            preferred_element_type=F32,
        )
        + bias
        for h in range(q_ref.shape[1] // HD)
    ]


def raised_from(scores, peaks):
    return [jnp.exp((s - peaks[h : h + 1]) * HD ** (-0.5)) for h, s in enumerate(scores)]


def reduced(reduce, per_head):
    return jnp.concatenate([reduce(x, axis=0, keepdims=True) for x in per_head], axis=0)


def mixes_of(kv_refs, raised):
    inner = kv_refs[0].shape[1] // 2
    return [
        lax.dot_general(
            jnp.concatenate([r[:, head_cols(h, inner)] for r in kv_refs], axis=0),
            x.astype(BF16),
            (((0,), (0,)), ((), ())),
            preferred_element_type=F32,
        )
        for h, x in enumerate(raised)
    ]


def near_kernel(n_kv, tile_len, slots_of, lists_ref, q_weight_ref, normed_ref, *refs):
    kv_refs = refs[:n_kv]
    q_ref, peak_ref, total_ref, mix_ref = refs[n_kv:]
    q_ref[...] = projected(normed_ref[...], q_weight_ref[...])
    count = normed_ref.shape[0]
    bias = masking(lists_ref, slots_of(), tile_len, 0, n_kv * count, count)
    scores = scores_of(q_ref, kv_refs, bias)
    peaks = reduced(jnp.max, scores)
    raised = raised_from(scores, peaks)
    peak_ref[...] = peaks
    total_ref[...] = reduced(jnp.sum, raised)
    for h, mix in enumerate(mixes_of(kv_refs, raised)):
        mix_ref[head_cols(h), :] = mix


def finish_kernel(
    n_kv, tile_len, slots_of, first,
    lists_ref, modulate_ref, out_weight_ref, rows_ref, q_ref, peak_ref, total_ref, mix_ref, *refs
):
    kv_refs, (finished_ref, mixed_ref) = refs[:n_kv], refs[n_kv:]
    count = rows_ref.shape[0]
    bias = masking(lists_ref, slots_of(), tile_len, first, n_kv * count, count)
    scores = scores_of(q_ref, kv_refs, bias)
    before = peak_ref[...]
    peaks = jnp.maximum(reduced(jnp.max, scores), before)
    raised = raised_from(scores, peaks)
    kept = jnp.exp((before - peaks) * HD ** (-0.5))
    share = 1.0 / (total_ref[...] * kept + reduced(jnp.sum, raised))
    kept = kept * share
    for h, mix in enumerate(mixes_of(kv_refs, raised)):
        mixed_ref[head_cols(h), :] = (
            mix_ref[head_cols(h), :] * kept[h : h + 1] + mix * share[h : h + 1]
        ).astype(BF16)
    branch = lax.dot_general(
        mixed_ref[...],
        out_weight_ref[...],
        (((0,), (0,)), ((), ())),
        preferred_element_type=F32,
    )
    finished_ref[...] = (rows_ref[...].astype(F32) + modulate_ref[2:3, :] * branch).astype(BF16)


def swap_perm(size):
    return [(i, i ^ 1) for i in range(size)]


def relay_perm(size):
    return [(i, i + 2) for i in range(0, size - 2, 2)] + [(i, i - 2) for i in range(3, size, 2)]


def beyond_perm(size):
    return [((i + (2 if i % 2 == 0 else -2)) % size, i) for i in range(size)]


def in_hbm(x):
    return pltpu.with_memory_space_constraint(x, pltpu.HBM)


def after(x, *others):
    return lax.optimization_barrier((x, *others))[0]


def call(kernel, ins, outs, args, scratch=(), name=None):
    return pl.pallas_call(
        kernel,
        out_shape=outs,
        in_specs=ins,
        out_specs=[VMEM] * len(outs),
        scratch_shapes=scratch,
        compiler_params=PARAMS,
        name=name,
    )(*args)


def body(clip_tokens, qkv_weight, out_weight, modulation, domain_ids, tile_lists):
    col_tiles, tile_len, width = clip_tokens.shape[3:]
    own_count = col_tiles * tile_len
    inner = out_weight.shape[1]
    heads = inner // HD
    frames, rows = lax.axis_size("frame"), lax.axis_size("row")
    segments = lax.axis_size("segment")
    modulation_table = jnp.transpose(modulation[0], (1, 0, 2))
    weight = qkv_weight[0]
    own = clip_tokens.reshape(own_count, width)

    def held(count, wide, dtype=BF16):
        return pltpu.VMEM((count, wide), dtype)

    tokens = lax.ppermute(own, "frame", swap_perm(frames))
    beyond = [lax.ppermute(own, "frame", beyond_perm(frames))] if frames > 2 else []
    lists = lax.ppermute(tile_lists[0, 0], "frame", swap_perm(frames))

    modulate, q_weight, pair_weight, out_w, kv_own = call(
        functools.partial(load_kernel, inner),
        [pl.BlockSpec(memory_space=pl.ANY)] + [HBM] * 4,
        [
            held(3, width, F32),
            held(width, inner),
            held(width, 2 * inner),
            held(inner, width),
            held(own_count, 2 * inner),
        ],
        [domain_ids, *map(in_hbm, (modulation_table, weight, out_weight[0], own))],
        [
            pltpu.SMEM(domain_ids.shape, jnp.int32),
            pltpu.VMEM(modulation_table.shape, BF16),
            pltpu.VMEM((own_count, width), BF16),
            pltpu.SemaphoreType.DMA((7,)),
        ],
        "own_pairs",
    )

    def slots_of():
        odd_frame = 1 - lax.axis_index("frame") % 2
        odd_row = lax.axis_index("row") % 2
        row_slot = 2 + len(beyond)
        return [
            0,
            2 - odd_frame,
            1 + odd_frame,
            row_slot + 1 - odd_row,
            row_slot + odd_row,
        ]

    def pairs_of(arrived, name, with_rows=False):
        outs = [held(own_count, 2 * inner)] + [held(own_count, width)] * with_rows
        return call(pair_kernel, [VMEM] * 3, outs, [modulate, pair_weight, arrived], name=name)

    tokens, lists = lax.optimization_barrier((tokens, lists, kv_own))[:2]
    kv_tokens, normed = pairs_of(tokens, "pairs", True)
    kv_rows = [lax.ppermute(kv_tokens, "row", swap_perm(rows))]
    if rows > 2:
        kv_rows.append(lax.ppermute(kv_rows[0], "row", relay_perm(rows)))
    kv_beyond = [pairs_of(after(b, kv_tokens), "beyond_pairs")[0] for b in beyond]
    near = [kv_tokens, kv_own, *kv_beyond]
    q, *partial = call(
        functools.partial(near_kernel, len(near), tile_len, slots_of),
        [VMEM] * (3 + len(near)),
        [
            held(own_count, inner),
            held(heads, own_count, F32),
            held(heads, own_count, F32),
            held(inner, own_count, F32),
        ],
        [lists, q_weight, normed, *near],
        name="near_attention",
    )
    (finished,) = call(
        functools.partial(
            finish_kernel, len(kv_rows), tile_len, slots_of, len(near) * col_tiles
        ),
        [VMEM] * (8 + len(kv_rows)),
        [jax.ShapeDtypeStruct((own_count, width), BF16)],
        [lists, modulate, out_w, tokens, q, *partial, *kv_rows],
        [pltpu.VMEM((inner, own_count), BF16)],
        name="finish",
    )
    onward = [
        (s * frames + f, (s + 1) % segments * frames + (f ^ 1))
        for s in range(segments)
        for f in range(frames)
    ]
    return lax.ppermute(finished.reshape(clip_tokens.shape), ("segment", "frame"), onward)


def solution(mesh):
    return jax.shard_map(
        body,
        mesh=mesh,
        in_specs=(
            P("segment", "frame", "row", None, None, None),
            P("segment", None, None),
            P("segment", None, None),
            P("segment", None, None, None),
            P("segment"),
            P("frame", "row", None, None),
        ),
        out_specs=P("segment", "frame", "row", None, None, None),
        check_vma=False,
    )
```

time: 75.1 us -> 32.4 us (0.43)
  local copies, waits for them, and re-layouts: 21.2 us -> 0.75 us
  waiting for transfers between devices: 27 us -> 14.7 us
  matrix products: 10.7 us -> 0 us
  Pallas kernels: 0 us -> 8.44 us
  other arithmetic: 4.2 us -> 0 us
  starting transfers between devices: 10.4 us -> 7.58 us
    ppermute x5, waiting for transfers between devices: 27 us -> 14.7 us  [the longest x1 11.8 us: body(): lax.ppermute(finished.reshape(clip_tokens.shape), ('segment', 'frame'), o...]
    dot_general x5 -> x0, matrix products: 10.7 us -> none  [the longest x1 4.1 us: body(): projected = jnp.dot(normed, weight, preferred_element_type=jnp.float32)]
    slice x5 -> x0, local copies, waits for them, and re-layouts: 8.67 us -> none  [the longest x2 5.6 us: body(): picked[..., :inner_width].reshape(col_tiles, key_count, head_count, HD)]
    pallas_call x0 -> x5, Pallas kernels: none -> 8.44 us  [call(): pl.pallas_call(kernel, out_shape=outs, in_specs=ins, out_specs=[VMEM] * l...]
    unnamed x15 -> x1, local copies, waits for them, and re-layouts: 5.89 us -> 0.75 us
    gather x1 -> x0, local copies, waits for them, and re-layouts: 3.73 us -> none  [body(): picked = candidates[chosen].reshape(col_tiles, -1, 2 * inner_width)]
    ppermute x5, starting transfers between devices: 10.4 us -> 7.58 us  [the longest x1 2.94 us: body(): tokens = lax.ppermute(own, 'frame', swap_perm(frames))]
    reduce_sum x2 -> x0, other arithmetic: 2.38 us -> none  [the longest x1 1.25 us: normalize(): row_var = jnp.mean(centered * centered, axis=-1, keepdims=True)]
  transfers between devices with their start and end apart: 5 -> 5, of which waited for: 4 -> 3; matrix products, arithmetic and copies ran while one was open for 9% -> 0% of each run, Pallas kernels for 0% -> 23%
where the time goes in v2:
time: 32.4 us; the launch traced here: 32.2 us
  waiting for transfers between devices  14.7 us (45%)
  Pallas kernels  8.44 us (26%)
  starting transfers between devices  7.58 us (23%)
  local copies, waits for them, and re-layouts  0.75 us (2%)
  between operations  0.71 us (2%)
    ppermute x1, waiting for transfers between devices, body(): lax.ppermute(finished.reshape(clip_tokens.shape), ('segment', 'frame'), o...  11.8 us
    pallas_call x5, Pallas kernels, call(): pl.pallas_call(kernel, out_shape=outs, in_specs=ins, out_specs=[VMEM] * l...  8.44 us
    ppermute x1, starting transfers between devices, body(): tokens = lax.ppermute(own, 'frame', swap_perm(frames))  2.94 us
    ppermute x1, waiting for transfers between devices, body(): lists = lax.ppermute(tile_lists[0, 0], 'frame', swap_perm(frames))  2.64 us
    ppermute x1, starting transfers between devices, body(): lax.ppermute(finished.reshape(clip_tokens.shape), ('segment', 'frame'), o...  2.52 us
    ppermute x1, starting transfers between devices, body(): lax.ppermute(own, 'frame', beyond_perm(frames))  1.52 us
    unnamed x1, local copies, waits for them, and re-layouts  0.75 us
  transfers between devices with their start and end apart: 5, of which 3 were waited for; matrix products, arithmetic and copies ran while one was open for 0% of the time, Pallas kernels for 23%

profile of v2, /device:TPU:0, one launch (start us, length us, event | category | flops | bytes accessed | tf_op | source)
XLA Modules:
  0.0 32.2 jit_solution(2510061182341912538)
XLA Ops:
  0.0 2.9 %collective-permute-start = (bf16[128,1536]{1,0:T(8,128)(2,1)}, bf16[128,1536]{1,0:T(8,128)(2,1)S(1)}, u32[]{:S(2)}, u32[]{:S(2)}) collective-permute-start(bf16[128,1536]{1,0:T(8,128)(2,1)} %bitcast.11), channel_id=1, source_target_pairs={{0,2},{2,0},{4,6},{6,4},{1,3},{3,1},{5,7},{7,5},{8,10},{10,8},{12,... | collective-permute-start | bytes 1179656 | tf_op jit(solution)/shard_map/ppermute | solution.py:235
  2.9 1.5 %collective-permute-start.2 = (bf16[128,1536]{1,0:T(8,128)(2,1)}, bf16[128,1536]{1,0:T(8,128)(2,1)S(1)}, u32[]{:S(2)}, u32[]{:S(2)}) collective-permute-start(bf16[128,1536]{1,0:T(8,128)(2,1)} %bitcast.12), channel_id=1, source_target_pairs={{4,0},{6,2},{0,4},{2,6},{5,1},{7,3},{1,5},{3,7},{12,8},{14,10},{8,... | collective-permute-start | bytes 1179656 | tf_op jit(solution)/shard_map/ppermute | solution.py:236
  4.5 0.5 %collective-permute-start.1 = (s32[2,6]{1,0:T(2,128)}, s32[2,6]{1,0:T(2,128)S(1)}, u32[]{:S(2)}, u32[]{:S(2)}) collective-permute-start(s32[2,6]{1,0:T(2,128)} %bitcast.15), channel_id=1, source_target_pairs={{0,2},{2,0},{4,6},{6,4},{1,3},{3,1},{5,7},{7,5},{8,10},{10,8},{12,... | collective-permute-start | bytes 152 | tf_op jit(solution)/shard_map/ppermute | solution.py:237
  5.6 4.0 %own_pairs.1 = (f32[3,1536]{1,0:T(4,128)S(1)}, bf16[1536,768]{1,0:T(8,128)(2,1)S(1)}, bf16[1536,1536]{1,0:T(8,128)(2,1)S(1)}, bf16[768,1536]{1,0:T(8,128)(2,1)S(1)}, bf16[128,1536]{1,0:T(8,128)(2,1)S(1)}) custom-call(s32[1]{0:T(128)S(6)} %copy.8.domain_hbm, bf16[3,8,1536]{2,1,0:T(8,128)(2,1)} %bitcast.14, bf16[1536,2304]{1,0:T(8,128)(2,1)} %bitcast.9, ...), custom_call_target="tpu_custom_call" | custom-call | tf_op jit(solution)/shard_map/own_pairs/pallas_call | solution.py:210
  9.7 2.6 %collective-permute-done.1.lists_ref = s32[2,6]{1,0:T(2,128)S(1)} collective-permute-done((s32[2,6]{1,0:T(2,128)}, s32[2,6]{1,0:T(2,128)S(1)}, u32[]{:S(2)}, u32[]{:S(2)}) %collective-permute-start.1) | collective-permute-done | bytes 80 | tf_op jit(solution)/shard_map/ppermute | solution.py:237
  12.3 0.0 collective-permute-done.rows_ref
  12.3 1.0 %pairs.1 = (bf16[128,1536]{1,0:T(8,128)(2,1)S(1)}, bf16[128,1536]{1,0:T(8,128)(2,1)S(1)}) custom-call(f32[3,1536]{1,0:T(4,128)S(1)} %get-tuple-element.21.modulate_ref, bf16[1536,1536]{1,0:T(8,128)(2,1)S(1)} %get-tuple-element.25.weight_ref, bf16[128,1536]{1,0:T(8,128)(2,1)S(1)} %collective-permute-done.rows_ref), custom_call_target="tpu_custom_call" | custom-call | tf_op jit(solution)/shard_map/pairs/pallas_call | solution.py:210
  13.3 0.1 collective-permute-start.3
  13.4 0.3 collective-permute-done.2.rows_ref
  13.7 1.0 %beyond_pairs.1.refs_2_ = bf16[128,1536]{1,0:T(8,128)(2,1)S(1)} custom-call(f32[3,1536]{1,0:T(4,128)S(1)} %get-tuple-element.21.modulate_ref, bf16[1536,1536]{1,0:T(8,128)(2,1)S(1)} %get-tuple-element.25.weight_ref, bf16[128,1536]{1,0:T(8,128)(2,1)S(1)} %collective-permute-done.2.rows_ref), custom_call_target="tpu_custom_call" | custom-call | tf_op jit(solution)/shard_map/beyond_pairs/pallas_call | solution.py:210
  14.8 1.4 %near_attention.1 = (bf16[128,768]{1,0:T(8,128)(2,1)S(1)}, f32[6,128]{1,0:T(8,128)S(1)}, f32[6,128]{1,0:T(8,128)S(1)}, f32[768,128]{1,0:T(8,128)S(1)}) custom-call(s32[2,6]{1,0:T(2,128)S(1)} %collective-permute-done.1.lists_ref, bf16[1536,768]{1,0:T(8,128)(2,1)S(1)} %get-tuple-element.24.q_weight_ref, bf16[128,1536]{1,0:T(8,128)(2,1)S(1)} %get-tuple-element.26.normed_ref, ...), custom_call_target="tpu_custom_call" | custom-call | tf_op jit(solution)/shard_map/near_attention/pallas_call | solution.py:210
  16.1 0.0 collective-permute-done.3.refs_0_
  16.1 1.0 %finish.1 = bf16[128,1536]{1,0:T(8,128)(2,1)S(1)} custom-call(s32[2,6]{1,0:T(2,128)S(1)} %collective-permute-done.1.lists_ref, f32[3,1536]{1,0:T(4,128)S(1)} %get-tuple-element.21.modulate_ref, bf16[768,1536]{1,0:T(8,128)(2,1)S(1)} %get-tuple-element.22.out_weight_ref, bf16[128,1536]{1,0:T(8,128)(2,1)S(1)} %collective-permute-done.rows_ref, ...), custom_call_target="tpu_custom_call" | custom-call | tf_op jit(solution)/shard_map/finish/pallas_call | solution.py:210
  17.2 2.5 %collective-permute-start.4 = (bf16[1,1,1,2,64,1536]{5,4,3,2,1,0:T(8,128)(2,1)S(1)}, bf16[1,1,1,2,64,1536]{5,4,3,2,1,0:T(8,128)(2,1)S(1)}, u32[]{:S(2)}, u32[]{:S(2)}) collective-permute-start(bf16[1,1,1,2,64,1536]{5,4,3,2,1,0:T(8,128)(2,1)S(1)} %bitcast.8), channel_id=1, source_target_pairs={{0,10},{2,8},{4,14},{6,12},{8,18},{10,16},{12,22},{14,20},{16,26},... | collective-permute-start | bytes 1179656 | tf_op jit(solution)/shard_map/ppermute | solution.py:309
  19.7 11.8 %collective-permute-done.4 = bf16[1,1,1,2,64,1536]{5,4,3,2,1,0:T(8,128)(2,1)S(1)} collective-permute-done((bf16[1,1,1,2,64,1536]{5,4,3,2,1,0:T(8,128)(2,1)S(1)}, bf16[1,1,1,2,64,1536]{5,4,3,2,1,0:T(8,128)(2,1)S(1)}, u32[]{:S(2)}, u32[]{:S(2)}) %collective-permute-start.4) | collective-permute-done | bytes 393248 | tf_op jit(solution)/shard_map/ppermute | solution.py:309
  31.5 0.7 %copy.9 = bf16[1,1,1,2,64,1536]{5,4,3,2,1,0:T(8,128)(2,1)} copy(bf16[1,1,1,2,64,1536]{5,4,3,2,1,0:T(8,128)(2,1)S(1)} %collective-permute-done.4) | data formatting | bytes 786432
Async XLA Ops:
  0.0 12.3 %collective-permute-start = (bf16[128,1536]{1,0:T(8,128)(2,1)}, bf16[128,1536]{1,0:T(8,128)(2,1)S(1)}, u32[]{:S(2)}, u32[]{:S(2)}) collective-permute-start(bf16[128,1536]{1,0:T(8,128)(2,1)} %bitcast.11), channel_id=1, source_target_pairs={{0,2},{2,0},{4,6},{6,4},{1,3},{3,1},{5,7},{7,5},{8,10},{10,8},{12,... | collective-permute-start | bytes 1179656 | tf_op jit(solution)/shard_map/ppermute | solution.py:235
  2.9 10.8 %collective-permute-start.2 = (bf16[128,1536]{1,0:T(8,128)(2,1)}, bf16[128,1536]{1,0:T(8,128)(2,1)S(1)}, u32[]{:S(2)}, u32[]{:S(2)}) collective-permute-start(bf16[128,1536]{1,0:T(8,128)(2,1)} %bitcast.12), channel_id=1, source_target_pairs={{4,0},{6,2},{0,4},{2,6},{5,1},{7,3},{1,5},{3,7},{12,8},{14,10},{8,... | collective-permute-start | bytes 1179656 | tf_op jit(solution)/shard_map/ppermute | solution.py:236
  4.5 7.9 %collective-permute-start.1 = (s32[2,6]{1,0:T(2,128)}, s32[2,6]{1,0:T(2,128)S(1)}, u32[]{:S(2)}, u32[]{:S(2)}) collective-permute-start(s32[2,6]{1,0:T(2,128)} %bitcast.15), channel_id=1, source_target_pairs={{0,2},{2,0},{4,6},{6,4},{1,3},{3,1},{5,7},{7,5},{8,10},{10,8},{12,... | collective-permute-start | bytes 152 | tf_op jit(solution)/shard_map/ppermute | solution.py:237
  13.3 2.8 %collective-permute-start.3 = (bf16[128,1536]{1,0:T(8,128)(2,1)S(1)}, bf16[128,1536]{1,0:T(8,128)(2,1)S(1)}, u32[]{:S(2)}, u32[]{:S(2)}) collective-permute-start(bf16[128,1536]{1,0:T(8,128)(2,1)S(1)} %get-tuple-element.27.refs_0_), channel_id=1, source_target_pairs={{0,1},{1,0},{2,3},{3,2},{4,5},{5,4},{6,7},{7,6},{8,9},{9,8},{10,11... | collective-permute-start | bytes 1179656 | tf_op jit(solution)/shard_map/ppermute | solution.py:277
  17.2 14.3 %collective-permute-start.4 = (bf16[1,1,1,2,64,1536]{5,4,3,2,1,0:T(8,128)(2,1)S(1)}, bf16[1,1,1,2,64,1536]{5,4,3,2,1,0:T(8,128)(2,1)S(1)}, u32[]{:S(2)}, u32[]{:S(2)}) collective-permute-start(bf16[1,1,1,2,64,1536]{5,4,3,2,1,0:T(8,128)(2,1)S(1)} %bitcast.8), channel_id=1, source_target_pairs={{0,10},{2,8},{4,14},{6,12},{8,18},{10,16},{12,22},{14,20},{16,26},... | collective-permute-start | bytes 1179656 | tf_op jit(solution)/shard_map/ppermute | solution.py:309

commit v3 on v2

--- a/solution.py
+++ b/solution.py
@@ -10,6 +10,8 @@
 HD = 128
 EPSILON = 1e-06
 MASKED = -1e30
+RAW = 4
+LOADS = 4
 F32 = jnp.float32
 BF16 = jnp.bfloat16
 VMEM = pl.BlockSpec(memory_space=pltpu.VMEM)
@@ -41,27 +43,25 @@
 
 
 def load_kernel(
-    inner, domain_hbm, modulation_hbm, weight_hbm, out_weight_hbm, own_hbm,
-    modulate_ref, q_weight_ref, pair_weight_ref, out_weight_ref, kv_ref, domain_ref, modulation_ref, own_ref, sems
+    inner, domain_hbm, modulation_hbm, weight_hbm, own_hbm,
+    modulate_ref, weight_ref, kv_ref, *refs
 ):
+    *tail_ref, domain_ref, modulation_ref, own_ref, sems = refs
     first = [
-        pltpu.make_async_copy(modulation_hbm, modulation_ref, sems.at[0]),
-        pltpu.make_async_copy(own_hbm, own_ref, sems.at[1]),
-        pltpu.make_async_copy(domain_hbm, domain_ref, sems.at[6]),
-    ]
+        pltpu.make_async_copy(domain_hbm, domain_ref, sems.at[0]),
+        pltpu.make_async_copy(modulation_hbm, modulation_ref, sems.at[1]),
+        pltpu.make_async_copy(own_hbm, own_ref, sems.at[2]),
+    ]
+    part = 2 * inner // LOADS
     loads = [
         pltpu.make_async_copy(
-            weight_hbm.at[:, pl.ds((i + 1) * inner, inner)],
-            pair_weight_ref.at[:, pl.ds(i * inner, inner)],
-            sems.at[2 + i],
+            weight_hbm.at[:, pl.ds(inner + i * part, part)],
+            weight_ref.at[:, pl.ds(i * part, part)],
+            sems.at[3 + i],
         )
-        for i in range(2)
-    ]
-    rest = [
-        pltpu.make_async_copy(weight_hbm.at[:, pl.ds(0, inner)], q_weight_ref, sems.at[4]),
-        pltpu.make_async_copy(out_weight_hbm, out_weight_ref, sems.at[5]),
-    ]
-    for load in first + loads + rest:
+        for i in range(LOADS)
+    ]
+    for load in first + loads:
         load.start()
     for load in first:
         load.wait()
@@ -69,17 +69,32 @@
     rows = normalized((own_ref,), modulate_ref)
     for i, load in enumerate(loads):
         load.wait()
-        cols = slice(i * inner, (i + 1) * inner)
-        kv_ref[:, cols] = projected(rows, pair_weight_ref[:, cols])
-    for load in rest:
+        cols = slice(i * part, (i + 1) * part)
+        pairs = projected(rows, weight_ref[:, cols])
+        kv_ref[:, cols] = pairs
+        for ref in tail_ref:
+            ref[:, cols] = pairs[rows.shape[0] - ref.shape[0] :]
+
+
+def beyond_kernel(inner, n_rows, weight_hbm, out_weight_hbm, modulate_ref, pair_weight_ref, *refs):
+    rows_refs, (q_weight_ref, out_weight_ref) = refs[:n_rows], refs[n_rows : n_rows + 2]
+    *kv_refs, sems = refs[n_rows + 2 :]
+    loads = [
+        pltpu.make_async_copy(weight_hbm.at[:, pl.ds(0, inner)], q_weight_ref, sems.at[0]),
+        pltpu.make_async_copy(out_weight_hbm, out_weight_ref, sems.at[1]),
+    ]
+    for load in loads:
+        load.start()
+    for rows_ref, kv_ref in zip(rows_refs, kv_refs):
+        kv_ref[...] = projected(normalized((rows_ref,), modulate_ref), pair_weight_ref[...])
+    for load in loads:
         load.wait()
 
 
-def pair_kernel(modulate_ref, weight_ref, rows_ref, kv_ref, *normed_ref):
+def pair_kernel(modulate_ref, weight_ref, rows_ref, kv_ref, normed_ref):
     rows = normalized((rows_ref,), modulate_ref)
+    normed_ref[...] = rows
     kv_ref[...] = projected(rows, weight_ref[...])
-    for ref in normed_ref:
-        ref[...] = rows
 
 
 def masking(lists_ref, slots, tile_len, first, key_count, query_count):
@@ -148,8 +163,8 @@
     kv_refs = refs[:n_kv]
     q_ref, peak_ref, total_ref, mix_ref = refs[n_kv:]
     q_ref[...] = projected(normed_ref[...], q_weight_ref[...])
-    count = normed_ref.shape[0]
-    bias = masking(lists_ref, slots_of(), tile_len, 0, n_kv * count, count)
+    count, key_count = normed_ref.shape[0], sum(r.shape[0] for r in kv_refs)
+    bias = masking(lists_ref, slots_of(), tile_len, 0, key_count, count)
     scores = scores_of(q_ref, kv_refs, bias)
     peaks = reduced(jnp.max, scores)
     raised = raised_from(scores, peaks)
@@ -206,7 +221,7 @@
     return lax.optimization_barrier((x, *others))[0]
 
 
-def call(kernel, ins, outs, args, scratch=(), name=None):
+def call(kernel, ins, outs, args, scratch=(), name=None, weight=1):
     return pl.pallas_call(
         kernel,
         out_shape=outs,
@@ -214,6 +229,7 @@
         out_specs=[VMEM] * len(outs),
         scratch_shapes=scratch,
         compiler_params=PARAMS,
+        cost_estimate=pl.CostEstimate(flops=weight, bytes_accessed=0, transcendentals=0),
         name=name,
     )(*args)
 
@@ -232,52 +248,66 @@
     def held(count, wide, dtype=BF16):
         return pltpu.VMEM((count, wide), dtype)
 
-    tokens = lax.ppermute(own, "frame", swap_perm(frames))
-    beyond = [lax.ppermute(own, "frame", beyond_perm(frames))] if frames > 2 else []
-    lists = lax.ppermute(tile_lists[0, 0], "frame", swap_perm(frames))
-
-    modulate, q_weight, pair_weight, out_w, kv_own = call(
+    def from_partner(x):
+        return lax.ppermute(x, "frame", swap_perm(frames))
+
+    def from_beyond(x):
+        return lax.ppermute(x, "frame", beyond_perm(frames))
+
+    tokens = from_partner(own)
+    lists = from_partner(tile_lists[0, 0])
+    far = frames > 2
+    sent = own_count * RAW // 8
+    beyond = [from_beyond(own[:sent])] if far else []
+
+    modulate, pair_weight, kv_own, *tail = call(
         functools.partial(load_kernel, inner),
-        [pl.BlockSpec(memory_space=pl.ANY)] + [HBM] * 4,
-        [
-            held(3, width, F32),
-            held(width, inner),
-            held(width, 2 * inner),
-            held(inner, width),
-            held(own_count, 2 * inner),
-        ],
-        [domain_ids, *map(in_hbm, (modulation_table, weight, out_weight[0], own))],
+        [pl.BlockSpec(memory_space=pl.ANY)] + [HBM] * 3,
+        [held(3, width, F32), held(width, 2 * inner), held(own_count, 2 * inner)]
+        + [held(own_count - sent, 2 * inner)] * far,
+        [domain_ids, *map(in_hbm, (modulation_table, weight, own))],
         [
             pltpu.SMEM(domain_ids.shape, jnp.int32),
             pltpu.VMEM(modulation_table.shape, BF16),
             pltpu.VMEM((own_count, width), BF16),
-            pltpu.SemaphoreType.DMA((7,)),
+            pltpu.SemaphoreType.DMA((3 + LOADS,)),
         ],
         "own_pairs",
     )
+    kv_tail = [from_beyond(t) for t in tail]
+    q_weight, out_w, *kv_beyond = call(
+        functools.partial(beyond_kernel, inner, len(beyond)),
+        [HBM] * 2 + [VMEM] * (2 + len(beyond)),
+        [held(width, inner), held(inner, width)] + [held(sent, 2 * inner)] * far,
+        [in_hbm(weight), in_hbm(out_weight[0]), modulate, pair_weight, *beyond],
+        [pltpu.SemaphoreType.DMA((2,))],
+        "beyond_pairs",
+    )
+    kv_beyond += kv_tail
+    near_tiles = 2 + far
 
     def slots_of():
         odd_frame = 1 - lax.axis_index("frame") % 2
         odd_row = lax.axis_index("row") % 2
-        row_slot = 2 + len(beyond)
         return [
             0,
             2 - odd_frame,
             1 + odd_frame,
-            row_slot + 1 - odd_row,
-            row_slot + odd_row,
+            near_tiles + 1 - odd_row,
+            near_tiles + odd_row,
         ]
 
-    def pairs_of(arrived, name, with_rows=False):
-        outs = [held(own_count, 2 * inner)] + [held(own_count, width)] * with_rows
-        return call(pair_kernel, [VMEM] * 3, outs, [modulate, pair_weight, arrived], name=name)
-
-    tokens, lists = lax.optimization_barrier((tokens, lists, kv_own))[:2]
-    kv_tokens, normed = pairs_of(tokens, "pairs", True)
+    tokens = after(tokens, q_weight)
+    kv_tokens, normed = call(
+        pair_kernel,
+        [VMEM] * 3,
+        [held(own_count, 2 * inner), held(own_count, width)],
+        [modulate, pair_weight, tokens],
+        name="pairs",
+    )
     kv_rows = [lax.ppermute(kv_tokens, "row", swap_perm(rows))]
     if rows > 2:
         kv_rows.append(lax.ppermute(kv_rows[0], "row", relay_perm(rows)))
-    kv_beyond = [pairs_of(after(b, kv_tokens), "beyond_pairs")[0] for b in beyond]
     near = [kv_tokens, kv_own, *kv_beyond]
     q, *partial = call(
         functools.partial(near_kernel, len(near), tile_len, slots_of),
@@ -290,16 +320,17 @@
         ],
         [lists, q_weight, normed, *near],
         name="near_attention",
+        weight=10**10,
     )
     (finished,) = call(
         functools.partial(
-            finish_kernel, len(kv_rows), tile_len, slots_of, len(near) * col_tiles
+            finish_kernel, len(kv_rows), tile_len, slots_of, near_tiles * col_tiles
         ),
         [VMEM] * (8 + len(kv_rows)),
         [jax.ShapeDtypeStruct((own_count, width), BF16)],
         [lists, modulate, out_w, tokens, q, *partial, *kv_rows],
         [pltpu.VMEM((inner, own_count), BF16)],
-        name="finish",
+        "finish",
     )
     onward = [
         (s * frames + f, (s + 1) % segments * frames + (f ^ 1))

time: 32.4 us -> 31.5 us (0.972)
  waiting for transfers between devices: 14.7 us -> 13.2 us
  local copies, waits for them, and re-layouts: 0.75 us -> 1.73 us
  starting transfers between devices: 7.58 us -> 6.88 us
  Pallas kernels: 8.44 us -> 8.79 us
    ppermute x3 -> x4, waiting for transfers between devices: 2.94 us -> 1.93 us  [the longest x2 1.92 us: from_beyond(): return lax.ppermute(x, 'frame', beyond_perm(frames))]
    slice x0 -> x1, local copies, waits for them, and re-layouts: none -> 0.97 us  [body(): beyond = [from_beyond(own[:sent])] if far else []]
    ppermute x1, starting transfers between devices: 2.52 us -> 1.6 us  [body(): lax.ppermute(finished.reshape(clip_tokens.shape), ('segment', 'frame'), o...]
    ppermute x1, waiting for transfers between devices: 11.8 us -> 11.3 us  [body(): lax.ppermute(finished.reshape(clip_tokens.shape), ('segment', 'frame'), o...]
    pallas_call x5, Pallas kernels: 8.44 us -> 8.79 us  [call(): pl.pallas_call(kernel, out_shape=outs, in_specs=ins, out_specs=[VMEM] * l...]
    ppermute x3 -> x4, starting transfers between devices: 4.99 us -> 5.21 us  [the longest x2 3.05 us: from_partner(): return lax.ppermute(x, 'frame', swap_perm(frames))]
    unnamed x1 -> x3, local copies, waits for them, and re-layouts: 0.75 us -> 0.75 us
  transfers between devices with their start and end apart: 5 -> 6, of which waited for: 3 -> 3; matrix products, arithmetic and copies ran while one was open for 0% -> 3% of each run, Pallas kernels for 23% -> 25%
where the time goes in v3:
time: 31.5 us; the launch traced here: 31.3 us
  waiting for transfers between devices  13.2 us (42%)
  Pallas kernels  8.79 us (28%)
  starting transfers between devices  6.88 us (22%)
  local copies, waits for them, and re-layouts  1.73 us (5%)
  between operations  0.74 us (2%)
    ppermute x1, waiting for transfers between devices, body(): lax.ppermute(finished.reshape(clip_tokens.shape), ('segment', 'frame'), o...  11.3 us
    pallas_call x5, Pallas kernels, call(): pl.pallas_call(kernel, out_shape=outs, in_specs=ins, out_specs=[VMEM] * l...  8.79 us
    ppermute x2, starting transfers between devices, from_partner(): return lax.ppermute(x, 'frame', swap_perm(frames))  3.05 us
    ppermute x2, starting transfers between devices, from_beyond(): return lax.ppermute(x, 'frame', beyond_perm(frames))  2.16 us
    ppermute x2, waiting for transfers between devices, from_beyond(): return lax.ppermute(x, 'frame', beyond_perm(frames))  1.92 us
    ppermute x1, starting transfers between devices, body(): lax.ppermute(finished.reshape(clip_tokens.shape), ('segment', 'frame'), o...  1.6 us
    slice x1, local copies, waits for them, and re-layouts, body(): beyond = [from_beyond(own[:sent])] if far else []  0.97 us
    unnamed x3, local copies, waits for them, and re-layouts  0.75 us
  transfers between devices with their start and end apart: 6, of which 3 were waited for; matrix products, arithmetic and copies ran while one was open for 3% of the time, Pallas kernels for 25%

profile of v3, /device:TPU:0, one launch (start us, length us, event | category | flops | bytes accessed | tf_op | source)
XLA Modules:
  0.0 31.3 jit_solution(3173328497299649078)
XLA Ops:
  0.0 2.9 %collective-permute-start.2 = (bf16[128,1536]{1,0:T(8,128)(2,1)}, bf16[128,1536]{1,0:T(8,128)(2,1)S(1)}, u32[]{:S(2)}, u32[]{:S(2)}) collective-permute-start(bf16[128,1536]{1,0:T(8,128)(2,1)} %bitcast.14), channel_id=1, source_target_pairs={{0,2},{2,0},{4,6},{6,4},{1,3},{3,1},{5,7},{7,5},{8,10},{10,8},{12,... | collective-permute-start | bytes 1179656 | tf_op jit(solution)/shard_map/ppermute | solution.py:252
  2.9 1.0 %slice_bitcast_fusion = bf16[64,1536]{1,0:T(8,128)(2,1)S(1)} fusion(bf16[1,1,1,2,64,1536]{5,4,3,2,1,0:T(8,128)(2,1)} %param.6), kind=kLoop, calls=%fused_computation | loop fusion | bytes 393216 | tf_op jit(solution)/shard_map/slice | solution.py:261
  3.9 1.6 %collective-permute-start.1 = (bf16[64,1536]{1,0:T(8,128)(2,1)S(1)}, bf16[64,1536]{1,0:T(8,128)(2,1)S(1)}, u32[]{:S(2)}, u32[]{:S(2)}) collective-permute-start(bf16[64,1536]{1,0:T(8,128)(2,1)S(1)} %slice_bitcast_fusion), channel_id=1, source_target_pairs={{4,0},{6,2},{0,4},{2,6},{5,1},{7,3},{1,5},{3,7},{12,8},{14,10},{8,... | collective-permute-start | bytes 589832 | tf_op jit(solution)/shard_map/ppermute | solution.py:255
  6.2 0.0 copy-start
  6.2 3.0 %own_pairs.1 = (f32[3,1536]{1,0:T(4,128)S(1)}, bf16[1536,1536]{1,0:T(8,128)(2,1)S(1)}, bf16[128,1536]{1,0:T(8,128)(2,1)S(1)}, bf16[64,1536]{1,0:T(8,128)(2,1)S(1)}) custom-call(s32[1]{0:T(128)S(6)} %copy.8.domain_hbm, bf16[3,8,1536]{2,1,0:T(8,128)(2,1)} %bitcast.16, bf16[1536,2304]{1,0:T(8,128)(2,1)} %bitcast.11, bf16[128,1536]{1,0:T(8,128)(2,1)} %bitcast.15), custom_call_target="tpu_custom_call" | custom-call | flops 1 | tf_op jit(solution)/shard_map/own_pairs/pallas_call | solution.py:225
  9.2 0.6 %collective-permute-start.3 = (bf16[64,1536]{1,0:T(8,128)(2,1)S(1)}, bf16[64,1536]{1,0:T(8,128)(2,1)S(1)}, u32[]{:S(2)}, u32[]{:S(2)}) collective-permute-start(bf16[64,1536]{1,0:T(8,128)(2,1)S(1)} %get-tuple-element.28), channel_id=1, source_target_pairs={{4,0},{6,2},{0,4},{2,6},{5,1},{7,3},{1,5},{3,7},{12,8},{14,10},{8,... | collective-permute-start | bytes 589832 | tf_op jit(solution)/shard_map/ppermute | solution.py:255
  9.7 0.0 copy-done
  9.7 0.1 collective-permute-start
  9.9 0.5 %collective-permute-done.1.refs_0_ = bf16[64,1536]{1,0:T(8,128)(2,1)S(1)} collective-permute-done((bf16[64,1536]{1,0:T(8,128)(2,1)S(1)}, bf16[64,1536]{1,0:T(8,128)(2,1)S(1)}, u32[]{:S(2)}, u32[]{:S(2)}) %collective-permute-start.1) | collective-permute-done | bytes 196640 | tf_op jit(solution)/shard_map/ppermute | solution.py:255
  10.3 2.4 %beyond_pairs.1 = (bf16[1536,768]{1,0:T(8,128)(2,1)S(1)}, bf16[768,1536]{1,0:T(8,128)(2,1)S(1)}, bf16[64,1536]{1,0:T(8,128)(2,1)S(1)}) custom-call(bf16[1536,2304]{1,0:T(8,128)(2,1)} %bitcast.12, bf16[768,1536]{1,0:T(8,128)(2,1)} %bitcast.13, f32[3,1536]{1,0:T(4,128)S(1)} %get-tuple-element.19.modulate_ref, ...), custom_call_target="tpu_custom_call" | custom-call | flops 1 | tf_op jit(solution)/shard_map/beyond_pairs/pallas_call | solution.py:225
  12.8 0.0 collective-permute-done.2.rows_ref
  12.8 1.0 %pairs.1 = (bf16[128,1536]{1,0:T(8,128)(2,1)S(1)}, bf16[128,1536]{1,0:T(8,128)(2,1)S(1)}) custom-call(f32[3,1536]{1,0:T(4,128)S(1)} %get-tuple-element.19.modulate_ref, bf16[1536,1536]{1,0:T(8,128)(2,1)S(1)} %get-tuple-element.20.pair_weight_ref.weight_ref, bf16[128,1536]{1,0:T(8,128)(2,1)S(1)} %collective-permute-done.2.rows_ref), custom_call_target="tpu_custom_call" | custom-call | flops 1 | tf_op jit(solution)/shard_map/pairs/pallas_call | solution.py:225
  13.8 0.1 collective-permute-start.4
  13.9 0.0 collective-permute-done.lists_ref
  13.9 1.4 %collective-permute-done.3.refs_3_ = bf16[64,1536]{1,0:T(8,128)(2,1)S(1)} collective-permute-done((bf16[64,1536]{1,0:T(8,128)(2,1)S(1)}, bf16[64,1536]{1,0:T(8,128)(2,1)S(1)}, u32[]{:S(2)}, u32[]{:S(2)}) %collective-permute-start.3) | collective-permute-done | bytes 196640 | tf_op jit(solution)/shard_map/ppermute | solution.py:255
  15.3 1.4 %near_attention.1 = (bf16[128,768]{1,0:T(8,128)(2,1)S(1)}, f32[6,128]{1,0:T(8,128)S(1)}, f32[6,128]{1,0:T(8,128)S(1)}, f32[768,128]{1,0:T(8,128)S(1)}) custom-call(s32[2,6]{1,0:T(2,128)S(1)} %collective-permute-done.lists_ref, bf16[1536,768]{1,0:T(8,128)(2,1)S(1)} %get-tuple-element.22.q_weight_ref, bf16[128,1536]{1,0:T(8,128)(2,1)S(1)} %get-tuple-element.24.normed_ref, ...), custom_call_target="tpu_custom_call" | custom-call | flops 10000000000 | tf_op jit(solution)/shard_map/near_attention/pallas_call | solution.py:225
  16.7 0.0 collective-permute-done.4.refs_0_
  16.7 1.0 %finish.1 = bf16[128,1536]{1,0:T(8,128)(2,1)S(1)} custom-call(s32[2,6]{1,0:T(2,128)S(1)} %collective-permute-done.lists_ref, f32[3,1536]{1,0:T(4,128)S(1)} %get-tuple-element.19.modulate_ref, bf16[768,1536]{1,0:T(8,128)(2,1)S(1)} %get-tuple-element.21.out_weight_ref, bf16[128,1536]{1,0:T(8,128)(2,1)S(1)} %collective-permute-done.2.rows_ref, ...), custom_call_target="tpu_custom_call" | custom-call | flops 1 | tf_op jit(solution)/shard_map/finish/pallas_call | solution.py:225
  17.7 1.6 %collective-permute-start.5 = (bf16[1,1,1,2,64,1536]{5,4,3,2,1,0:T(8,128)(2,1)S(1)}, bf16[1,1,1,2,64,1536]{5,4,3,2,1,0:T(8,128)(2,1)S(1)}, u32[]{:S(2)}, u32[]{:S(2)}) collective-permute-start(bf16[1,1,1,2,64,1536]{5,4,3,2,1,0:T(8,128)(2,1)S(1)} %bitcast.10), channel_id=1, source_target_pairs={{0,10},{2,8},{4,14},{6,12},{8,18},{10,16},{12,22},{14,20},{16,26},... | collective-permute-start | bytes 1179656 | tf_op jit(solution)/shard_map/ppermute | solution.py:340
  19.3 11.3 %collective-permute-done.5 = bf16[1,1,1,2,64,1536]{5,4,3,2,1,0:T(8,128)(2,1)S(1)} collective-permute-done((bf16[1,1,1,2,64,1536]{5,4,3,2,1,0:T(8,128)(2,1)S(1)}, bf16[1,1,1,2,64,1536]{5,4,3,2,1,0:T(8,128)(2,1)S(1)}, u32[]{:S(2)}, u32[]{:S(2)}) %collective-permute-start.5) | collective-permute-done | bytes 393248 | tf_op jit(solution)/shard_map/ppermute | solution.py:340
  30.6 0.7 %copy.9 = bf16[1,1,1,2,64,1536]{5,4,3,2,1,0:T(8,128)(2,1)} copy(bf16[1,1,1,2,64,1536]{5,4,3,2,1,0:T(8,128)(2,1)S(1)} %collective-permute-done.5) | data formatting | bytes 786432
Async XLA Ops:
  0.0 12.8 %collective-permute-start.2 = (bf16[128,1536]{1,0:T(8,128)(2,1)}, bf16[128,1536]{1,0:T(8,128)(2,1)S(1)}, u32[]{:S(2)}, u32[]{:S(2)}) collective-permute-start(bf16[128,1536]{1,0:T(8,128)(2,1)} %bitcast.14), channel_id=1, source_target_pairs={{0,2},{2,0},{4,6},{6,4},{1,3},{3,1},{5,7},{7,5},{8,10},{10,8},{12,... | collective-permute-start | bytes 1179656 | tf_op jit(solution)/shard_map/ppermute | solution.py:252
  3.9 6.4 %collective-permute-start.1 = (bf16[64,1536]{1,0:T(8,128)(2,1)S(1)}, bf16[64,1536]{1,0:T(8,128)(2,1)S(1)}, u32[]{:S(2)}, u32[]{:S(2)}) collective-permute-start(bf16[64,1536]{1,0:T(8,128)(2,1)S(1)} %slice_bitcast_fusion), channel_id=1, source_target_pairs={{4,0},{6,2},{0,4},{2,6},{5,1},{7,3},{1,5},{3,7},{12,8},{14,10},{8,... | collective-permute-start | bytes 589832 | tf_op jit(solution)/shard_map/ppermute | solution.py:255
  6.2 3.6 %copy-start = (s32[1,1,2,6]{3,2,1,0:T(2,128)S(1)}, s32[1,1,2,6]{3,2,1,0:T(2,128)}, u32[]{:S(2)}) copy-start(s32[1,1,2,6]{3,2,1,0:T(2,128)} %param.11) | copy-start | bytes 148
  9.2 6.1 %collective-permute-start.3 = (bf16[64,1536]{1,0:T(8,128)(2,1)S(1)}, bf16[64,1536]{1,0:T(8,128)(2,1)S(1)}, u32[]{:S(2)}, u32[]{:S(2)}) collective-permute-start(bf16[64,1536]{1,0:T(8,128)(2,1)S(1)} %get-tuple-element.28), channel_id=1, source_target_pairs={{4,0},{6,2},{0,4},{2,6},{5,1},{7,3},{1,5},{3,7},{12,8},{14,10},{8,... | collective-permute-start | bytes 589832 | tf_op jit(solution)/shard_map/ppermute | solution.py:255
  9.7 4.1 %collective-permute-start = (s32[2,6]{1,0:T(2,128)S(1)}, s32[2,6]{1,0:T(2,128)S(1)}, u32[]{:S(2)}, u32[]{:S(2)}) collective-permute-start(s32[2,6]{1,0:T(2,128)S(1)} %bitcast.17), channel_id=1, source_target_pairs={{0,2},{2,0},{4,6},{6,4},{1,3},{3,1},{5,7},{7,5},{8,10},{10,8},{12,... | collective-permute-start | bytes 152 | tf_op jit(solution)/shard_map/ppermute | solution.py:252
  13.8 2.9 %collective-permute-start.4 = (bf16[128,1536]{1,0:T(8,128)(2,1)S(1)}, bf16[128,1536]{1,0:T(8,128)(2,1)S(1)}, u32[]{:S(2)}, u32[]{:S(2)}) collective-permute-start(bf16[128,1536]{1,0:T(8,128)(2,1)S(1)} %get-tuple-element.25.refs_0_), channel_id=1, source_target_pairs={{0,1},{1,0},{2,3},{3,2},{4,5},{5,4},{6,7},{7,6},{8,9},{9,8},{10,11... | collective-permute-start | bytes 1179656 | tf_op jit(solution)/shard_map/ppermute | solution.py:308
  17.7 12.9 %collective-permute-start.5 = (bf16[1,1,1,2,64,1536]{5,4,3,2,1,0:T(8,128)(2,1)S(1)}, bf16[1,1,1,2,64,1536]{5,4,3,2,1,0:T(8,128)(2,1)S(1)}, u32[]{:S(2)}, u32[]{:S(2)}) collective-permute-start(bf16[1,1,1,2,64,1536]{5,4,3,2,1,0:T(8,128)(2,1)S(1)} %bitcast.10), channel_id=1, source_target_pairs={{0,10},{2,8},{4,14},{6,12},{8,18},{10,16},{12,22},{14,20},{16,26},... | collective-permute-start | bytes 1179656 | tf_op jit(solution)/shard_map/ppermute | solution.py:340

commit v4 on v3

--- a/solution.py
+++ b/solution.py
@@ -12,6 +12,7 @@
 MASKED = -1e30
 RAW = 4
 LOADS = 4
+FIRST = 7
 F32 = jnp.float32
 BF16 = jnp.bfloat16
 VMEM = pl.BlockSpec(memory_space=pltpu.VMEM)
@@ -44,7 +45,7 @@
 
 def load_kernel(
     inner, domain_hbm, modulation_hbm, weight_hbm, own_hbm,
-    modulate_ref, weight_ref, kv_ref, *refs
+    modulate_ref, q_weight_ref, weight_ref, kv_ref, *refs
 ):
     *tail_ref, domain_ref, modulation_ref, own_ref, sems = refs
     first = [
@@ -61,7 +62,8 @@
         )
         for i in range(LOADS)
     ]
-    for load in first + loads:
+    query = pltpu.make_async_copy(weight_hbm.at[:, pl.ds(0, inner)], q_weight_ref, sems.at[3 + LOADS])
+    for load in first + loads + [query]:
         load.start()
     for load in first:
         load.wait()
@@ -74,21 +76,11 @@
         kv_ref[:, cols] = pairs
         for ref in tail_ref:
             ref[:, cols] = pairs[rows.shape[0] - ref.shape[0] :]
-
-
-def beyond_kernel(inner, n_rows, weight_hbm, out_weight_hbm, modulate_ref, pair_weight_ref, *refs):
-    rows_refs, (q_weight_ref, out_weight_ref) = refs[:n_rows], refs[n_rows : n_rows + 2]
-    *kv_refs, sems = refs[n_rows + 2 :]
-    loads = [
-        pltpu.make_async_copy(weight_hbm.at[:, pl.ds(0, inner)], q_weight_ref, sems.at[0]),
-        pltpu.make_async_copy(out_weight_hbm, out_weight_ref, sems.at[1]),
-    ]
-    for load in loads:
-        load.start()
-    for rows_ref, kv_ref in zip(rows_refs, kv_refs):
-        kv_ref[...] = projected(normalized((rows_ref,), modulate_ref), pair_weight_ref[...])
-    for load in loads:
-        load.wait()
+    query.wait()
+
+
+def beyond_kernel(modulate_ref, weight_ref, rows_ref, kv_ref):
+    kv_ref[...] = projected(normalized((rows_ref,), modulate_ref), weight_ref[...])
 
 
 def pair_kernel(modulate_ref, weight_ref, rows_ref, kv_ref, normed_ref):
@@ -110,15 +102,12 @@
     row = jnp.zeros((1, query_count), jnp.int32)
     for t in range(col_tiles):
         row = jnp.where(tile == t, bits[t : t + 1, :], row)
-    return jnp.concatenate(
-        [
-            jnp.broadcast_to(
-                jnp.where((row >> (first + p)) & 1 == 1, 0.0, MASKED), (tile_len, query_count)
-            )
-            for p in range(key_count // tile_len)
-        ],
-        axis=0,
-    )
+    parts, end = [], first + key_count
+    for p in range(first // tile_len, pl.cdiv(end, tile_len)):
+        size = min(end, (p + 1) * tile_len) - max(first, p * tile_len)
+        added = jnp.where((row >> p) & 1 == 1, 0.0, MASKED)
+        parts.append(jnp.broadcast_to(added, (size, query_count)))
+    return jnp.concatenate(parts, axis=0)
 
 
 def head_cols(h, offset=0):
@@ -159,7 +148,7 @@
     ]
 
 
-def near_kernel(n_kv, tile_len, slots_of, lists_ref, q_weight_ref, normed_ref, *refs):
+def near_kernel(n_kv, tile_len, slots_of, lists_ref, q_weight_ref, _, normed_ref, *refs):
     kv_refs = refs[:n_kv]
     q_ref, peak_ref, total_ref, mix_ref = refs[n_kv:]
     q_ref[...] = projected(normed_ref[...], q_weight_ref[...])
@@ -178,9 +167,10 @@
     n_kv, tile_len, slots_of, first,
     lists_ref, modulate_ref, out_weight_ref, rows_ref, q_ref, peak_ref, total_ref, mix_ref, *refs
 ):
-    kv_refs, (finished_ref, mixed_ref) = refs[:n_kv], refs[n_kv:]
+    kv_refs, (mixed_ref, finished_ref) = refs[:n_kv], refs[n_kv:]
     count = rows_ref.shape[0]
-    bias = masking(lists_ref, slots_of(), tile_len, first, n_kv * count, count)
+    key_count = sum(r.shape[0] for r in kv_refs)
+    bias = masking(lists_ref, slots_of(), tile_len, first, key_count, count)
     scores = scores_of(q_ref, kv_refs, bias)
     before = peak_ref[...]
     peaks = jnp.maximum(reduced(jnp.max, scores), before)
@@ -192,13 +182,20 @@
         mixed_ref[head_cols(h), :] = (
             mix_ref[head_cols(h), :] * kept[h : h + 1] + mix * share[h : h + 1]
         ).astype(BF16)
+    output_columns(0, mixed_ref, modulate_ref, out_weight_ref, rows_ref, finished_ref)
+
+
+def output_columns(first, mixed_ref, modulate_ref, out_weight_ref, rows_ref, finished_ref):
+    cols = slice(first, first + finished_ref.shape[1])
     branch = lax.dot_general(
         mixed_ref[...],
-        out_weight_ref[...],
+        out_weight_ref[:, cols],
         (((0,), (0,)), ((), ())),
         preferred_element_type=F32,
     )
-    finished_ref[...] = (rows_ref[...].astype(F32) + modulate_ref[2:3, :] * branch).astype(BF16)
+    finished_ref[...] = (
+        rows_ref[:, cols].astype(F32) + modulate_ref[2:3, cols] * branch
+    ).astype(BF16)
 
 
 def swap_perm(size):
@@ -260,30 +257,31 @@
     sent = own_count * RAW // 8
     beyond = [from_beyond(own[:sent])] if far else []
 
-    modulate, pair_weight, kv_own, *tail = call(
+    modulate, q_weight, pair_weight, kv_own, *tail = call(
         functools.partial(load_kernel, inner),
         [pl.BlockSpec(memory_space=pl.ANY)] + [HBM] * 3,
-        [held(3, width, F32), held(width, 2 * inner), held(own_count, 2 * inner)]
+        [held(3, width, F32), held(width, inner), held(width, 2 * inner), held(own_count, 2 * inner)]
         + [held(own_count - sent, 2 * inner)] * far,
         [domain_ids, *map(in_hbm, (modulation_table, weight, own))],
         [
             pltpu.SMEM(domain_ids.shape, jnp.int32),
             pltpu.VMEM(modulation_table.shape, BF16),
             pltpu.VMEM((own_count, width), BF16),
-            pltpu.SemaphoreType.DMA((3 + LOADS,)),
+            pltpu.SemaphoreType.DMA((4 + LOADS,)),
         ],
         "own_pairs",
     )
     kv_tail = [from_beyond(t) for t in tail]
-    q_weight, out_w, *kv_beyond = call(
-        functools.partial(beyond_kernel, inner, len(beyond)),
-        [HBM] * 2 + [VMEM] * (2 + len(beyond)),
-        [held(width, inner), held(inner, width)] + [held(sent, 2 * inner)] * far,
-        [in_hbm(weight), in_hbm(out_weight[0]), modulate, pair_weight, *beyond],
-        [pltpu.SemaphoreType.DMA((2,))],
-        "beyond_pairs",
-    )
-    kv_beyond += kv_tail
+    kv_beyond = [
+        call(
+            beyond_kernel,
+            [VMEM] * 3,
+            [held(sent, 2 * inner)],
+            [modulate, pair_weight, b],
+            name="beyond_pairs",
+        )[0]
+        for b in beyond
+    ]
     near_tiles = 2 + far
 
     def slots_of():
@@ -297,7 +295,7 @@
             near_tiles + odd_row,
         ]
 
-    tokens = after(tokens, q_weight)
+    tokens = after(tokens, kv_own, *kv_beyond)
     kv_tokens, normed = call(
         pair_kernel,
         [VMEM] * 3,
@@ -311,33 +309,42 @@
     near = [kv_tokens, kv_own, *kv_beyond]
     q, *partial = call(
         functools.partial(near_kernel, len(near), tile_len, slots_of),
-        [VMEM] * (3 + len(near)),
+        [VMEM] * (4 + len(near)),
         [
             held(own_count, inner),
             held(heads, own_count, F32),
             held(heads, own_count, F32),
             held(inner, own_count, F32),
         ],
-        [lists, q_weight, normed, *near],
+        [lists, q_weight, out_weight[0], normed, *near],
         name="near_attention",
         weight=10**10,
     )
-    (finished,) = call(
+    late = [*kv_tail, *kv_rows]
+    first_cols = width * FIRST // 12
+    mixed, *finished = call(
         functools.partial(
-            finish_kernel, len(kv_rows), tile_len, slots_of, near_tiles * col_tiles
+            finish_kernel, len(late), tile_len, slots_of, sum(x.shape[0] for x in near)
         ),
-        [VMEM] * (8 + len(kv_rows)),
-        [jax.ShapeDtypeStruct((own_count, width), BF16)],
-        [lists, modulate, out_w, tokens, q, *partial, *kv_rows],
-        [pltpu.VMEM((inner, own_count), BF16)],
-        "finish",
+        [VMEM] * (8 + len(late)),
+        [held(inner, own_count), held(own_count, first_cols)],
+        [lists, modulate, out_weight[0], tokens, q, *partial, *late],
+        name="finish",
+    )
+    finished += call(
+        functools.partial(output_columns, first_cols),
+        [VMEM] * 4,
+        [held(own_count, width - first_cols)],
+        [mixed, modulate, out_weight[0], tokens],
+        name="finish_rest",
     )
     onward = [
         (s * frames + f, (s + 1) % segments * frames + (f ^ 1))
         for s in range(segments)
         for f in range(frames)
     ]
-    return lax.ppermute(finished.reshape(clip_tokens.shape), ("segment", "frame"), onward)
+    handed = [lax.ppermute(x, ("segment", "frame"), onward) for x in finished]
+    return jnp.concatenate(handed, axis=1).reshape(clip_tokens.shape)
 
 
 def solution(mesh):

time: 31.5 us -> 31.3 us (level)
  starting transfers between devices: 6.88 us -> 9.43 us
  waiting for transfers between devices: 13.2 us -> 11 us
  other arithmetic: 0 us -> 0.78 us
  local copies, waits for them, and re-layouts: 1.73 us -> 0.98 us
  Pallas kernels: 8.79 us -> 8.24 us
    ppermute x1 -> x2, starting transfers between devices: 1.6 us -> 4.15 us  [body(): handed = [lax.ppermute(x, ('segment', 'frame'), onward) for x in finished]]
    ppermute x1 -> x2, waiting for transfers between devices: 11.3 us -> 8.87 us  [body(): handed = [lax.ppermute(x, ('segment', 'frame'), onward) for x in finished]]
    ppermute x2, waiting for transfers between devices: 0.01 us -> 0.8 us  [from_partner(): return lax.ppermute(x, 'frame', swap_perm(frames))]
    concatenate x0 -> x1, other arithmetic: none -> 0.78 us  [body(): return jnp.concatenate(handed, axis=1).reshape(clip_tokens.shape)]
    unnamed x3 -> x2, local copies, waits for them, and re-layouts: 0.75 us -> 0.01 us
    ppermute x2, waiting for transfers between devices: 1.92 us -> 1.33 us  [from_beyond(): return lax.ppermute(x, 'frame', beyond_perm(frames))]
    pallas_call x5 -> x6, Pallas kernels: 8.79 us -> 8.24 us  [call(): pl.pallas_call(kernel, out_shape=outs, in_specs=ins, out_specs=[VMEM] * l...]
    ppermute x2, starting transfers between devices: 2.16 us -> 1.73 us  [from_beyond(): return lax.ppermute(x, 'frame', beyond_perm(frames))]
  transfers between devices with their start and end apart: 6 -> 7, of which waited for: 3 -> 4; matrix products, arithmetic and copies ran while one was open for 3% -> 3% of each run, Pallas kernels for 25% -> 23%
where the time goes in v4:
time: 31.3 us; the launch traced here: 31.2 us
  waiting for transfers between devices  11 us (35%)
  starting transfers between devices  9.43 us (30%)
  Pallas kernels  8.24 us (26%)
  local copies, waits for them, and re-layouts  0.98 us (3%)
  other arithmetic  0.78 us (2%)
  between operations  0.73 us (2%)
    ppermute x2, waiting for transfers between devices, body(): handed = [lax.ppermute(x, ('segment', 'frame'), onward) for x in finished]  8.87 us
    pallas_call x6, Pallas kernels, call(): pl.pallas_call(kernel, out_shape=outs, in_specs=ins, out_specs=[VMEM] * l...  8.24 us
    ppermute x2, starting transfers between devices, body(): handed = [lax.ppermute(x, ('segment', 'frame'), onward) for x in finished]  4.15 us
    ppermute x2, starting transfers between devices, from_partner(): return lax.ppermute(x, 'frame', swap_perm(frames))  3.47 us
    ppermute x2, starting transfers between devices, from_beyond(): return lax.ppermute(x, 'frame', beyond_perm(frames))  1.73 us
    ppermute x2, waiting for transfers between devices, from_beyond(): return lax.ppermute(x, 'frame', beyond_perm(frames))  1.33 us
    slice x1, local copies, waits for them, and re-layouts, body(): beyond = [from_beyond(own[:sent])] if far else []  0.97 us
    ppermute x2, waiting for transfers between devices, from_partner(): return lax.ppermute(x, 'frame', swap_perm(frames))  0.8 us
  transfers between devices with their start and end apart: 7, of which 4 were waited for; matrix products, arithmetic and copies ran while one was open for 3% of the time, Pallas kernels for 23%

profile of v4, /device:TPU:0, one launch (start us, length us, event | category | flops | bytes accessed | tf_op | source)
XLA Modules:
  0.0 31.2 jit_solution(14251559636894031028)
XLA Ops:
  0.0 2.9 %collective-permute-start.1 = (bf16[128,1536]{1,0:T(8,128)(2,1)}, bf16[128,1536]{1,0:T(8,128)(2,1)S(1)}, u32[]{:S(2)}, u32[]{:S(2)}) collective-permute-start(bf16[128,1536]{1,0:T(8,128)(2,1)} %bitcast.14), channel_id=1, source_target_pairs={{0,2},{2,0},{4,6},{6,4},{1,3},{3,1},{5,7},{7,5},{8,10},{10,8},{12,... | collective-permute-start | bytes 1179656 | tf_op jit(solution)/shard_map/ppermute | solution.py:249
  2.9 1.0 %slice_bitcast_fusion = bf16[64,1536]{1,0:T(8,128)(2,1)S(1)} fusion(bf16[1,1,1,2,64,1536]{5,4,3,2,1,0:T(8,128)(2,1)} %param.6), kind=kLoop, calls=%fused_computation.1 | loop fusion | bytes 393216 | tf_op jit(solution)/shard_map/slice | solution.py:258
  3.9 1.6 %collective-permute-start.2 = (bf16[64,1536]{1,0:T(8,128)(2,1)S(1)}, bf16[64,1536]{1,0:T(8,128)(2,1)S(1)}, u32[]{:S(2)}, u32[]{:S(2)}) collective-permute-start(bf16[64,1536]{1,0:T(8,128)(2,1)S(1)} %slice_bitcast_fusion), channel_id=1, source_target_pairs={{4,0},{6,2},{0,4},{2,6},{5,1},{7,3},{1,5},{3,7},{12,8},{14,10},{8,... | collective-permute-start | bytes 589832 | tf_op jit(solution)/shard_map/ppermute | solution.py:252
  5.5 0.5 %collective-permute-start = (s32[2,6]{1,0:T(2,128)}, s32[2,6]{1,0:T(2,128)S(1)}, u32[]{:S(2)}, u32[]{:S(2)}) collective-permute-start(s32[2,6]{1,0:T(2,128)} %bitcast.17), channel_id=1, source_target_pairs={{0,2},{2,0},{4,6},{6,4},{1,3},{3,1},{5,7},{7,5},{8,10},{10,8},{12,... | collective-permute-start | bytes 152 | tf_op jit(solution)/shard_map/ppermute | solution.py:249
  6.7 3.4 %own_pairs.1 = (f32[3,1536]{1,0:T(4,128)S(1)}, bf16[1536,768]{1,0:T(8,128)(2,1)S(1)}, bf16[1536,1536]{1,0:T(8,128)(2,1)S(1)}, bf16[128,1536]{1,0:T(8,128)(2,1)S(1)}, bf16[64,1536]{1,0:T(8,128)(2,1)S(1)}) custom-call(s32[1]{0:T(128)S(6)} %copy.7.domain_hbm, bf16[3,8,1536]{2,1,0:T(8,128)(2,1)} %bitcast.16, bf16[1536,2304]{1,0:T(8,128)(2,1)} %bitcast.13, ...), custom_call_target="tpu_custom_call" | custom-call | flops 1 | tf_op jit(solution)/shard_map/own_pairs/pallas_call | solution.py:222
  10.1 0.1 collective-permute-start.3
  10.2 0.1 collective-permute-done.2.rows_ref
  10.3 0.0 copy-start
  10.3 1.1 %beyond_pairs.1.refs_2_ = bf16[64,1536]{1,0:T(8,128)(2,1)S(1)} custom-call(f32[3,1536]{1,0:T(4,128)S(1)} %get-tuple-element.19.modulate_ref, bf16[1536,1536]{1,0:T(8,128)(2,1)S(1)} %get-tuple-element.21.weight_ref, bf16[64,1536]{1,0:T(8,128)(2,1)S(1)} %collective-permute-done.2.rows_ref), custom_call_target="tpu_custom_call" | custom-call | flops 1 | tf_op jit(solution)/shard_map/beyond_pairs/pallas_call | solution.py:222
  11.5 0.8 %collective-permute-done.1.rows_ref = bf16[128,1536]{1,0:T(8,128)(2,1)S(1)} collective-permute-done((bf16[128,1536]{1,0:T(8,128)(2,1)}, bf16[128,1536]{1,0:T(8,128)(2,1)S(1)}, u32[]{:S(2)}, u32[]{:S(2)}) %collective-permute-start.1) | collective-permute-done | bytes 393248 | tf_op jit(solution)/shard_map/ppermute | solution.py:249
  12.3 1.0 %pairs.1 = (bf16[128,1536]{1,0:T(8,128)(2,1)S(1)}, bf16[128,1536]{1,0:T(8,128)(2,1)S(1)}) custom-call(f32[3,1536]{1,0:T(4,128)S(1)} %get-tuple-element.19.modulate_ref, bf16[1536,1536]{1,0:T(8,128)(2,1)S(1)} %get-tuple-element.21.weight_ref, bf16[128,1536]{1,0:T(8,128)(2,1)S(1)} %collective-permute-done.1.rows_ref), custom_call_target="tpu_custom_call" | custom-call | flops 1 | tf_op jit(solution)/shard_map/pairs/pallas_call | solution.py:222
  13.3 0.1 collective-permute-start.4
  13.4 0.0 collective-permute-done.lists_ref
  13.4 0.0 copy-done
  13.4 1.3 %near_attention.1 = (bf16[128,768]{1,0:T(8,128)(2,1)S(1)}, f32[6,128]{1,0:T(8,128)S(1)}, f32[6,128]{1,0:T(8,128)S(1)}, f32[768,128]{1,0:T(8,128)S(1)}) custom-call(s32[2,6]{1,0:T(2,128)S(1)} %collective-permute-done.lists_ref, bf16[1536,768]{1,0:T(8,128)(2,1)S(1)} %get-tuple-element.23.q_weight_ref, bf16[768,1536]{1,0:T(8,128)(2,1)S(1)} %bitcast.10, ...), custom_call_target="tpu_custom_call" | custom-call | flops 10000000000 | tf_op jit(solution)/shard_map/near_attention/pallas_call | solution.py:222
  14.7 1.2 %collective-permute-done.3.refs_0_ = bf16[64,1536]{1,0:T(8,128)(2,1)S(1)} collective-permute-done((bf16[64,1536]{1,0:T(8,128)(2,1)S(1)}, bf16[64,1536]{1,0:T(8,128)(2,1)S(1)}, u32[]{:S(2)}, u32[]{:S(2)}) %collective-permute-start.3) | collective-permute-done | bytes 196640 | tf_op jit(solution)/shard_map/ppermute | solution.py:252
  15.9 0.0 collective-permute-done.4.refs_1_
  16.0 1.0 %finish.1 = (bf16[768,128]{1,0:T(8,128)(2,1)S(1)}, bf16[128,896]{1,0:T(8,128)(2,1)S(1)}) custom-call(s32[2,6]{1,0:T(2,128)S(1)} %collective-permute-done.lists_ref, f32[3,1536]{1,0:T(4,128)S(1)} %get-tuple-element.19.modulate_ref, bf16[768,1536]{1,0:T(8,128)(2,1)S(1)} %bitcast.11, bf16[128,1536]{1,0:T(8,128)(2,1)S(1)} %collective-permute-done.1.rows_ref, ...), custom_call_target="tpu_custom_call" | custom-call | flops 1 | tf_op jit(solution)/shard_map/finish/pallas_call | solution.py:222
  17.0 2.6 %collective-permute-start.5 = (bf16[128,896]{1,0:T(8,128)(2,1)S(1)}, bf16[128,896]{1,0:T(8,128)(2,1)S(1)}, u32[]{:S(2)}, u32[]{:S(2)}) collective-permute-start(bf16[128,896]{1,0:T(8,128)(2,1)S(1)} %get-tuple-element.31), channel_id=1, source_target_pairs={{0,10},{2,8},{4,14},{6,12},{8,18},{10,16},{12,22},{14,20},{16,26},... | collective-permute-start | bytes 688136 | tf_op jit(solution)/shard_map/ppermute | solution.py:346
  19.5 0.4 %finish_rest.1 = bf16[128,640]{1,0:T(8,128)(2,1)S(1)} custom-call(bf16[768,128]{1,0:T(8,128)(2,1)S(1)} %get-tuple-element.32.mixed_ref, f32[3,1536]{1,0:T(4,128)S(1)} %get-tuple-element.19.modulate_ref, bf16[768,1536]{1,0:T(8,128)(2,1)S(1)} %bitcast.12, bf16[128,1536]{1,0:T(8,128)(2,1)S(1)} %collective-permute-done.1.rows_ref), custom_call_target="tpu_custom_call" | custom-call | flops 1 | tf_op jit(solution)/shard_map/finish_rest/pallas_call | solution.py:222
  19.9 1.6 %collective-permute-start.6 = (bf16[128,640]{1,0:T(8,128)(2,1)S(1)}, bf16[128,640]{1,0:T(8,128)(2,1)S(1)}, u32[]{:S(2)}, u32[]{:S(2)}) collective-permute-start(bf16[128,640]{1,0:T(8,128)(2,1)S(1)} %finish_rest.1), channel_id=1, source_target_pairs={{0,10},{2,8},{4,14},{6,12},{8,18},{10,16},{12,22},{14,20},{16,26},... | collective-permute-start | bytes 491528 | tf_op jit(solution)/shard_map/ppermute | solution.py:346
  21.5 8.9 %collective-permute-done.6 = bf16[128,640]{1,0:T(8,128)(2,1)S(1)} collective-permute-done((bf16[128,640]{1,0:T(8,128)(2,1)S(1)}, bf16[128,640]{1,0:T(8,128)(2,1)S(1)}, u32[]{:S(2)}, u32[]{:S(2)}) %collective-permute-start.6) | collective-permute-done | bytes 163872 | tf_op jit(solution)/shard_map/ppermute | solution.py:346
  30.4 0.0 collective-permute-done.5
  30.4 0.8 %pad_maximum_fusion = bf16[128,1536]{1,0:T(8,128)(2,1)} fusion(bf16[128,640]{1,0:T(8,128)(2,1)S(1)} %collective-permute-done.6, bf16[128,896]{1,0:T(8,128)(2,1)S(1)} %collective-permute-done.5), kind=kLoop, calls=%fused_computation | loop fusion | flops 786432 | bytes 786432 | tf_op jit(solution)/shard_map/concatenate | solution.py:347
Async XLA Ops:
  0.0 12.3 %collective-permute-start.1 = (bf16[128,1536]{1,0:T(8,128)(2,1)}, bf16[128,1536]{1,0:T(8,128)(2,1)S(1)}, u32[]{:S(2)}, u32[]{:S(2)}) collective-permute-start(bf16[128,1536]{1,0:T(8,128)(2,1)} %bitcast.14), channel_id=1, source_target_pairs={{0,2},{2,0},{4,6},{6,4},{1,3},{3,1},{5,7},{7,5},{8,10},{10,8},{12,... | collective-permute-start | bytes 1179656 | tf_op jit(solution)/shard_map/ppermute | solution.py:249
  3.9 6.4 %collective-permute-start.2 = (bf16[64,1536]{1,0:T(8,128)(2,1)S(1)}, bf16[64,1536]{1,0:T(8,128)(2,1)S(1)}, u32[]{:S(2)}, u32[]{:S(2)}) collective-permute-start(bf16[64,1536]{1,0:T(8,128)(2,1)S(1)} %slice_bitcast_fusion), channel_id=1, source_target_pairs={{4,0},{6,2},{0,4},{2,6},{5,1},{7,3},{1,5},{3,7},{12,8},{14,10},{8,... | collective-permute-start | bytes 589832 | tf_op jit(solution)/shard_map/ppermute | solution.py:252
  5.5 7.9 %collective-permute-start = (s32[2,6]{1,0:T(2,128)}, s32[2,6]{1,0:T(2,128)S(1)}, u32[]{:S(2)}, u32[]{:S(2)}) collective-permute-start(s32[2,6]{1,0:T(2,128)} %bitcast.17), channel_id=1, source_target_pairs={{0,2},{2,0},{4,6},{6,4},{1,3},{3,1},{5,7},{7,5},{8,10},{10,8},{12,... | collective-permute-start | bytes 152 | tf_op jit(solution)/shard_map/ppermute | solution.py:249
  10.1 5.9 %collective-permute-start.3 = (bf16[64,1536]{1,0:T(8,128)(2,1)S(1)}, bf16[64,1536]{1,0:T(8,128)(2,1)S(1)}, u32[]{:S(2)}, u32[]{:S(2)}) collective-permute-start(bf16[64,1536]{1,0:T(8,128)(2,1)S(1)} %get-tuple-element.30), channel_id=1, source_target_pairs={{4,0},{6,2},{0,4},{2,6},{5,1},{7,3},{1,5},{3,7},{12,8},{14,10},{8,... | collective-permute-start | bytes 589832 | tf_op jit(solution)/shard_map/ppermute | solution.py:252
  10.3 3.0 %copy-start = (bf16[1,768,1536]{2,1,0:T(8,128)(2,1)S(1)}, bf16[1,768,1536]{2,1,0:T(8,128)(2,1)}, u32[]{:S(2)}) copy-start(bf16[1,768,1536]{2,1,0:T(8,128)(2,1)} %param.8) | copy-start | bytes 7077892
  13.3 2.7 %collective-permute-start.4 = (bf16[128,1536]{1,0:T(8,128)(2,1)S(1)}, bf16[128,1536]{1,0:T(8,128)(2,1)S(1)}, u32[]{:S(2)}, u32[]{:S(2)}) collective-permute-start(bf16[128,1536]{1,0:T(8,128)(2,1)S(1)} %get-tuple-element.25.refs_0_), channel_id=1, source_target_pairs={{0,1},{1,0},{2,3},{3,2},{4,5},{5,4},{6,7},{7,6},{8,9},{9,8},{10,11... | collective-permute-start | bytes 1179656 | tf_op jit(solution)/shard_map/ppermute | solution.py:306
  17.0 13.4 %collective-permute-start.5 = (bf16[128,896]{1,0:T(8,128)(2,1)S(1)}, bf16[128,896]{1,0:T(8,128)(2,1)S(1)}, u32[]{:S(2)}, u32[]{:S(2)}) collective-permute-start(bf16[128,896]{1,0:T(8,128)(2,1)S(1)} %get-tuple-element.31), channel_id=1, source_target_pairs={{0,10},{2,8},{4,14},{6,12},{8,18},{10,16},{12,22},{14,20},{16,26},... | collective-permute-start | bytes 688136 | tf_op jit(solution)/shard_map/ppermute | solution.py:346
  19.9 10.5 %collective-permute-start.6 = (bf16[128,640]{1,0:T(8,128)(2,1)S(1)}, bf16[128,640]{1,0:T(8,128)(2,1)S(1)}, u32[]{:S(2)}, u32[]{:S(2)}) collective-permute-start(bf16[128,640]{1,0:T(8,128)(2,1)S(1)} %finish_rest.1), channel_id=1, source_target_pairs={{0,10},{2,8},{4,14},{6,12},{8,18},{10,16},{12,22},{14,20},{16,26},... | collective-permute-start | bytes 491528 | tf_op jit(solution)/shard_map/ppermute | solution.py:346

commit v5 on v4

--- a/solution.py
+++ b/solution.py
@@ -10,7 +10,7 @@
 HD = 128
 EPSILON = 1e-06
 MASKED = -1e30
-RAW = 4
+RAW = 5
 LOADS = 4
 FIRST = 7
 F32 = jnp.float32
@@ -306,7 +306,7 @@
     kv_rows = [lax.ppermute(kv_tokens, "row", swap_perm(rows))]
     if rows > 2:
         kv_rows.append(lax.ppermute(kv_rows[0], "row", relay_perm(rows)))
-    near = [kv_tokens, kv_own, *kv_beyond]
+    near = [kv_tokens, kv_own]
     q, *partial = call(
         functools.partial(near_kernel, len(near), tile_len, slots_of),
         [VMEM] * (4 + len(near)),
@@ -320,7 +320,7 @@
         name="near_attention",
         weight=10**10,
     )
-    late = [*kv_tail, *kv_rows]
+    late = [*kv_beyond, *kv_tail, *kv_rows]
     first_cols = width * FIRST // 12
     mixed, *finished = call(
         functools.partial(

time: 31.3 us -> 31.3 us (level)
    ppermute x2, waiting for transfers between devices: 0.8 us -> 0.01 us  [from_partner(): return lax.ppermute(x, 'frame', swap_perm(frames))]
    ppermute x2, waiting for transfers between devices: 8.87 us -> 9.44 us  [body(): handed = [lax.ppermute(x, ('segment', 'frame'), onward) for x in finished]]
where the time goes in v5:
time: 31.3 us; the launch traced here: 31.2 us
  waiting for transfers between devices  11.1 us (35%)
  starting transfers between devices  9.41 us (30%)
  Pallas kernels  8.19 us (26%)
  local copies, waits for them, and re-layouts  1 us (3%)
  other arithmetic  0.78 us (2%)
  between operations  0.73 us (2%)
    ppermute x2, waiting for transfers between devices, body(): handed = [lax.ppermute(x, ('segment', 'frame'), onward) for x in finished]  9.44 us
    pallas_call x6, Pallas kernels, call(): pl.pallas_call(kernel, out_shape=outs, in_specs=ins, out_specs=[VMEM] * l...  8.19 us
    ppermute x2, starting transfers between devices, body(): handed = [lax.ppermute(x, ('segment', 'frame'), onward) for x in finished]  4.14 us
    ppermute x2, starting transfers between devices, from_partner(): return lax.ppermute(x, 'frame', swap_perm(frames))  3.47 us
    ppermute x2, starting transfers between devices, from_beyond(): return lax.ppermute(x, 'frame', beyond_perm(frames))  1.73 us
    ppermute x2, waiting for transfers between devices, from_beyond(): return lax.ppermute(x, 'frame', beyond_perm(frames))  1.56 us
    slice x1, local copies, waits for them, and re-layouts, body(): beyond = [from_beyond(own[:sent])] if far else []  0.99 us
    concatenate x1, other arithmetic, body(): return jnp.concatenate(handed, axis=1).reshape(clip_tokens.shape)  0.78 us
  transfers between devices with their start and end apart: 7, of which 4 were waited for; matrix products, arithmetic and copies ran while one was open for 3% of the time, Pallas kernels for 23%

profile of v5, /device:TPU:0, one launch (start us, length us, event | category | flops | bytes accessed | tf_op | source)
XLA Modules:
  0.0 31.2 jit_solution(18243539239138561790)
XLA Ops:
  0.0 2.9 %collective-permute-start.1 = (bf16[128,1536]{1,0:T(8,128)(2,1)}, bf16[128,1536]{1,0:T(8,128)(2,1)S(1)}, u32[]{:S(2)}, u32[]{:S(2)}) collective-permute-start(bf16[128,1536]{1,0:T(8,128)(2,1)} %bitcast.12), channel_id=1, source_target_pairs={{0,2},{2,0},{4,6},{6,4},{1,3},{3,1},{5,7},{7,5},{8,10},{10,8},{12,... | collective-permute-start | bytes 1179656 | tf_op jit(solution)/shard_map/ppermute | solution.py:249
  2.9 1.0 %slice.4 = bf16[80,1536]{1,0:T(8,128)(2,1)S(1)} slice(bf16[128,1536]{1,0:T(8,128)(2,1)} %bitcast.13), slice={[0:80], [0:1536]} | slice | bytes 491520 | tf_op jit(solution)/shard_map/slice | solution.py:258
  3.9 1.6 %collective-permute-start.2 = (bf16[80,1536]{1,0:T(8,128)(2,1)S(1)}, bf16[80,1536]{1,0:T(8,128)(2,1)S(1)}, u32[]{:S(2)}, u32[]{:S(2)}) collective-permute-start(bf16[80,1536]{1,0:T(8,128)(2,1)S(1)} %slice.4), channel_id=1, source_target_pairs={{4,0},{6,2},{0,4},{2,6},{5,1},{7,3},{1,5},{3,7},{12,8},{14,10},{8,... | collective-permute-start | bytes 737288 | tf_op jit(solution)/shard_map/ppermute | solution.py:252
  5.5 0.5 %collective-permute-start = (s32[2,6]{1,0:T(2,128)}, s32[2,6]{1,0:T(2,128)S(1)}, u32[]{:S(2)}, u32[]{:S(2)}) collective-permute-start(s32[2,6]{1,0:T(2,128)} %bitcast.16), channel_id=1, source_target_pairs={{0,2},{2,0},{4,6},{6,4},{1,3},{3,1},{5,7},{7,5},{8,10},{10,8},{12,... | collective-permute-start | bytes 152 | tf_op jit(solution)/shard_map/ppermute | solution.py:249
  6.7 3.4 %own_pairs.1 = (f32[3,1536]{1,0:T(4,128)S(1)}, bf16[1536,768]{1,0:T(8,128)(2,1)S(1)}, bf16[1536,1536]{1,0:T(8,128)(2,1)S(1)}, bf16[128,1536]{1,0:T(8,128)(2,1)S(1)}, bf16[48,1536]{1,0:T(8,128)(2,1)S(1)}) custom-call(s32[1]{0:T(128)S(6)} %copy.7.domain_hbm, bf16[3,8,1536]{2,1,0:T(8,128)(2,1)} %bitcast.15, bf16[1536,2304]{1,0:T(8,128)(2,1)} %bitcast.11, ...), custom_call_target="tpu_custom_call" | custom-call | flops 1 | tf_op jit(solution)/shard_map/own_pairs/pallas_call | solution.py:222
  10.1 0.1 collective-permute-start.3
  10.2 1.2 %collective-permute-done.2.rows_ref = bf16[80,1536]{1,0:T(8,128)(2,1)S(1)} collective-permute-done((bf16[80,1536]{1,0:T(8,128)(2,1)S(1)}, bf16[80,1536]{1,0:T(8,128)(2,1)S(1)}, u32[]{:S(2)}, u32[]{:S(2)}) %collective-permute-start.2) | collective-permute-done | bytes 245792 | tf_op jit(solution)/shard_map/ppermute | solution.py:252
  11.4 0.0 copy-start
  11.4 1.1 %beyond_pairs.1.refs_0_ = bf16[80,1536]{1,0:T(8,128)(2,1)S(1)} custom-call(f32[3,1536]{1,0:T(4,128)S(1)} %get-tuple-element.19.modulate_ref, bf16[1536,1536]{1,0:T(8,128)(2,1)S(1)} %get-tuple-element.21.weight_ref, bf16[80,1536]{1,0:T(8,128)(2,1)S(1)} %collective-permute-done.2.rows_ref), custom_call_target="tpu_custom_call" | custom-call | flops 1 | tf_op jit(solution)/shard_map/beyond_pairs/pallas_call | solution.py:222
  12.6 0.0 collective-permute-done.1.rows_ref
  12.6 1.0 %pairs.1 = (bf16[128,1536]{1,0:T(8,128)(2,1)S(1)}, bf16[128,1536]{1,0:T(8,128)(2,1)S(1)}) custom-call(f32[3,1536]{1,0:T(4,128)S(1)} %get-tuple-element.19.modulate_ref, bf16[1536,1536]{1,0:T(8,128)(2,1)S(1)} %get-tuple-element.21.weight_ref, bf16[128,1536]{1,0:T(8,128)(2,1)S(1)} %collective-permute-done.1.rows_ref), custom_call_target="tpu_custom_call" | custom-call | flops 1 | tf_op jit(solution)/shard_map/pairs/pallas_call | solution.py:222
  13.6 0.1 collective-permute-start.4
  13.7 0.0 collective-permute-done.lists_ref
  13.7 0.0 copy-done
  13.7 1.2 %near_attention.1 = (bf16[128,768]{1,0:T(8,128)(2,1)S(1)}, f32[6,128]{1,0:T(8,128)S(1)}, f32[6,128]{1,0:T(8,128)S(1)}, f32[768,128]{1,0:T(8,128)S(1)}) custom-call(s32[2,6]{1,0:T(2,128)S(1)} %collective-permute-done.lists_ref, bf16[1536,768]{1,0:T(8,128)(2,1)S(1)} %get-tuple-element.23.q_weight_ref, bf16[768,1536]{1,0:T(8,128)(2,1)S(1)} %bitcast.8, ...), custom_call_target="tpu_custom_call" | custom-call | flops 10000000000 | tf_op jit(solution)/shard_map/near_attention/pallas_call | solution.py:222
  14.9 0.4 %collective-permute-done.3.refs_1_ = bf16[48,1536]{1,0:T(8,128)(2,1)S(1)} collective-permute-done((bf16[48,1536]{1,0:T(8,128)(2,1)S(1)}, bf16[48,1536]{1,0:T(8,128)(2,1)S(1)}, u32[]{:S(2)}, u32[]{:S(2)}) %collective-permute-start.3) | collective-permute-done | bytes 147488 | tf_op jit(solution)/shard_map/ppermute | solution.py:252
  15.3 0.1 collective-permute-done.4.refs_2_
  15.4 1.1 %finish.1 = (bf16[768,128]{1,0:T(8,128)(2,1)S(1)}, bf16[128,896]{1,0:T(8,128)(2,1)S(1)}) custom-call(s32[2,6]{1,0:T(2,128)S(1)} %collective-permute-done.lists_ref, f32[3,1536]{1,0:T(4,128)S(1)} %get-tuple-element.19.modulate_ref, bf16[768,1536]{1,0:T(8,128)(2,1)S(1)} %bitcast.9, bf16[128,1536]{1,0:T(8,128)(2,1)S(1)} %collective-permute-done.1.rows_ref, ...), custom_call_target="tpu_custom_call" | custom-call | flops 1 | tf_op jit(solution)/shard_map/finish/pallas_call | solution.py:222
  16.5 2.5 %collective-permute-start.5 = (bf16[128,896]{1,0:T(8,128)(2,1)S(1)}, bf16[128,896]{1,0:T(8,128)(2,1)S(1)}, u32[]{:S(2)}, u32[]{:S(2)}) collective-permute-start(bf16[128,896]{1,0:T(8,128)(2,1)S(1)} %get-tuple-element.31), channel_id=1, source_target_pairs={{0,10},{2,8},{4,14},{6,12},{8,18},{10,16},{12,22},{14,20},{16,26},... | collective-permute-start | bytes 688136 | tf_op jit(solution)/shard_map/ppermute | solution.py:346
  19.0 0.4 %finish_rest.1 = bf16[128,640]{1,0:T(8,128)(2,1)S(1)} custom-call(bf16[768,128]{1,0:T(8,128)(2,1)S(1)} %get-tuple-element.32.mixed_ref, f32[3,1536]{1,0:T(4,128)S(1)} %get-tuple-element.19.modulate_ref, bf16[768,1536]{1,0:T(8,128)(2,1)S(1)} %bitcast.10, bf16[128,1536]{1,0:T(8,128)(2,1)S(1)} %collective-permute-done.1.rows_ref), custom_call_target="tpu_custom_call" | custom-call | flops 1 | tf_op jit(solution)/shard_map/finish_rest/pallas_call | solution.py:222
  19.3 1.6 %collective-permute-start.6 = (bf16[128,640]{1,0:T(8,128)(2,1)S(1)}, bf16[128,640]{1,0:T(8,128)(2,1)S(1)}, u32[]{:S(2)}, u32[]{:S(2)}) collective-permute-start(bf16[128,640]{1,0:T(8,128)(2,1)S(1)} %finish_rest.1), channel_id=1, source_target_pairs={{0,10},{2,8},{4,14},{6,12},{8,18},{10,16},{12,22},{14,20},{16,26},... | collective-permute-start | bytes 491528 | tf_op jit(solution)/shard_map/ppermute | solution.py:346
  21.0 9.4 %collective-permute-done.6 = bf16[128,640]{1,0:T(8,128)(2,1)S(1)} collective-permute-done((bf16[128,640]{1,0:T(8,128)(2,1)S(1)}, bf16[128,640]{1,0:T(8,128)(2,1)S(1)}, u32[]{:S(2)}, u32[]{:S(2)}) %collective-permute-start.6) | collective-permute-done | bytes 163872 | tf_op jit(solution)/shard_map/ppermute | solution.py:346
  30.4 0.0 collective-permute-done.5
  30.4 0.8 %pad_maximum_fusion = bf16[128,1536]{1,0:T(8,128)(2,1)} fusion(bf16[128,640]{1,0:T(8,128)(2,1)S(1)} %collective-permute-done.6, bf16[128,896]{1,0:T(8,128)(2,1)S(1)} %collective-permute-done.5), kind=kLoop, calls=%fused_computation | loop fusion | flops 786432 | bytes 786432 | tf_op jit(solution)/shard_map/concatenate | solution.py:347
Async XLA Ops:
  0.0 12.6 %collective-permute-start.1 = (bf16[128,1536]{1,0:T(8,128)(2,1)}, bf16[128,1536]{1,0:T(8,128)(2,1)S(1)}, u32[]{:S(2)}, u32[]{:S(2)}) collective-permute-start(bf16[128,1536]{1,0:T(8,128)(2,1)} %bitcast.12), channel_id=1, source_target_pairs={{0,2},{2,0},{4,6},{6,4},{1,3},{3,1},{5,7},{7,5},{8,10},{10,8},{12,... | collective-permute-start | bytes 1179656 | tf_op jit(solution)/shard_map/ppermute | solution.py:249
  3.9 7.5 %collective-permute-start.2 = (bf16[80,1536]{1,0:T(8,128)(2,1)S(1)}, bf16[80,1536]{1,0:T(8,128)(2,1)S(1)}, u32[]{:S(2)}, u32[]{:S(2)}) collective-permute-start(bf16[80,1536]{1,0:T(8,128)(2,1)S(1)} %slice.4), channel_id=1, source_target_pairs={{4,0},{6,2},{0,4},{2,6},{5,1},{7,3},{1,5},{3,7},{12,8},{14,10},{8,... | collective-permute-start | bytes 737288 | tf_op jit(solution)/shard_map/ppermute | solution.py:252
  5.5 8.2 %collective-permute-start = (s32[2,6]{1,0:T(2,128)}, s32[2,6]{1,0:T(2,128)S(1)}, u32[]{:S(2)}, u32[]{:S(2)}) collective-permute-start(s32[2,6]{1,0:T(2,128)} %bitcast.16), channel_id=1, source_target_pairs={{0,2},{2,0},{4,6},{6,4},{1,3},{3,1},{5,7},{7,5},{8,10},{10,8},{12,... | collective-permute-start | bytes 152 | tf_op jit(solution)/shard_map/ppermute | solution.py:249
  10.1 5.2 %collective-permute-start.3 = (bf16[48,1536]{1,0:T(8,128)(2,1)S(1)}, bf16[48,1536]{1,0:T(8,128)(2,1)S(1)}, u32[]{:S(2)}, u32[]{:S(2)}) collective-permute-start(bf16[48,1536]{1,0:T(8,128)(2,1)S(1)} %get-tuple-element.30), channel_id=1, source_target_pairs={{4,0},{6,2},{0,4},{2,6},{5,1},{7,3},{1,5},{3,7},{12,8},{14,10},{8,... | collective-permute-start | bytes 442376 | tf_op jit(solution)/shard_map/ppermute | solution.py:252
  11.4 2.3 %copy-start = (bf16[1,768,1536]{2,1,0:T(8,128)(2,1)S(1)}, bf16[1,768,1536]{2,1,0:T(8,128)(2,1)}, u32[]{:S(2)}) copy-start(bf16[1,768,1536]{2,1,0:T(8,128)(2,1)} %param.8) | copy-start | bytes 7077892
  13.6 1.8 %collective-permute-start.4 = (bf16[128,1536]{1,0:T(8,128)(2,1)S(1)}, bf16[128,1536]{1,0:T(8,128)(2,1)S(1)}, u32[]{:S(2)}, u32[]{:S(2)}) collective-permute-start(bf16[128,1536]{1,0:T(8,128)(2,1)S(1)} %get-tuple-element.25.refs_0_), channel_id=1, source_target_pairs={{0,1},{1,0},{2,3},{3,2},{4,5},{5,4},{6,7},{7,6},{8,9},{9,8},{10,11... | collective-permute-start | bytes 1179656 | tf_op jit(solution)/shard_map/ppermute | solution.py:306
  16.5 13.9 %collective-permute-start.5 = (bf16[128,896]{1,0:T(8,128)(2,1)S(1)}, bf16[128,896]{1,0:T(8,128)(2,1)S(1)}, u32[]{:S(2)}, u32[]{:S(2)}) collective-permute-start(bf16[128,896]{1,0:T(8,128)(2,1)S(1)} %get-tuple-element.31), channel_id=1, source_target_pairs={{0,10},{2,8},{4,14},{6,12},{8,18},{10,16},{12,22},{14,20},{16,26},... | collective-permute-start | bytes 688136 | tf_op jit(solution)/shard_map/ppermute | solution.py:346
  19.3 11.1 %collective-permute-start.6 = (bf16[128,640]{1,0:T(8,128)(2,1)S(1)}, bf16[128,640]{1,0:T(8,128)(2,1)S(1)}, u32[]{:S(2)}, u32[]{:S(2)}) collective-permute-start(bf16[128,640]{1,0:T(8,128)(2,1)S(1)} %finish_rest.1), channel_id=1, source_target_pairs={{0,10},{2,8},{4,14},{6,12},{8,18},{10,16},{12,22},{14,20},{16,26},... | collective-permute-start | bytes 491528 | tf_op jit(solution)/shard_map/ppermute | solution.py:346

commit v6 on v5

--- a/solution.py
+++ b/solution.py
@@ -198,6 +198,19 @@
     ).astype(BF16)
 
 
+def first_kernel(part_ref, whole_hbm, sem):
+    copy = pltpu.make_async_copy(part_ref, whole_hbm.at[:, pl.ds(0, part_ref.shape[1])], sem)
+    copy.start()
+    copy.wait()
+
+
+def rest_kernel(_, part_ref, whole_hbm, sem):
+    first = whole_hbm.shape[1] - part_ref.shape[1]
+    copy = pltpu.make_async_copy(part_ref, whole_hbm.at[:, pl.ds(first, part_ref.shape[1])], sem)
+    copy.start()
+    copy.wait()
+
+
 def swap_perm(size):
     return [(i, i ^ 1) for i in range(size)]
 
@@ -344,7 +357,27 @@
         for f in range(frames)
     ]
     handed = [lax.ppermute(x, ("segment", "frame"), onward) for x in finished]
-    return jnp.concatenate(handed, axis=1).reshape(clip_tokens.shape)
+    result = jax.ShapeDtypeStruct((own_count, width), BF16)
+    out = pl.pallas_call(
+        first_kernel,
+        out_shape=result,
+        in_specs=[VMEM],
+        out_specs=HBM,
+        scratch_shapes=[pltpu.SemaphoreType.DMA],
+        compiler_params=PARAMS,
+        name="first_columns",
+    )(handed[0])
+    out = pl.pallas_call(
+        rest_kernel,
+        out_shape=result,
+        in_specs=[HBM, VMEM],
+        out_specs=HBM,
+        scratch_shapes=[pltpu.SemaphoreType.DMA],
+        input_output_aliases={0: 0},
+        compiler_params=PARAMS,
+        name="other_columns",
+    )(out, handed[1])
+    return out.reshape(clip_tokens.shape)
 
 
 def solution(mesh):

time: 31.3 us -> 31.2 us (level)
  Pallas kernels: 8.19 us -> 9.56 us
  other arithmetic: 0.78 us -> 0 us
  waiting for transfers between devices: 11.1 us -> 10.4 us
    pallas_call x0 -> x2, Pallas kernels: none -> 1.37 us  [the longest x1 0.7 us: body(): pl.pallas_call(first_kernel, out_shape=result, in_specs=[VMEM], out_specs...]
    concatenate x1 -> x0, other arithmetic: 0.78 us -> none  [body(): return jnp.concatenate(handed, axis=1).reshape(clip_tokens.shape)]
    ppermute x2, waiting for transfers between devices: 9.44 us -> 8.74 us  [body(): handed = [lax.ppermute(x, ('segment', 'frame'), onward) for x in finished]]
  transfers between devices with their start and end apart: 7 -> 7, of which waited for: 4 -> 5; matrix products, arithmetic and copies ran while one was open for 3% -> 3% of each run, Pallas kernels for 23% -> 25%
where the time goes in v6:
time: 31.2 us; the launch traced here: 31.1 us
  waiting for transfers between devices  10.4 us (33%)
  Pallas kernels  9.56 us (31%)
  starting transfers between devices  9.41 us (30%)
  local copies, waits for them, and re-layouts  1 us (3%)
  between operations  0.74 us (2%)
    ppermute x2, waiting for transfers between devices, body(): handed = [lax.ppermute(x, ('segment', 'frame'), onward) for x in finished]  8.74 us
    pallas_call x6, Pallas kernels, call(): pl.pallas_call(kernel, out_shape=outs, in_specs=ins, out_specs=[VMEM] * l...  8.19 us
    ppermute x2, starting transfers between devices, body(): handed = [lax.ppermute(x, ('segment', 'frame'), onward) for x in finished]  4.14 us
    ppermute x2, starting transfers between devices, from_partner(): return lax.ppermute(x, 'frame', swap_perm(frames))  3.47 us
    ppermute x2, starting transfers between devices, from_beyond(): return lax.ppermute(x, 'frame', beyond_perm(frames))  1.73 us
    ppermute x2, waiting for transfers between devices, from_beyond(): return lax.ppermute(x, 'frame', beyond_perm(frames))  1.56 us
    slice x1, local copies, waits for them, and re-layouts, body(): beyond = [from_beyond(own[:sent])] if far else []  0.99 us
    pallas_call x1, Pallas kernels, body(): pl.pallas_call(first_kernel, out_shape=result, in_specs=[VMEM], out_specs...  0.7 us
  transfers between devices with their start and end apart: 7, of which 5 were waited for; matrix products, arithmetic and copies ran while one was open for 3% of the time, Pallas kernels for 25%

profile of v6, /device:TPU:0, one launch (start us, length us, event | category | flops | bytes accessed | tf_op | source)
XLA Modules:
  0.0 31.1 jit_solution(13805239392789289145)
XLA Ops:
  0.0 2.9 %collective-permute-start.1 = (bf16[128,1536]{1,0:T(8,128)(2,1)}, bf16[128,1536]{1,0:T(8,128)(2,1)S(1)}, u32[]{:S(2)}, u32[]{:S(2)}) collective-permute-start(bf16[128,1536]{1,0:T(8,128)(2,1)} %bitcast.12), channel_id=1, source_target_pairs={{0,2},{2,0},{4,6},{6,4},{1,3},{3,1},{5,7},{7,5},{8,10},{10,8},{12,... | collective-permute-start | bytes 1179656 | tf_op jit(solution)/shard_map/ppermute | solution.py:262
  2.9 1.0 %slice.4 = bf16[80,1536]{1,0:T(8,128)(2,1)S(1)} slice(bf16[128,1536]{1,0:T(8,128)(2,1)} %bitcast.13), slice={[0:80], [0:1536]} | slice | bytes 491520 | tf_op jit(solution)/shard_map/slice | solution.py:271
  3.9 1.6 %collective-permute-start.2 = (bf16[80,1536]{1,0:T(8,128)(2,1)S(1)}, bf16[80,1536]{1,0:T(8,128)(2,1)S(1)}, u32[]{:S(2)}, u32[]{:S(2)}) collective-permute-start(bf16[80,1536]{1,0:T(8,128)(2,1)S(1)} %slice.4), channel_id=1, source_target_pairs={{4,0},{6,2},{0,4},{2,6},{5,1},{7,3},{1,5},{3,7},{12,8},{14,10},{8,... | collective-permute-start | bytes 737288 | tf_op jit(solution)/shard_map/ppermute | solution.py:265
  5.5 0.5 %collective-permute-start = (s32[2,6]{1,0:T(2,128)}, s32[2,6]{1,0:T(2,128)S(1)}, u32[]{:S(2)}, u32[]{:S(2)}) collective-permute-start(s32[2,6]{1,0:T(2,128)} %bitcast.16), channel_id=1, source_target_pairs={{0,2},{2,0},{4,6},{6,4},{1,3},{3,1},{5,7},{7,5},{8,10},{10,8},{12,... | collective-permute-start | bytes 152 | tf_op jit(solution)/shard_map/ppermute | solution.py:262
  6.7 3.4 %own_pairs.1 = (f32[3,1536]{1,0:T(4,128)S(1)}, bf16[1536,768]{1,0:T(8,128)(2,1)S(1)}, bf16[1536,1536]{1,0:T(8,128)(2,1)S(1)}, bf16[128,1536]{1,0:T(8,128)(2,1)S(1)}, bf16[48,1536]{1,0:T(8,128)(2,1)S(1)}) custom-call(s32[1]{0:T(128)S(6)} %copy.9.domain_hbm, bf16[3,8,1536]{2,1,0:T(8,128)(2,1)} %bitcast.15, bf16[1536,2304]{1,0:T(8,128)(2,1)} %bitcast.11, ...), custom_call_target="tpu_custom_call" | custom-call | flops 1 | tf_op jit(solution)/shard_map/own_pairs/pallas_call | solution.py:235
  10.1 0.1 collective-permute-start.3
  10.2 1.2 %collective-permute-done.2.rows_ref = bf16[80,1536]{1,0:T(8,128)(2,1)S(1)} collective-permute-done((bf16[80,1536]{1,0:T(8,128)(2,1)S(1)}, bf16[80,1536]{1,0:T(8,128)(2,1)S(1)}, u32[]{:S(2)}, u32[]{:S(2)}) %collective-permute-start.2) | collective-permute-done | bytes 245792 | tf_op jit(solution)/shard_map/ppermute | solution.py:265
  11.4 0.0 copy-start
  11.4 1.1 %beyond_pairs.1.refs_0_ = bf16[80,1536]{1,0:T(8,128)(2,1)S(1)} custom-call(f32[3,1536]{1,0:T(4,128)S(1)} %get-tuple-element.19.modulate_ref, bf16[1536,1536]{1,0:T(8,128)(2,1)S(1)} %get-tuple-element.21.weight_ref, bf16[80,1536]{1,0:T(8,128)(2,1)S(1)} %collective-permute-done.2.rows_ref), custom_call_target="tpu_custom_call" | custom-call | flops 1 | tf_op jit(solution)/shard_map/beyond_pairs/pallas_call | solution.py:235
  12.6 0.0 collective-permute-done.1.rows_ref
  12.6 1.0 %pairs.1 = (bf16[128,1536]{1,0:T(8,128)(2,1)S(1)}, bf16[128,1536]{1,0:T(8,128)(2,1)S(1)}) custom-call(f32[3,1536]{1,0:T(4,128)S(1)} %get-tuple-element.19.modulate_ref, bf16[1536,1536]{1,0:T(8,128)(2,1)S(1)} %get-tuple-element.21.weight_ref, bf16[128,1536]{1,0:T(8,128)(2,1)S(1)} %collective-permute-done.1.rows_ref), custom_call_target="tpu_custom_call" | custom-call | flops 1 | tf_op jit(solution)/shard_map/pairs/pallas_call | solution.py:235
  13.6 0.1 collective-permute-start.4
  13.7 0.0 collective-permute-done.lists_ref
  13.7 0.0 copy-done
  13.7 1.2 %near_attention.1 = (bf16[128,768]{1,0:T(8,128)(2,1)S(1)}, f32[6,128]{1,0:T(8,128)S(1)}, f32[6,128]{1,0:T(8,128)S(1)}, f32[768,128]{1,0:T(8,128)S(1)}) custom-call(s32[2,6]{1,0:T(2,128)S(1)} %collective-permute-done.lists_ref, bf16[1536,768]{1,0:T(8,128)(2,1)S(1)} %get-tuple-element.23.q_weight_ref, bf16[768,1536]{1,0:T(8,128)(2,1)S(1)} %bitcast.8, ...), custom_call_target="tpu_custom_call" | custom-call | flops 10000000000 | tf_op jit(solution)/shard_map/near_attention/pallas_call | solution.py:235
  14.9 0.4 %collective-permute-done.3.refs_1_ = bf16[48,1536]{1,0:T(8,128)(2,1)S(1)} collective-permute-done((bf16[48,1536]{1,0:T(8,128)(2,1)S(1)}, bf16[48,1536]{1,0:T(8,128)(2,1)S(1)}, u32[]{:S(2)}, u32[]{:S(2)}) %collective-permute-start.3) | collective-permute-done | bytes 147488 | tf_op jit(solution)/shard_map/ppermute | solution.py:265
  15.3 0.1 collective-permute-done.4.refs_2_
  15.4 1.1 %finish.1 = (bf16[768,128]{1,0:T(8,128)(2,1)S(1)}, bf16[128,896]{1,0:T(8,128)(2,1)S(1)}) custom-call(s32[2,6]{1,0:T(2,128)S(1)} %collective-permute-done.lists_ref, f32[3,1536]{1,0:T(4,128)S(1)} %get-tuple-element.19.modulate_ref, bf16[768,1536]{1,0:T(8,128)(2,1)S(1)} %bitcast.9, bf16[128,1536]{1,0:T(8,128)(2,1)S(1)} %collective-permute-done.1.rows_ref, ...), custom_call_target="tpu_custom_call" | custom-call | flops 1 | tf_op jit(solution)/shard_map/finish/pallas_call | solution.py:235
  16.5 2.5 %collective-permute-start.5 = (bf16[128,896]{1,0:T(8,128)(2,1)S(1)}, bf16[128,896]{1,0:T(8,128)(2,1)S(1)}, u32[]{:S(2)}, u32[]{:S(2)}) collective-permute-start(bf16[128,896]{1,0:T(8,128)(2,1)S(1)} %get-tuple-element.31), channel_id=1, source_target_pairs={{0,10},{2,8},{4,14},{6,12},{8,18},{10,16},{12,22},{14,20},{16,26},... | collective-permute-start | bytes 688136 | tf_op jit(solution)/shard_map/ppermute | solution.py:359
  19.0 0.4 %finish_rest.1 = bf16[128,640]{1,0:T(8,128)(2,1)S(1)} custom-call(bf16[768,128]{1,0:T(8,128)(2,1)S(1)} %get-tuple-element.32.mixed_ref, f32[3,1536]{1,0:T(4,128)S(1)} %get-tuple-element.19.modulate_ref, bf16[768,1536]{1,0:T(8,128)(2,1)S(1)} %bitcast.10, bf16[128,1536]{1,0:T(8,128)(2,1)S(1)} %collective-permute-done.1.rows_ref), custom_call_target="tpu_custom_call" | custom-call | flops 1 | tf_op jit(solution)/shard_map/finish_rest/pallas_call | solution.py:235
  19.3 1.6 %collective-permute-start.6 = (bf16[128,640]{1,0:T(8,128)(2,1)S(1)}, bf16[128,640]{1,0:T(8,128)(2,1)S(1)}, u32[]{:S(2)}, u32[]{:S(2)}) collective-permute-start(bf16[128,640]{1,0:T(8,128)(2,1)S(1)} %finish_rest.1), channel_id=1, source_target_pairs={{0,10},{2,8},{4,14},{6,12},{8,18},{10,16},{12,22},{14,20},{16,26},... | collective-permute-start | bytes 491528 | tf_op jit(solution)/shard_map/ppermute | solution.py:359
  21.0 6.7 %collective-permute-done.5.part_ref = bf16[128,896]{1,0:T(8,128)(2,1)S(1)} collective-permute-done((bf16[128,896]{1,0:T(8,128)(2,1)S(1)}, bf16[128,896]{1,0:T(8,128)(2,1)S(1)}, u32[]{:S(2)}, u32[]{:S(2)}) %collective-permute-start.5) | collective-permute-done | bytes 229408 | tf_op jit(solution)/shard_map/ppermute | solution.py:359
  27.6 0.7 %first_columns.1._ = bf16[128,1536]{1,0:T(8,128)(2,1)} custom-call(bf16[128,896]{1,0:T(8,128)(2,1)S(1)} %collective-permute-done.5.part_ref), custom_call_target="tpu_custom_call" | custom-call | tf_op jit(solution)/shard_map/first_columns/pallas_call | solution.py:361
  28.4 2.1 %collective-permute-done.6.part_ref = bf16[128,640]{1,0:T(8,128)(2,1)S(1)} collective-permute-done((bf16[128,640]{1,0:T(8,128)(2,1)S(1)}, bf16[128,640]{1,0:T(8,128)(2,1)S(1)}, u32[]{:S(2)}, u32[]{:S(2)}) %collective-permute-start.6) | collective-permute-done | bytes 163872 | tf_op jit(solution)/shard_map/ppermute | solution.py:359
  30.4 0.7 %other_columns.1 = bf16[128,1536]{1,0:T(8,128)(2,1)} custom-call(bf16[128,1536]{1,0:T(8,128)(2,1)} %first_columns.1._, bf16[128,640]{1,0:T(8,128)(2,1)S(1)} %collective-permute-done.6.part_ref), custom_call_target="tpu_custom_call", output_to_operand_aliasing={{}: (0, {})} | custom-call | tf_op jit(solution)/shard_map/other_columns/pallas_call | solution.py:370
Async XLA Ops:
  0.0 12.6 %collective-permute-start.1 = (bf16[128,1536]{1,0:T(8,128)(2,1)}, bf16[128,1536]{1,0:T(8,128)(2,1)S(1)}, u32[]{:S(2)}, u32[]{:S(2)}) collective-permute-start(bf16[128,1536]{1,0:T(8,128)(2,1)} %bitcast.12), channel_id=1, source_target_pairs={{0,2},{2,0},{4,6},{6,4},{1,3},{3,1},{5,7},{7,5},{8,10},{10,8},{12,... | collective-permute-start | bytes 1179656 | tf_op jit(solution)/shard_map/ppermute | solution.py:262
  3.9 7.5 %collective-permute-start.2 = (bf16[80,1536]{1,0:T(8,128)(2,1)S(1)}, bf16[80,1536]{1,0:T(8,128)(2,1)S(1)}, u32[]{:S(2)}, u32[]{:S(2)}) collective-permute-start(bf16[80,1536]{1,0:T(8,128)(2,1)S(1)} %slice.4), channel_id=1, source_target_pairs={{4,0},{6,2},{0,4},{2,6},{5,1},{7,3},{1,5},{3,7},{12,8},{14,10},{8,... | collective-permute-start | bytes 737288 | tf_op jit(solution)/shard_map/ppermute | solution.py:265
  5.5 8.2 %collective-permute-start = (s32[2,6]{1,0:T(2,128)}, s32[2,6]{1,0:T(2,128)S(1)}, u32[]{:S(2)}, u32[]{:S(2)}) collective-permute-start(s32[2,6]{1,0:T(2,128)} %bitcast.16), channel_id=1, source_target_pairs={{0,2},{2,0},{4,6},{6,4},{1,3},{3,1},{5,7},{7,5},{8,10},{10,8},{12,... | collective-permute-start | bytes 152 | tf_op jit(solution)/shard_map/ppermute | solution.py:262
  10.1 5.2 %collective-permute-start.3 = (bf16[48,1536]{1,0:T(8,128)(2,1)S(1)}, bf16[48,1536]{1,0:T(8,128)(2,1)S(1)}, u32[]{:S(2)}, u32[]{:S(2)}) collective-permute-start(bf16[48,1536]{1,0:T(8,128)(2,1)S(1)} %get-tuple-element.30), channel_id=1, source_target_pairs={{4,0},{6,2},{0,4},{2,6},{5,1},{7,3},{1,5},{3,7},{12,8},{14,10},{8,... | collective-permute-start | bytes 442376 | tf_op jit(solution)/shard_map/ppermute | solution.py:265
  11.4 2.3 %copy-start = (bf16[1,768,1536]{2,1,0:T(8,128)(2,1)S(1)}, bf16[1,768,1536]{2,1,0:T(8,128)(2,1)}, u32[]{:S(2)}) copy-start(bf16[1,768,1536]{2,1,0:T(8,128)(2,1)} %param.8) | copy-start | bytes 7077892
  13.6 1.8 %collective-permute-start.4 = (bf16[128,1536]{1,0:T(8,128)(2,1)S(1)}, bf16[128,1536]{1,0:T(8,128)(2,1)S(1)}, u32[]{:S(2)}, u32[]{:S(2)}) collective-permute-start(bf16[128,1536]{1,0:T(8,128)(2,1)S(1)} %get-tuple-element.25.refs_0_), channel_id=1, source_target_pairs={{0,1},{1,0},{2,3},{3,2},{4,5},{5,4},{6,7},{7,6},{8,9},{9,8},{10,11... | collective-permute-start | bytes 1179656 | tf_op jit(solution)/shard_map/ppermute | solution.py:319
  16.5 11.2 %collective-permute-start.5 = (bf16[128,896]{1,0:T(8,128)(2,1)S(1)}, bf16[128,896]{1,0:T(8,128)(2,1)S(1)}, u32[]{:S(2)}, u32[]{:S(2)}) collective-permute-start(bf16[128,896]{1,0:T(8,128)(2,1)S(1)} %get-tuple-element.31), channel_id=1, source_target_pairs={{0,10},{2,8},{4,14},{6,12},{8,18},{10,16},{12,22},{14,20},{16,26},... | collective-permute-start | bytes 688136 | tf_op jit(solution)/shard_map/ppermute | solution.py:359
  19.3 11.1 %collective-permute-start.6 = (bf16[128,640]{1,0:T(8,128)(2,1)S(1)}, bf16[128,640]{1,0:T(8,128)(2,1)S(1)}, u32[]{:S(2)}, u32[]{:S(2)}) collective-permute-start(bf16[128,640]{1,0:T(8,128)(2,1)S(1)} %finish_rest.1), channel_id=1, source_target_pairs={{0,10},{2,8},{4,14},{6,12},{8,18},{10,16},{12,22},{14,20},{16,26},... | collective-permute-start | bytes 491528 | tf_op jit(solution)/shard_map/ppermute | solution.py:359

commit v7 on v6

--- a/solution.py
+++ b/solution.py
@@ -164,24 +164,39 @@
 
 
 def finish_kernel(
-    n_kv, tile_len, slots_of, first,
+    n_far, n_kv, tile_len, slots_of, has_far, first,
     lists_ref, modulate_ref, out_weight_ref, rows_ref, q_ref, peak_ref, total_ref, mix_ref, *refs
 ):
-    kv_refs, (mixed_ref, finished_ref) = refs[:n_kv], refs[n_kv:]
-    count = rows_ref.shape[0]
-    key_count = sum(r.shape[0] for r in kv_refs)
-    bias = masking(lists_ref, slots_of(), tile_len, first, key_count, count)
-    scores = scores_of(q_ref, kv_refs, bias)
-    before = peak_ref[...]
-    peaks = jnp.maximum(reduced(jnp.max, scores), before)
-    raised = raised_from(scores, peaks)
-    kept = jnp.exp((before - peaks) * HD ** (-0.5))
-    share = 1.0 / (total_ref[...] * kept + reduced(jnp.sum, raised))
-    kept = kept * share
-    for h, mix in enumerate(mixes_of(kv_refs, raised)):
-        mixed_ref[head_cols(h), :] = (
-            mix_ref[head_cols(h), :] * kept[h : h + 1] + mix * share[h : h + 1]
-        ).astype(BF16)
+    mixed_ref, finished_ref = refs[n_kv:]
+
+    def join(kv_refs, first):
+        key_count = sum(r.shape[0] for r in kv_refs)
+        bias = masking(lists_ref, slots_of(), tile_len, first, key_count, rows_ref.shape[0])
+        scores = scores_of(q_ref, kv_refs, bias)
+        before = peak_ref[...]
+        peaks = jnp.maximum(reduced(jnp.max, scores), before)
+        raised = raised_from(scores, peaks)
+        kept = jnp.exp((before - peaks) * HD ** (-0.5))
+        share = 1.0 / (total_ref[...] * kept + reduced(jnp.sum, raised))
+        kept = kept * share
+        for h, mix in enumerate(mixes_of(kv_refs, raised)):
+            mixed_ref[head_cols(h), :] = (
+                mix_ref[head_cols(h), :] * kept[h : h + 1] + mix * share[h : h + 1]
+            ).astype(BF16)
+
+    if n_far:
+        far = has_far()
+
+        @pl.when(far)
+        def _():
+            join(refs[:n_kv], first)
+
+        @pl.when(jnp.logical_not(far))
+        def _():
+            join(refs[n_far:n_kv], first + sum(r.shape[0] for r in refs[:n_far]))
+
+    else:
+        join(refs[:n_kv], first)
     output_columns(0, mixed_ref, modulate_ref, out_weight_ref, rows_ref, finished_ref)
 
 
@@ -333,11 +348,21 @@
         name="near_attention",
         weight=10**10,
     )
+    def has_far():
+        frame = lax.axis_index("frame")
+        return jnp.where(frame % 2 == 0, frame + 2 < frames, frame >= 2)
+
     late = [*kv_beyond, *kv_tail, *kv_rows]
     first_cols = width * FIRST // 12
     mixed, *finished = call(
         functools.partial(
-            finish_kernel, len(late), tile_len, slots_of, sum(x.shape[0] for x in near)
+            finish_kernel,
+            len(late) - len(kv_rows),
+            len(late),
+            tile_len,
+            slots_of,
+            has_far,
+            sum(x.shape[0] for x in near),
         ),
         [VMEM] * (8 + len(late)),
         [held(inner, own_count), held(own_count, first_cols)],

time: 31.2 us -> 31.2 us (level)
  no operation moved by 1% of the time
where the time goes in v7:
time: 31.2 us; the launch traced here: 31.1 us
  waiting for transfers between devices  10.3 us (33%)
  Pallas kernels  9.61 us (31%)
  starting transfers between devices  9.43 us (30%)
  local copies, waits for them, and re-layouts  1 us (3%)
  between operations  0.74 us (2%)
    ppermute x2, waiting for transfers between devices, body(): handed = [lax.ppermute(x, ('segment', 'frame'), onward) for x in finished]  8.67 us
    pallas_call x6, Pallas kernels, call(): pl.pallas_call(kernel, out_shape=outs, in_specs=ins, out_specs=[VMEM] * l...  8.25 us
    ppermute x2, starting transfers between devices, body(): handed = [lax.ppermute(x, ('segment', 'frame'), onward) for x in finished]  4.15 us
    ppermute x2, starting transfers between devices, from_partner(): return lax.ppermute(x, 'frame', swap_perm(frames))  3.47 us
    ppermute x2, starting transfers between devices, from_beyond(): return lax.ppermute(x, 'frame', beyond_perm(frames))  1.73 us
    ppermute x2, waiting for transfers between devices, from_beyond(): return lax.ppermute(x, 'frame', beyond_perm(frames))  1.56 us
    slice x1, local copies, waits for them, and re-layouts, body(): beyond = [from_beyond(own[:sent])] if far else []  0.99 us
    pallas_call x1, Pallas kernels, body(): pl.pallas_call(first_kernel, out_shape=result, in_specs=[VMEM], out_specs...  0.7 us
  transfers between devices with their start and end apart: 7, of which 5 were waited for; matrix products, arithmetic and copies ran while one was open for 3% of the time, Pallas kernels for 25%

profile of v7, /device:TPU:0, one launch (start us, length us, event | category | flops | bytes accessed | tf_op | source)
XLA Modules:
  0.0 31.1 jit_solution(8820456576622958586)
XLA Ops:
  0.0 2.9 %collective-permute-start.1 = (bf16[128,1536]{1,0:T(8,128)(2,1)}, bf16[128,1536]{1,0:T(8,128)(2,1)S(1)}, u32[]{:S(2)}, u32[]{:S(2)}) collective-permute-start(bf16[128,1536]{1,0:T(8,128)(2,1)} %bitcast.12), channel_id=1, source_target_pairs={{0,2},{2,0},{4,6},{6,4},{1,3},{3,1},{5,7},{7,5},{8,10},{10,8},{12,... | collective-permute-start | bytes 1179656 | tf_op jit(solution)/shard_map/ppermute | solution.py:277
  2.9 1.0 %slice.4 = bf16[80,1536]{1,0:T(8,128)(2,1)S(1)} slice(bf16[128,1536]{1,0:T(8,128)(2,1)} %bitcast.13), slice={[0:80], [0:1536]} | slice | bytes 491520 | tf_op jit(solution)/shard_map/slice | solution.py:286
  3.9 1.6 %collective-permute-start.2 = (bf16[80,1536]{1,0:T(8,128)(2,1)S(1)}, bf16[80,1536]{1,0:T(8,128)(2,1)S(1)}, u32[]{:S(2)}, u32[]{:S(2)}) collective-permute-start(bf16[80,1536]{1,0:T(8,128)(2,1)S(1)} %slice.4), channel_id=1, source_target_pairs={{4,0},{6,2},{0,4},{2,6},{5,1},{7,3},{1,5},{3,7},{12,8},{14,10},{8,... | collective-permute-start | bytes 737288 | tf_op jit(solution)/shard_map/ppermute | solution.py:280
  5.5 0.5 %collective-permute-start = (s32[2,6]{1,0:T(2,128)}, s32[2,6]{1,0:T(2,128)S(1)}, u32[]{:S(2)}, u32[]{:S(2)}) collective-permute-start(s32[2,6]{1,0:T(2,128)} %bitcast.16), channel_id=1, source_target_pairs={{0,2},{2,0},{4,6},{6,4},{1,3},{3,1},{5,7},{7,5},{8,10},{10,8},{12,... | collective-permute-start | bytes 152 | tf_op jit(solution)/shard_map/ppermute | solution.py:277
  6.7 3.4 %own_pairs.1 = (f32[3,1536]{1,0:T(4,128)S(1)}, bf16[1536,768]{1,0:T(8,128)(2,1)S(1)}, bf16[1536,1536]{1,0:T(8,128)(2,1)S(1)}, bf16[128,1536]{1,0:T(8,128)(2,1)S(1)}, bf16[48,1536]{1,0:T(8,128)(2,1)S(1)}) custom-call(s32[1]{0:T(128)S(6)} %copy.9.domain_hbm, bf16[3,8,1536]{2,1,0:T(8,128)(2,1)} %bitcast.15, bf16[1536,2304]{1,0:T(8,128)(2,1)} %bitcast.11, ...), custom_call_target="tpu_custom_call" | custom-call | flops 1 | tf_op jit(solution)/shard_map/own_pairs/pallas_call | solution.py:250
  10.1 0.1 collective-permute-start.3
  10.2 1.2 %collective-permute-done.2.rows_ref = bf16[80,1536]{1,0:T(8,128)(2,1)S(1)} collective-permute-done((bf16[80,1536]{1,0:T(8,128)(2,1)S(1)}, bf16[80,1536]{1,0:T(8,128)(2,1)S(1)}, u32[]{:S(2)}, u32[]{:S(2)}) %collective-permute-start.2) | collective-permute-done | bytes 245792 | tf_op jit(solution)/shard_map/ppermute | solution.py:280
  11.4 0.0 copy-start
  11.4 1.1 %beyond_pairs.1.refs_0_ = bf16[80,1536]{1,0:T(8,128)(2,1)S(1)} custom-call(f32[3,1536]{1,0:T(4,128)S(1)} %get-tuple-element.19.modulate_ref, bf16[1536,1536]{1,0:T(8,128)(2,1)S(1)} %get-tuple-element.21.weight_ref, bf16[80,1536]{1,0:T(8,128)(2,1)S(1)} %collective-permute-done.2.rows_ref), custom_call_target="tpu_custom_call" | custom-call | flops 1 | tf_op jit(solution)/shard_map/beyond_pairs/pallas_call | solution.py:250
  12.6 0.0 collective-permute-done.1.rows_ref
  12.6 1.0 %pairs.1 = (bf16[128,1536]{1,0:T(8,128)(2,1)S(1)}, bf16[128,1536]{1,0:T(8,128)(2,1)S(1)}) custom-call(f32[3,1536]{1,0:T(4,128)S(1)} %get-tuple-element.19.modulate_ref, bf16[1536,1536]{1,0:T(8,128)(2,1)S(1)} %get-tuple-element.21.weight_ref, bf16[128,1536]{1,0:T(8,128)(2,1)S(1)} %collective-permute-done.1.rows_ref), custom_call_target="tpu_custom_call" | custom-call | flops 1 | tf_op jit(solution)/shard_map/pairs/pallas_call | solution.py:250
  13.6 0.1 collective-permute-start.4
  13.7 0.0 collective-permute-done.lists_ref
  13.7 0.0 copy-done
  13.7 1.2 %near_attention.1 = (bf16[128,768]{1,0:T(8,128)(2,1)S(1)}, f32[6,128]{1,0:T(8,128)S(1)}, f32[6,128]{1,0:T(8,128)S(1)}, f32[768,128]{1,0:T(8,128)S(1)}) custom-call(s32[2,6]{1,0:T(2,128)S(1)} %collective-permute-done.lists_ref, bf16[1536,768]{1,0:T(8,128)(2,1)S(1)} %get-tuple-element.23.q_weight_ref, bf16[768,1536]{1,0:T(8,128)(2,1)S(1)} %bitcast.8, ...), custom_call_target="tpu_custom_call" | custom-call | flops 10000000000 | tf_op jit(solution)/shard_map/near_attention/pallas_call | solution.py:250
  14.9 0.4 %collective-permute-done.3.refs_1_ = bf16[48,1536]{1,0:T(8,128)(2,1)S(1)} collective-permute-done((bf16[48,1536]{1,0:T(8,128)(2,1)S(1)}, bf16[48,1536]{1,0:T(8,128)(2,1)S(1)}, u32[]{:S(2)}, u32[]{:S(2)}) %collective-permute-start.3) | collective-permute-done | bytes 147488 | tf_op jit(solution)/shard_map/ppermute | solution.py:280
  15.3 0.1 collective-permute-done.4.refs_2_
  15.4 1.1 %finish.1 = (bf16[768,128]{1,0:T(8,128)(2,1)S(1)}, bf16[128,896]{1,0:T(8,128)(2,1)S(1)}) custom-call(s32[2,6]{1,0:T(2,128)S(1)} %collective-permute-done.lists_ref, f32[3,1536]{1,0:T(4,128)S(1)} %get-tuple-element.19.modulate_ref, bf16[768,1536]{1,0:T(8,128)(2,1)S(1)} %bitcast.9, bf16[128,1536]{1,0:T(8,128)(2,1)S(1)} %collective-permute-done.1.rows_ref, ...), custom_call_target="tpu_custom_call" | custom-call | flops 1 | tf_op jit(solution)/shard_map/finish/pallas_call | solution.py:250
  16.5 2.3 %collective-permute-start.5 = (bf16[128,896]{1,0:T(8,128)(2,1)S(1)}, bf16[128,896]{1,0:T(8,128)(2,1)S(1)}, u32[]{:S(2)}, u32[]{:S(2)}) collective-permute-start(bf16[128,896]{1,0:T(8,128)(2,1)S(1)} %get-tuple-element.31), channel_id=1, source_target_pairs={{0,10},{2,8},{4,14},{6,12},{8,18},{10,16},{12,22},{14,20},{16,26},... | collective-permute-start | bytes 688136 | tf_op jit(solution)/shard_map/ppermute | solution.py:384
  18.8 0.4 %finish_rest.1 = bf16[128,640]{1,0:T(8,128)(2,1)S(1)} custom-call(bf16[768,128]{1,0:T(8,128)(2,1)S(1)} %get-tuple-element.32.mixed_ref, f32[3,1536]{1,0:T(4,128)S(1)} %get-tuple-element.19.modulate_ref, bf16[768,1536]{1,0:T(8,128)(2,1)S(1)} %bitcast.10, bf16[128,1536]{1,0:T(8,128)(2,1)S(1)} %collective-permute-done.1.rows_ref), custom_call_target="tpu_custom_call" | custom-call | flops 1 | tf_op jit(solution)/shard_map/finish_rest/pallas_call | solution.py:250
  19.2 1.8 %collective-permute-start.6 = (bf16[128,640]{1,0:T(8,128)(2,1)S(1)}, bf16[128,640]{1,0:T(8,128)(2,1)S(1)}, u32[]{:S(2)}, u32[]{:S(2)}) collective-permute-start(bf16[128,640]{1,0:T(8,128)(2,1)S(1)} %finish_rest.1), channel_id=1, source_target_pairs={{0,10},{2,8},{4,14},{6,12},{8,18},{10,16},{12,22},{14,20},{16,26},... | collective-permute-start | bytes 491528 | tf_op jit(solution)/shard_map/ppermute | solution.py:384
  21.0 6.7 %collective-permute-done.5.part_ref = bf16[128,896]{1,0:T(8,128)(2,1)S(1)} collective-permute-done((bf16[128,896]{1,0:T(8,128)(2,1)S(1)}, bf16[128,896]{1,0:T(8,128)(2,1)S(1)}, u32[]{:S(2)}, u32[]{:S(2)}) %collective-permute-start.5) | collective-permute-done | bytes 229408 | tf_op jit(solution)/shard_map/ppermute | solution.py:384
  27.7 0.7 %first_columns.1._ = bf16[128,1536]{1,0:T(8,128)(2,1)} custom-call(bf16[128,896]{1,0:T(8,128)(2,1)S(1)} %collective-permute-done.5.part_ref), custom_call_target="tpu_custom_call" | custom-call | tf_op jit(solution)/shard_map/first_columns/pallas_call | solution.py:386
  28.4 2.0 %collective-permute-done.6.part_ref = bf16[128,640]{1,0:T(8,128)(2,1)S(1)} collective-permute-done((bf16[128,640]{1,0:T(8,128)(2,1)S(1)}, bf16[128,640]{1,0:T(8,128)(2,1)S(1)}, u32[]{:S(2)}, u32[]{:S(2)}) %collective-permute-start.6) | collective-permute-done | bytes 163872 | tf_op jit(solution)/shard_map/ppermute | solution.py:384
  30.4 0.7 %other_columns.1 = bf16[128,1536]{1,0:T(8,128)(2,1)} custom-call(bf16[128,1536]{1,0:T(8,128)(2,1)} %first_columns.1._, bf16[128,640]{1,0:T(8,128)(2,1)S(1)} %collective-permute-done.6.part_ref), custom_call_target="tpu_custom_call", output_to_operand_aliasing={{}: (0, {})} | custom-call | tf_op jit(solution)/shard_map/other_columns/pallas_call | solution.py:395
Async XLA Ops:
  0.0 12.6 %collective-permute-start.1 = (bf16[128,1536]{1,0:T(8,128)(2,1)}, bf16[128,1536]{1,0:T(8,128)(2,1)S(1)}, u32[]{:S(2)}, u32[]{:S(2)}) collective-permute-start(bf16[128,1536]{1,0:T(8,128)(2,1)} %bitcast.12), channel_id=1, source_target_pairs={{0,2},{2,0},{4,6},{6,4},{1,3},{3,1},{5,7},{7,5},{8,10},{10,8},{12,... | collective-permute-start | bytes 1179656 | tf_op jit(solution)/shard_map/ppermute | solution.py:277
  3.9 7.5 %collective-permute-start.2 = (bf16[80,1536]{1,0:T(8,128)(2,1)S(1)}, bf16[80,1536]{1,0:T(8,128)(2,1)S(1)}, u32[]{:S(2)}, u32[]{:S(2)}) collective-permute-start(bf16[80,1536]{1,0:T(8,128)(2,1)S(1)} %slice.4), channel_id=1, source_target_pairs={{4,0},{6,2},{0,4},{2,6},{5,1},{7,3},{1,5},{3,7},{12,8},{14,10},{8,... | collective-permute-start | bytes 737288 | tf_op jit(solution)/shard_map/ppermute | solution.py:280
  5.5 8.2 %collective-permute-start = (s32[2,6]{1,0:T(2,128)}, s32[2,6]{1,0:T(2,128)S(1)}, u32[]{:S(2)}, u32[]{:S(2)}) collective-permute-start(s32[2,6]{1,0:T(2,128)} %bitcast.16), channel_id=1, source_target_pairs={{0,2},{2,0},{4,6},{6,4},{1,3},{3,1},{5,7},{7,5},{8,10},{10,8},{12,... | collective-permute-start | bytes 152 | tf_op jit(solution)/shard_map/ppermute | solution.py:277
  10.1 5.2 %collective-permute-start.3 = (bf16[48,1536]{1,0:T(8,128)(2,1)S(1)}, bf16[48,1536]{1,0:T(8,128)(2,1)S(1)}, u32[]{:S(2)}, u32[]{:S(2)}) collective-permute-start(bf16[48,1536]{1,0:T(8,128)(2,1)S(1)} %get-tuple-element.30), channel_id=1, source_target_pairs={{4,0},{6,2},{0,4},{2,6},{5,1},{7,3},{1,5},{3,7},{12,8},{14,10},{8,... | collective-permute-start | bytes 442376 | tf_op jit(solution)/shard_map/ppermute | solution.py:280
  11.4 2.3 %copy-start = (bf16[1,768,1536]{2,1,0:T(8,128)(2,1)S(1)}, bf16[1,768,1536]{2,1,0:T(8,128)(2,1)}, u32[]{:S(2)}) copy-start(bf16[1,768,1536]{2,1,0:T(8,128)(2,1)} %param.8) | copy-start | bytes 7077892
  13.6 1.8 %collective-permute-start.4 = (bf16[128,1536]{1,0:T(8,128)(2,1)S(1)}, bf16[128,1536]{1,0:T(8,128)(2,1)S(1)}, u32[]{:S(2)}, u32[]{:S(2)}) collective-permute-start(bf16[128,1536]{1,0:T(8,128)(2,1)S(1)} %get-tuple-element.25.refs_0_), channel_id=1, source_target_pairs={{0,1},{1,0},{2,3},{3,2},{4,5},{5,4},{6,7},{7,6},{8,9},{9,8},{10,11... | collective-permute-start | bytes 1179656 | tf_op jit(solution)/shard_map/ppermute | solution.py:334
  16.5 11.2 %collective-permute-start.5 = (bf16[128,896]{1,0:T(8,128)(2,1)S(1)}, bf16[128,896]{1,0:T(8,128)(2,1)S(1)}, u32[]{:S(2)}, u32[]{:S(2)}) collective-permute-start(bf16[128,896]{1,0:T(8,128)(2,1)S(1)} %get-tuple-element.31), channel_id=1, source_target_pairs={{0,10},{2,8},{4,14},{6,12},{8,18},{10,16},{12,22},{14,20},{16,26},... | collective-permute-start | bytes 688136 | tf_op jit(solution)/shard_map/ppermute | solution.py:384
  19.2 11.2 %collective-permute-start.6 = (bf16[128,640]{1,0:T(8,128)(2,1)S(1)}, bf16[128,640]{1,0:T(8,128)(2,1)S(1)}, u32[]{:S(2)}, u32[]{:S(2)}) collective-permute-start(bf16[128,640]{1,0:T(8,128)(2,1)S(1)} %finish_rest.1), channel_id=1, source_target_pairs={{0,10},{2,8},{4,14},{6,12},{8,18},{10,16},{12,22},{14,20},{16,26},... | collective-permute-start | bytes 491528 | tf_op jit(solution)/shard_map/ppermute | solution.py:384

commit v8 on v7

--- a/solution.py
+++ b/solution.py
@@ -12,7 +12,7 @@
 MASKED = -1e30
 RAW = 5
 LOADS = 4
-FIRST = 7
+PARTS = (5, 4, 3)
 F32 = jnp.float32
 BF16 = jnp.bfloat16
 VMEM = pl.BlockSpec(memory_space=pltpu.VMEM)
@@ -219,8 +219,7 @@
     copy.wait()
 
 
-def rest_kernel(_, part_ref, whole_hbm, sem):
-    first = whole_hbm.shape[1] - part_ref.shape[1]
+def rest_kernel(first, _, part_ref, whole_hbm, sem):
     copy = pltpu.make_async_copy(part_ref, whole_hbm.at[:, pl.ds(first, part_ref.shape[1])], sem)
     copy.start()
     copy.wait()
@@ -353,7 +352,7 @@
         return jnp.where(frame % 2 == 0, frame + 2 < frames, frame >= 2)
 
     late = [*kv_beyond, *kv_tail, *kv_rows]
-    first_cols = width * FIRST // 12
+    cuts = [width * sum(PARTS[:i]) // sum(PARTS) for i in range(len(PARTS) + 1)]
     mixed, *finished = call(
         functools.partial(
             finish_kernel,
@@ -365,17 +364,18 @@
             sum(x.shape[0] for x in near),
         ),
         [VMEM] * (8 + len(late)),
-        [held(inner, own_count), held(own_count, first_cols)],
+        [held(inner, own_count), held(own_count, cuts[1])],
         [lists, modulate, out_weight[0], tokens, q, *partial, *late],
         name="finish",
     )
-    finished += call(
-        functools.partial(output_columns, first_cols),
-        [VMEM] * 4,
-        [held(own_count, width - first_cols)],
-        [mixed, modulate, out_weight[0], tokens],
-        name="finish_rest",
-    )
+    for start, end in zip(cuts[1:-1], cuts[2:]):
+        finished += call(
+            functools.partial(output_columns, start),
+            [VMEM] * 4,
+            [held(own_count, end - start)],
+            [mixed, modulate, out_weight[0], tokens],
+            name="finish_rest",
+        )
     onward = [
         (s * frames + f, (s + 1) % segments * frames + (f ^ 1))
         for s in range(segments)
@@ -392,16 +392,17 @@
         compiler_params=PARAMS,
         name="first_columns",
     )(handed[0])
-    out = pl.pallas_call(
-        rest_kernel,
-        out_shape=result,
-        in_specs=[HBM, VMEM],
-        out_specs=HBM,
-        scratch_shapes=[pltpu.SemaphoreType.DMA],
-        input_output_aliases={0: 0},
-        compiler_params=PARAMS,
-        name="other_columns",
-    )(out, handed[1])
+    for start, part in zip(cuts[1:], handed[1:]):
+        out = pl.pallas_call(
+            functools.partial(rest_kernel, start),
+            out_shape=result,
+            in_specs=[HBM, VMEM],
+            out_specs=HBM,
+            scratch_shapes=[pltpu.SemaphoreType.DMA],
+            input_output_aliases={0: 0},
+            compiler_params=PARAMS,
+            name="other_columns",
+        )(out, part)
     return out.reshape(clip_tokens.shape)
 
 

time: 31.2 us -> 31.2 us (level)
  waiting for transfers between devices: 10.3 us -> 7.09 us
  starting transfers between devices: 9.43 us -> 11.8 us
  Pallas kernels: 9.61 us -> 10.4 us
    ppermute x2 -> x3, waiting for transfers between devices: 8.67 us -> 5.46 us  [body(): handed = [lax.ppermute(x, ('segment', 'frame'), onward) for x in finished]]
    ppermute x2 -> x3, starting transfers between devices: 4.15 us -> 6.5 us  [body(): handed = [lax.ppermute(x, ('segment', 'frame'), onward) for x in finished]]
    pallas_call x1 -> x2, Pallas kernels: 0.67 us -> 1.31 us  [body(): pl.pallas_call(functools.partial(rest_kernel, start), out_shape=result, i...]
    pallas_call x6 -> x7, Pallas kernels: 8.25 us -> 8.43 us  [call(): pl.pallas_call(kernel, out_shape=outs, in_specs=ins, out_specs=[VMEM] * l...]
  transfers between devices with their start and end apart: 7 -> 8, of which waited for: 5 -> 6; matrix products, arithmetic and copies ran while one was open for 3% -> 3% of each run, Pallas kernels for 25% -> 28%
where the time goes in v8:
time: 31.2 us; the launch traced here: 31 us
  starting transfers between devices  11.8 us (38%)
  Pallas kernels  10.4 us (33%)
  waiting for transfers between devices  7.09 us (23%)
  local copies, waits for them, and re-layouts  1 us (3%)
  between operations  0.75 us (2%)
    pallas_call x7, Pallas kernels, call(): pl.pallas_call(kernel, out_shape=outs, in_specs=ins, out_specs=[VMEM] * l...  8.43 us
    ppermute x3, starting transfers between devices, body(): handed = [lax.ppermute(x, ('segment', 'frame'), onward) for x in finished]  6.5 us
    ppermute x3, waiting for transfers between devices, body(): handed = [lax.ppermute(x, ('segment', 'frame'), onward) for x in finished]  5.46 us
    ppermute x2, starting transfers between devices, from_partner(): return lax.ppermute(x, 'frame', swap_perm(frames))  3.47 us
    ppermute x2, starting transfers between devices, from_beyond(): return lax.ppermute(x, 'frame', beyond_perm(frames))  1.73 us
    ppermute x2, waiting for transfers between devices, from_beyond(): return lax.ppermute(x, 'frame', beyond_perm(frames))  1.52 us
    pallas_call x2, Pallas kernels, body(): pl.pallas_call(functools.partial(rest_kernel, start), out_shape=result, i...  1.31 us
    slice x1, local copies, waits for them, and re-layouts, body(): beyond = [from_beyond(own[:sent])] if far else []  0.99 us
  transfers between devices with their start and end apart: 8, of which 6 were waited for; matrix products, arithmetic and copies ran while one was open for 3% of the time, Pallas kernels for 28%

profile of v8, /device:TPU:0, one launch (start us, length us, event | category | flops | bytes accessed | tf_op | source)
XLA Modules:
  0.0 31.0 jit_solution(2437089208675317791)
XLA Ops:
  0.0 2.9 %collective-permute-start.1 = (bf16[128,1536]{1,0:T(8,128)(2,1)}, bf16[128,1536]{1,0:T(8,128)(2,1)S(1)}, u32[]{:S(2)}, u32[]{:S(2)}) collective-permute-start(bf16[128,1536]{1,0:T(8,128)(2,1)} %bitcast.13), channel_id=1, source_target_pairs={{0,2},{2,0},{4,6},{6,4},{1,3},{3,1},{5,7},{7,5},{8,10},{10,8},{12,... | collective-permute-start | bytes 1179656 | tf_op jit(solution)/shard_map/ppermute | solution.py:276
  2.9 1.0 %slice.4 = bf16[80,1536]{1,0:T(8,128)(2,1)S(1)} slice(bf16[128,1536]{1,0:T(8,128)(2,1)} %bitcast.14), slice={[0:80], [0:1536]} | slice | bytes 491520 | tf_op jit(solution)/shard_map/slice | solution.py:285
  3.9 1.6 %collective-permute-start.2 = (bf16[80,1536]{1,0:T(8,128)(2,1)S(1)}, bf16[80,1536]{1,0:T(8,128)(2,1)S(1)}, u32[]{:S(2)}, u32[]{:S(2)}) collective-permute-start(bf16[80,1536]{1,0:T(8,128)(2,1)S(1)} %slice.4), channel_id=1, source_target_pairs={{4,0},{6,2},{0,4},{2,6},{5,1},{7,3},{1,5},{3,7},{12,8},{14,10},{8,... | collective-permute-start | bytes 737288 | tf_op jit(solution)/shard_map/ppermute | solution.py:279
  5.5 0.5 %collective-permute-start = (s32[2,6]{1,0:T(2,128)}, s32[2,6]{1,0:T(2,128)S(1)}, u32[]{:S(2)}, u32[]{:S(2)}) collective-permute-start(s32[2,6]{1,0:T(2,128)} %bitcast.17), channel_id=1, source_target_pairs={{0,2},{2,0},{4,6},{6,4},{1,3},{3,1},{5,7},{7,5},{8,10},{10,8},{12,... | collective-permute-start | bytes 152 | tf_op jit(solution)/shard_map/ppermute | solution.py:276
  6.7 3.4 %own_pairs.1 = (f32[3,1536]{1,0:T(4,128)S(1)}, bf16[1536,768]{1,0:T(8,128)(2,1)S(1)}, bf16[1536,1536]{1,0:T(8,128)(2,1)S(1)}, bf16[128,1536]{1,0:T(8,128)(2,1)S(1)}, bf16[48,1536]{1,0:T(8,128)(2,1)S(1)}) custom-call(s32[1]{0:T(128)S(6)} %copy.11.domain_hbm, bf16[3,8,1536]{2,1,0:T(8,128)(2,1)} %bitcast.16, bf16[1536,2304]{1,0:T(8,128)(2,1)} %bitcast.12, ...), custom_call_target="tpu_custom_call" | custom-call | flops 1 | tf_op jit(solution)/shard_map/own_pairs/pallas_call | solution.py:249
  10.1 0.1 collective-permute-start.3
  10.2 1.2 %collective-permute-done.2.rows_ref = bf16[80,1536]{1,0:T(8,128)(2,1)S(1)} collective-permute-done((bf16[80,1536]{1,0:T(8,128)(2,1)S(1)}, bf16[80,1536]{1,0:T(8,128)(2,1)S(1)}, u32[]{:S(2)}, u32[]{:S(2)}) %collective-permute-start.2) | collective-permute-done | bytes 245792 | tf_op jit(solution)/shard_map/ppermute | solution.py:279
  11.4 0.0 copy-start
  11.4 1.1 %beyond_pairs.1.refs_0_ = bf16[80,1536]{1,0:T(8,128)(2,1)S(1)} custom-call(f32[3,1536]{1,0:T(4,128)S(1)} %get-tuple-element.19.modulate_ref, bf16[1536,1536]{1,0:T(8,128)(2,1)S(1)} %get-tuple-element.21.weight_ref, bf16[80,1536]{1,0:T(8,128)(2,1)S(1)} %collective-permute-done.2.rows_ref), custom_call_target="tpu_custom_call" | custom-call | flops 1 | tf_op jit(solution)/shard_map/beyond_pairs/pallas_call | solution.py:249
  12.6 0.0 collective-permute-done.1.rows_ref
  12.6 1.0 %pairs.1 = (bf16[128,1536]{1,0:T(8,128)(2,1)S(1)}, bf16[128,1536]{1,0:T(8,128)(2,1)S(1)}) custom-call(f32[3,1536]{1,0:T(4,128)S(1)} %get-tuple-element.19.modulate_ref, bf16[1536,1536]{1,0:T(8,128)(2,1)S(1)} %get-tuple-element.21.weight_ref, bf16[128,1536]{1,0:T(8,128)(2,1)S(1)} %collective-permute-done.1.rows_ref), custom_call_target="tpu_custom_call" | custom-call | flops 1 | tf_op jit(solution)/shard_map/pairs/pallas_call | solution.py:249
  13.6 0.1 collective-permute-start.4
  13.7 0.0 collective-permute-done.lists_ref
  13.7 0.0 copy-done
  13.7 1.2 %near_attention.1 = (bf16[128,768]{1,0:T(8,128)(2,1)S(1)}, f32[6,128]{1,0:T(8,128)S(1)}, f32[6,128]{1,0:T(8,128)S(1)}, f32[768,128]{1,0:T(8,128)S(1)}) custom-call(s32[2,6]{1,0:T(2,128)S(1)} %collective-permute-done.lists_ref, bf16[1536,768]{1,0:T(8,128)(2,1)S(1)} %get-tuple-element.23.q_weight_ref, bf16[768,1536]{1,0:T(8,128)(2,1)S(1)} %bitcast.8, ...), custom_call_target="tpu_custom_call" | custom-call | flops 10000000000 | tf_op jit(solution)/shard_map/near_attention/pallas_call | solution.py:249
  15.0 0.3 %collective-permute-done.3.refs_1_ = bf16[48,1536]{1,0:T(8,128)(2,1)S(1)} collective-permute-done((bf16[48,1536]{1,0:T(8,128)(2,1)S(1)}, bf16[48,1536]{1,0:T(8,128)(2,1)S(1)}, u32[]{:S(2)}, u32[]{:S(2)}) %collective-permute-start.3) | collective-permute-done | bytes 147488 | tf_op jit(solution)/shard_map/ppermute | solution.py:279
  15.3 0.1 collective-permute-done.4.refs_2_
  15.4 1.0 %finish.1 = (bf16[768,128]{1,0:T(8,128)(2,1)S(1)}, bf16[128,640]{1,0:T(8,128)(2,1)S(1)}) custom-call(s32[2,6]{1,0:T(2,128)S(1)} %collective-permute-done.lists_ref, f32[3,1536]{1,0:T(4,128)S(1)} %get-tuple-element.19.modulate_ref, bf16[768,1536]{1,0:T(8,128)(2,1)S(1)} %bitcast.9, bf16[128,1536]{1,0:T(8,128)(2,1)S(1)} %collective-permute-done.1.rows_ref, ...), custom_call_target="tpu_custom_call" | custom-call | flops 1 | tf_op jit(solution)/shard_map/finish/pallas_call | solution.py:249
  16.5 2.3 %collective-permute-start.5 = (bf16[128,640]{1,0:T(8,128)(2,1)S(1)}, bf16[128,640]{1,0:T(8,128)(2,1)S(1)}, u32[]{:S(2)}, u32[]{:S(2)}) collective-permute-start(bf16[128,640]{1,0:T(8,128)(2,1)S(1)} %get-tuple-element.31), channel_id=1, source_target_pairs={{0,10},{2,8},{4,14},{6,12},{8,18},{10,16},{12,22},{14,20},{16,26},... | collective-permute-start | bytes 491528 | tf_op jit(solution)/shard_map/ppermute | solution.py:384
  18.8 0.3 finish_rest.2
  19.1 1.8 %collective-permute-start.6 = (bf16[128,512]{1,0:T(8,128)(2,1)S(1)}, bf16[128,512]{1,0:T(8,128)(2,1)S(1)}, u32[]{:S(2)}, u32[]{:S(2)}) collective-permute-start(bf16[128,512]{1,0:T(8,128)(2,1)S(1)} %finish_rest.2), channel_id=1, source_target_pairs={{0,10},{2,8},{4,14},{6,12},{8,18},{10,16},{12,22},{14,20},{16,26},... | collective-permute-start | bytes 393224 | tf_op jit(solution)/shard_map/ppermute | solution.py:384
  20.9 0.3 finish_rest.3
  21.2 2.3 %collective-permute-start.7 = (bf16[128,384]{1,0:T(8,128)(2,1)S(1)}, bf16[128,384]{1,0:T(8,128)(2,1)S(1)}, u32[]{:S(2)}, u32[]{:S(2)}) collective-permute-start(bf16[128,384]{1,0:T(8,128)(2,1)S(1)} %finish_rest.3), channel_id=1, source_target_pairs={{0,10},{2,8},{4,14},{6,12},{8,18},{10,16},{12,22},{14,20},{16,26},... | collective-permute-start | bytes 294920 | tf_op jit(solution)/shard_map/ppermute | solution.py:384
  23.6 2.7 %collective-permute-done.5.part_ref = bf16[128,640]{1,0:T(8,128)(2,1)S(1)} collective-permute-done((bf16[128,640]{1,0:T(8,128)(2,1)S(1)}, bf16[128,640]{1,0:T(8,128)(2,1)S(1)}, u32[]{:S(2)}, u32[]{:S(2)}) %collective-permute-start.5) | collective-permute-done | bytes 163872 | tf_op jit(solution)/shard_map/ppermute | solution.py:384
  26.3 0.7 %first_columns.1._ = bf16[128,1536]{1,0:T(8,128)(2,1)} custom-call(bf16[128,640]{1,0:T(8,128)(2,1)S(1)} %collective-permute-done.5.part_ref), custom_call_target="tpu_custom_call" | custom-call | tf_op jit(solution)/shard_map/first_columns/pallas_call | solution.py:386
  26.9 2.1 %collective-permute-done.6.part_ref = bf16[128,512]{1,0:T(8,128)(2,1)S(1)} collective-permute-done((bf16[128,512]{1,0:T(8,128)(2,1)S(1)}, bf16[128,512]{1,0:T(8,128)(2,1)S(1)}, u32[]{:S(2)}, u32[]{:S(2)}) %collective-permute-start.6) | collective-permute-done | bytes 131104 | tf_op jit(solution)/shard_map/ppermute | solution.py:384
  29.1 0.7 %other_columns.2._ = bf16[128,1536]{1,0:T(8,128)(2,1)} custom-call(bf16[128,1536]{1,0:T(8,128)(2,1)} %first_columns.1._, bf16[128,512]{1,0:T(8,128)(2,1)S(1)} %collective-permute-done.6.part_ref), custom_call_target="tpu_custom_call", output_to_operand_aliasing={{}: (0, {})} | custom-call | tf_op jit(solution)/shard_map/other_columns/pallas_call | solution.py:396
  29.7 0.6 %collective-permute-done.7.part_ref = bf16[128,384]{1,0:T(8,128)(2,1)S(1)} collective-permute-done((bf16[128,384]{1,0:T(8,128)(2,1)S(1)}, bf16[128,384]{1,0:T(8,128)(2,1)S(1)}, u32[]{:S(2)}, u32[]{:S(2)}) %collective-permute-start.7) | collective-permute-done | bytes 98336 | tf_op jit(solution)/shard_map/ppermute | solution.py:384
  30.4 0.6 %other_columns.3 = bf16[128,1536]{1,0:T(8,128)(2,1)} custom-call(bf16[128,1536]{1,0:T(8,128)(2,1)} %other_columns.2._, bf16[128,384]{1,0:T(8,128)(2,1)S(1)} %collective-permute-done.7.part_ref), custom_call_target="tpu_custom_call", output_to_operand_aliasing={{}: (0, {})} | custom-call | tf_op jit(solution)/shard_map/other_columns/pallas_call | solution.py:396
Async XLA Ops:
  0.0 12.6 %collective-permute-start.1 = (bf16[128,1536]{1,0:T(8,128)(2,1)}, bf16[128,1536]{1,0:T(8,128)(2,1)S(1)}, u32[]{:S(2)}, u32[]{:S(2)}) collective-permute-start(bf16[128,1536]{1,0:T(8,128)(2,1)} %bitcast.13), channel_id=1, source_target_pairs={{0,2},{2,0},{4,6},{6,4},{1,3},{3,1},{5,7},{7,5},{8,10},{10,8},{12,... | collective-permute-start | bytes 1179656 | tf_op jit(solution)/shard_map/ppermute | solution.py:276
  3.9 7.5 %collective-permute-start.2 = (bf16[80,1536]{1,0:T(8,128)(2,1)S(1)}, bf16[80,1536]{1,0:T(8,128)(2,1)S(1)}, u32[]{:S(2)}, u32[]{:S(2)}) collective-permute-start(bf16[80,1536]{1,0:T(8,128)(2,1)S(1)} %slice.4), channel_id=1, source_target_pairs={{4,0},{6,2},{0,4},{2,6},{5,1},{7,3},{1,5},{3,7},{12,8},{14,10},{8,... | collective-permute-start | bytes 737288 | tf_op jit(solution)/shard_map/ppermute | solution.py:279
  5.5 8.2 %collective-permute-start = (s32[2,6]{1,0:T(2,128)}, s32[2,6]{1,0:T(2,128)S(1)}, u32[]{:S(2)}, u32[]{:S(2)}) collective-permute-start(s32[2,6]{1,0:T(2,128)} %bitcast.17), channel_id=1, source_target_pairs={{0,2},{2,0},{4,6},{6,4},{1,3},{3,1},{5,7},{7,5},{8,10},{10,8},{12,... | collective-permute-start | bytes 152 | tf_op jit(solution)/shard_map/ppermute | solution.py:276
  10.1 5.2 %collective-permute-start.3 = (bf16[48,1536]{1,0:T(8,128)(2,1)S(1)}, bf16[48,1536]{1,0:T(8,128)(2,1)S(1)}, u32[]{:S(2)}, u32[]{:S(2)}) collective-permute-start(bf16[48,1536]{1,0:T(8,128)(2,1)S(1)} %get-tuple-element.30), channel_id=1, source_target_pairs={{4,0},{6,2},{0,4},{2,6},{5,1},{7,3},{1,5},{3,7},{12,8},{14,10},{8,... | collective-permute-start | bytes 442376 | tf_op jit(solution)/shard_map/ppermute | solution.py:279
  11.4 2.3 %copy-start = (bf16[1,768,1536]{2,1,0:T(8,128)(2,1)S(1)}, bf16[1,768,1536]{2,1,0:T(8,128)(2,1)}, u32[]{:S(2)}) copy-start(bf16[1,768,1536]{2,1,0:T(8,128)(2,1)} %param.8) | copy-start | bytes 7077892
  13.6 1.8 %collective-permute-start.4 = (bf16[128,1536]{1,0:T(8,128)(2,1)S(1)}, bf16[128,1536]{1,0:T(8,128)(2,1)S(1)}, u32[]{:S(2)}, u32[]{:S(2)}) collective-permute-start(bf16[128,1536]{1,0:T(8,128)(2,1)S(1)} %get-tuple-element.25.refs_0_), channel_id=1, source_target_pairs={{0,1},{1,0},{2,3},{3,2},{4,5},{5,4},{6,7},{7,6},{8,9},{9,8},{10,11... | collective-permute-start | bytes 1179656 | tf_op jit(solution)/shard_map/ppermute | solution.py:333
  16.5 9.8 %collective-permute-start.5 = (bf16[128,640]{1,0:T(8,128)(2,1)S(1)}, bf16[128,640]{1,0:T(8,128)(2,1)S(1)}, u32[]{:S(2)}, u32[]{:S(2)}) collective-permute-start(bf16[128,640]{1,0:T(8,128)(2,1)S(1)} %get-tuple-element.31), channel_id=1, source_target_pairs={{0,10},{2,8},{4,14},{6,12},{8,18},{10,16},{12,22},{14,20},{16,26},... | collective-permute-start | bytes 491528 | tf_op jit(solution)/shard_map/ppermute | solution.py:384
  19.1 10.0 %collective-permute-start.6 = (bf16[128,512]{1,0:T(8,128)(2,1)S(1)}, bf16[128,512]{1,0:T(8,128)(2,1)S(1)}, u32[]{:S(2)}, u32[]{:S(2)}) collective-permute-start(bf16[128,512]{1,0:T(8,128)(2,1)S(1)} %finish_rest.2), channel_id=1, source_target_pairs={{0,10},{2,8},{4,14},{6,12},{8,18},{10,16},{12,22},{14,20},{16,26},... | collective-permute-start | bytes 393224 | tf_op jit(solution)/shard_map/ppermute | solution.py:384
  21.2 9.1 %collective-permute-start.7 = (bf16[128,384]{1,0:T(8,128)(2,1)S(1)}, bf16[128,384]{1,0:T(8,128)(2,1)S(1)}, u32[]{:S(2)}, u32[]{:S(2)}) collective-permute-start(bf16[128,384]{1,0:T(8,128)(2,1)S(1)} %finish_rest.3), channel_id=1, source_target_pairs={{0,10},{2,8},{4,14},{6,12},{8,18},{10,16},{12,22},{14,20},{16,26},... | collective-permute-start | bytes 294920 | tf_op jit(solution)/shard_map/ppermute | solution.py:384

commit v9 on v8

--- a/solution.py
+++ b/solution.py
@@ -279,7 +279,7 @@
         return lax.ppermute(x, "frame", beyond_perm(frames))
 
     tokens = from_partner(own)
-    lists = from_partner(tile_lists[0, 0])
+
     far = frames > 2
     sent = own_count * RAW // 8
     beyond = [from_beyond(own[:sent])] if far else []
@@ -309,6 +309,7 @@
         )[0]
         for b in beyond
     ]
+    lists = from_partner(after(tile_lists[0, 0], kv_own))
     near_tiles = 2 + far
 
     def slots_of():

time: 31.2 us -> 31.2 us (level)
  no operation moved by 1% of the time
where the time goes in v9:
time: 31.2 us; the launch traced here: 31 us
  starting transfers between devices  11.7 us (38%)
  Pallas kernels  10.4 us (33%)
  waiting for transfers between devices  7.11 us (23%)
  local copies, waits for them, and re-layouts  1 us (3%)
  between operations  0.76 us (2%)
    pallas_call x7, Pallas kernels, call(): pl.pallas_call(kernel, out_shape=outs, in_specs=ins, out_specs=[VMEM] * l...  8.43 us
    ppermute x3, starting transfers between devices, body(): handed = [lax.ppermute(x, ('segment', 'frame'), onward) for x in finished]  6.5 us
    ppermute x3, waiting for transfers between devices, body(): handed = [lax.ppermute(x, ('segment', 'frame'), onward) for x in finished]  5.46 us
    ppermute x2, starting transfers between devices, from_partner(): return lax.ppermute(x, 'frame', swap_perm(frames))  3.54 us
    ppermute x2, starting transfers between devices, from_beyond(): return lax.ppermute(x, 'frame', beyond_perm(frames))  1.63 us
    ppermute x2, waiting for transfers between devices, from_beyond(): return lax.ppermute(x, 'frame', beyond_perm(frames))  1.55 us
    pallas_call x2, Pallas kernels, body(): pl.pallas_call(functools.partial(rest_kernel, start), out_shape=result, i...  1.31 us
    slice x1, local copies, waits for them, and re-layouts, body(): beyond = [from_beyond(own[:sent])] if far else []  0.99 us
  transfers between devices with their start and end apart: 8, of which 6 were waited for; matrix products, arithmetic and copies ran while one was open for 3% of the time, Pallas kernels for 28%

profile of v9, /device:TPU:0, one launch (start us, length us, event | category | flops | bytes accessed | tf_op | source)
XLA Modules:
  0.0 31.0 jit_solution(13609347719508330455)
XLA Ops:
  0.0 0.0 copy-start.1
  0.0 2.9 %collective-permute-start.1 = (bf16[128,1536]{1,0:T(8,128)(2,1)}, bf16[128,1536]{1,0:T(8,128)(2,1)S(1)}, u32[]{:S(2)}, u32[]{:S(2)}) collective-permute-start(bf16[128,1536]{1,0:T(8,128)(2,1)} %bitcast.13), channel_id=1, source_target_pairs={{0,2},{2,0},{4,6},{6,4},{1,3},{3,1},{5,7},{7,5},{8,10},{10,8},{12,... | collective-permute-start | bytes 1179656 | tf_op jit(solution)/shard_map/ppermute | solution.py:276
  2.9 1.0 %slice.4 = bf16[80,1536]{1,0:T(8,128)(2,1)S(1)} slice(bf16[128,1536]{1,0:T(8,128)(2,1)} %bitcast.14), slice={[0:80], [0:1536]} | slice | bytes 491520 | tf_op jit(solution)/shard_map/slice | solution.py:285
  3.9 1.6 %collective-permute-start.2 = (bf16[80,1536]{1,0:T(8,128)(2,1)S(1)}, bf16[80,1536]{1,0:T(8,128)(2,1)S(1)}, u32[]{:S(2)}, u32[]{:S(2)}) collective-permute-start(bf16[80,1536]{1,0:T(8,128)(2,1)S(1)} %slice.4), channel_id=1, source_target_pairs={{4,0},{6,2},{0,4},{2,6},{5,1},{7,3},{1,5},{3,7},{12,8},{14,10},{8,... | collective-permute-start | bytes 737288 | tf_op jit(solution)/shard_map/ppermute | solution.py:279
  6.2 3.4 %own_pairs.1 = (f32[3,1536]{1,0:T(4,128)S(1)}, bf16[1536,768]{1,0:T(8,128)(2,1)S(1)}, bf16[1536,1536]{1,0:T(8,128)(2,1)S(1)}, bf16[128,1536]{1,0:T(8,128)(2,1)S(1)}, bf16[48,1536]{1,0:T(8,128)(2,1)S(1)}) custom-call(s32[1]{0:T(128)S(6)} %copy.11.domain_hbm, bf16[3,8,1536]{2,1,0:T(8,128)(2,1)} %bitcast.16, bf16[1536,2304]{1,0:T(8,128)(2,1)} %bitcast.12, ...), custom_call_target="tpu_custom_call" | custom-call | flops 1 | tf_op jit(solution)/shard_map/own_pairs/pallas_call | solution.py:249
  9.6 0.0 copy-done.1
  9.6 0.6 %collective-permute-start = (s32[2,6]{1,0:T(2,128)S(1)}, s32[2,6]{1,0:T(2,128)S(1)}, u32[]{:S(2)}, u32[]{:S(2)}) collective-permute-start(s32[2,6]{1,0:T(2,128)S(1)} %bitcast.17), channel_id=1, source_target_pairs={{0,2},{2,0},{4,6},{6,4},{1,3},{3,1},{5,7},{7,5},{8,10},{10,8},{12,... | collective-permute-start | bytes 152 | tf_op jit(solution)/shard_map/ppermute | solution.py:276
  10.2 0.1 collective-permute-start.3
  10.2 1.2 %collective-permute-done.2.rows_ref = bf16[80,1536]{1,0:T(8,128)(2,1)S(1)} collective-permute-done((bf16[80,1536]{1,0:T(8,128)(2,1)S(1)}, bf16[80,1536]{1,0:T(8,128)(2,1)S(1)}, u32[]{:S(2)}, u32[]{:S(2)}) %collective-permute-start.2) | collective-permute-done | bytes 245792 | tf_op jit(solution)/shard_map/ppermute | solution.py:279
  11.4 0.0 copy-start
  11.4 1.1 %beyond_pairs.1.refs_0_ = bf16[80,1536]{1,0:T(8,128)(2,1)S(1)} custom-call(f32[3,1536]{1,0:T(4,128)S(1)} %get-tuple-element.22.modulate_ref, bf16[1536,1536]{1,0:T(8,128)(2,1)S(1)} %get-tuple-element.23.weight_ref, bf16[80,1536]{1,0:T(8,128)(2,1)S(1)} %collective-permute-done.2.rows_ref), custom_call_target="tpu_custom_call" | custom-call | flops 1 | tf_op jit(solution)/shard_map/beyond_pairs/pallas_call | solution.py:249
  12.6 0.0 collective-permute-done.1.rows_ref
  12.6 1.0 %pairs.1 = (bf16[128,1536]{1,0:T(8,128)(2,1)S(1)}, bf16[128,1536]{1,0:T(8,128)(2,1)S(1)}) custom-call(f32[3,1536]{1,0:T(4,128)S(1)} %get-tuple-element.22.modulate_ref, bf16[1536,1536]{1,0:T(8,128)(2,1)S(1)} %get-tuple-element.23.weight_ref, bf16[128,1536]{1,0:T(8,128)(2,1)S(1)} %collective-permute-done.1.rows_ref), custom_call_target="tpu_custom_call" | custom-call | flops 1 | tf_op jit(solution)/shard_map/pairs/pallas_call | solution.py:249
  13.6 0.1 collective-permute-start.4
  13.7 0.0 collective-permute-done.lists_ref
  13.7 0.0 copy-done
  13.7 1.2 %near_attention.1 = (bf16[128,768]{1,0:T(8,128)(2,1)S(1)}, f32[6,128]{1,0:T(8,128)S(1)}, f32[6,128]{1,0:T(8,128)S(1)}, f32[768,128]{1,0:T(8,128)S(1)}) custom-call(s32[2,6]{1,0:T(2,128)S(1)} %collective-permute-done.lists_ref, bf16[1536,768]{1,0:T(8,128)(2,1)S(1)} %get-tuple-element.25.q_weight_ref, bf16[768,1536]{1,0:T(8,128)(2,1)S(1)} %bitcast.8, ...), custom_call_target="tpu_custom_call" | custom-call | flops 10000000000 | tf_op jit(solution)/shard_map/near_attention/pallas_call | solution.py:249
  15.0 0.4 %collective-permute-done.3.refs_1_ = bf16[48,1536]{1,0:T(8,128)(2,1)S(1)} collective-permute-done((bf16[48,1536]{1,0:T(8,128)(2,1)S(1)}, bf16[48,1536]{1,0:T(8,128)(2,1)S(1)}, u32[]{:S(2)}, u32[]{:S(2)}) %collective-permute-start.3) | collective-permute-done | bytes 147488 | tf_op jit(solution)/shard_map/ppermute | solution.py:279
  15.3 0.1 collective-permute-done.4.refs_2_
  15.4 1.0 %finish.1 = (bf16[768,128]{1,0:T(8,128)(2,1)S(1)}, bf16[128,640]{1,0:T(8,128)(2,1)S(1)}) custom-call(s32[2,6]{1,0:T(2,128)S(1)} %collective-permute-done.lists_ref, f32[3,1536]{1,0:T(4,128)S(1)} %get-tuple-element.22.modulate_ref, bf16[768,1536]{1,0:T(8,128)(2,1)S(1)} %bitcast.9, bf16[128,1536]{1,0:T(8,128)(2,1)S(1)} %collective-permute-done.1.rows_ref, ...), custom_call_target="tpu_custom_call" | custom-call | flops 1 | tf_op jit(solution)/shard_map/finish/pallas_call | solution.py:249
  16.5 2.4 %collective-permute-start.5 = (bf16[128,640]{1,0:T(8,128)(2,1)S(1)}, bf16[128,640]{1,0:T(8,128)(2,1)S(1)}, u32[]{:S(2)}, u32[]{:S(2)}) collective-permute-start(bf16[128,640]{1,0:T(8,128)(2,1)S(1)} %get-tuple-element.33), channel_id=1, source_target_pairs={{0,10},{2,8},{4,14},{6,12},{8,18},{10,16},{12,22},{14,20},{16,26},... | collective-permute-start | bytes 491528 | tf_op jit(solution)/shard_map/ppermute | solution.py:385
  18.8 0.3 finish_rest.2
  19.1 1.8 %collective-permute-start.6 = (bf16[128,512]{1,0:T(8,128)(2,1)S(1)}, bf16[128,512]{1,0:T(8,128)(2,1)S(1)}, u32[]{:S(2)}, u32[]{:S(2)}) collective-permute-start(bf16[128,512]{1,0:T(8,128)(2,1)S(1)} %finish_rest.2), channel_id=1, source_target_pairs={{0,10},{2,8},{4,14},{6,12},{8,18},{10,16},{12,22},{14,20},{16,26},... | collective-permute-start | bytes 393224 | tf_op jit(solution)/shard_map/ppermute | solution.py:385
  20.9 0.3 finish_rest.3
  21.2 2.3 %collective-permute-start.7 = (bf16[128,384]{1,0:T(8,128)(2,1)S(1)}, bf16[128,384]{1,0:T(8,128)(2,1)S(1)}, u32[]{:S(2)}, u32[]{:S(2)}) collective-permute-start(bf16[128,384]{1,0:T(8,128)(2,1)S(1)} %finish_rest.3), channel_id=1, source_target_pairs={{0,10},{2,8},{4,14},{6,12},{8,18},{10,16},{12,22},{14,20},{16,26},... | collective-permute-start | bytes 294920 | tf_op jit(solution)/shard_map/ppermute | solution.py:385
  23.6 2.7 %collective-permute-done.5.part_ref = bf16[128,640]{1,0:T(8,128)(2,1)S(1)} collective-permute-done((bf16[128,640]{1,0:T(8,128)(2,1)S(1)}, bf16[128,640]{1,0:T(8,128)(2,1)S(1)}, u32[]{:S(2)}, u32[]{:S(2)}) %collective-permute-start.5) | collective-permute-done | bytes 163872 | tf_op jit(solution)/shard_map/ppermute | solution.py:385
  26.3 0.7 %first_columns.1._ = bf16[128,1536]{1,0:T(8,128)(2,1)} custom-call(bf16[128,640]{1,0:T(8,128)(2,1)S(1)} %collective-permute-done.5.part_ref), custom_call_target="tpu_custom_call" | custom-call | tf_op jit(solution)/shard_map/first_columns/pallas_call | solution.py:387
  26.9 2.1 %collective-permute-done.6.part_ref = bf16[128,512]{1,0:T(8,128)(2,1)S(1)} collective-permute-done((bf16[128,512]{1,0:T(8,128)(2,1)S(1)}, bf16[128,512]{1,0:T(8,128)(2,1)S(1)}, u32[]{:S(2)}, u32[]{:S(2)}) %collective-permute-start.6) | collective-permute-done | bytes 131104 | tf_op jit(solution)/shard_map/ppermute | solution.py:385
  29.1 0.7 %other_columns.2._ = bf16[128,1536]{1,0:T(8,128)(2,1)} custom-call(bf16[128,1536]{1,0:T(8,128)(2,1)} %first_columns.1._, bf16[128,512]{1,0:T(8,128)(2,1)S(1)} %collective-permute-done.6.part_ref), custom_call_target="tpu_custom_call", output_to_operand_aliasing={{}: (0, {})} | custom-call | tf_op jit(solution)/shard_map/other_columns/pallas_call | solution.py:397
  29.7 0.6 %collective-permute-done.7.part_ref = bf16[128,384]{1,0:T(8,128)(2,1)S(1)} collective-permute-done((bf16[128,384]{1,0:T(8,128)(2,1)S(1)}, bf16[128,384]{1,0:T(8,128)(2,1)S(1)}, u32[]{:S(2)}, u32[]{:S(2)}) %collective-permute-start.7) | collective-permute-done | bytes 98336 | tf_op jit(solution)/shard_map/ppermute | solution.py:385
  30.4 0.6 %other_columns.3 = bf16[128,1536]{1,0:T(8,128)(2,1)} custom-call(bf16[128,1536]{1,0:T(8,128)(2,1)} %other_columns.2._, bf16[128,384]{1,0:T(8,128)(2,1)S(1)} %collective-permute-done.7.part_ref), custom_call_target="tpu_custom_call", output_to_operand_aliasing={{}: (0, {})} | custom-call | tf_op jit(solution)/shard_map/other_columns/pallas_call | solution.py:397
Async XLA Ops:
  0.0 9.6 %copy-start.1 = (s32[1,1,2,6]{3,2,1,0:T(2,128)S(1)}, s32[1,1,2,6]{3,2,1,0:T(2,128)}, u32[]{:S(2)}) copy-start(s32[1,1,2,6]{3,2,1,0:T(2,128)} %param.11) | copy-start | bytes 148
  0.0 12.6 %collective-permute-start.1 = (bf16[128,1536]{1,0:T(8,128)(2,1)}, bf16[128,1536]{1,0:T(8,128)(2,1)S(1)}, u32[]{:S(2)}, u32[]{:S(2)}) collective-permute-start(bf16[128,1536]{1,0:T(8,128)(2,1)} %bitcast.13), channel_id=1, source_target_pairs={{0,2},{2,0},{4,6},{6,4},{1,3},{3,1},{5,7},{7,5},{8,10},{10,8},{12,... | collective-permute-start | bytes 1179656 | tf_op jit(solution)/shard_map/ppermute | solution.py:276
  3.9 7.5 %collective-permute-start.2 = (bf16[80,1536]{1,0:T(8,128)(2,1)S(1)}, bf16[80,1536]{1,0:T(8,128)(2,1)S(1)}, u32[]{:S(2)}, u32[]{:S(2)}) collective-permute-start(bf16[80,1536]{1,0:T(8,128)(2,1)S(1)} %slice.4), channel_id=1, source_target_pairs={{4,0},{6,2},{0,4},{2,6},{5,1},{7,3},{1,5},{3,7},{12,8},{14,10},{8,... | collective-permute-start | bytes 737288 | tf_op jit(solution)/shard_map/ppermute | solution.py:279
  9.6 4.1 %collective-permute-start = (s32[2,6]{1,0:T(2,128)S(1)}, s32[2,6]{1,0:T(2,128)S(1)}, u32[]{:S(2)}, u32[]{:S(2)}) collective-permute-start(s32[2,6]{1,0:T(2,128)S(1)} %bitcast.17), channel_id=1, source_target_pairs={{0,2},{2,0},{4,6},{6,4},{1,3},{3,1},{5,7},{7,5},{8,10},{10,8},{12,... | collective-permute-start | bytes 152 | tf_op jit(solution)/shard_map/ppermute | solution.py:276
  10.2 5.1 %collective-permute-start.3 = (bf16[48,1536]{1,0:T(8,128)(2,1)S(1)}, bf16[48,1536]{1,0:T(8,128)(2,1)S(1)}, u32[]{:S(2)}, u32[]{:S(2)}) collective-permute-start(bf16[48,1536]{1,0:T(8,128)(2,1)S(1)} %get-tuple-element.32), channel_id=1, source_target_pairs={{4,0},{6,2},{0,4},{2,6},{5,1},{7,3},{1,5},{3,7},{12,8},{14,10},{8,... | collective-permute-start | bytes 442376 | tf_op jit(solution)/shard_map/ppermute | solution.py:279
  11.4 2.3 %copy-start = (bf16[1,768,1536]{2,1,0:T(8,128)(2,1)S(1)}, bf16[1,768,1536]{2,1,0:T(8,128)(2,1)}, u32[]{:S(2)}) copy-start(bf16[1,768,1536]{2,1,0:T(8,128)(2,1)} %param.8) | copy-start | bytes 7077892
  13.6 1.8 %collective-permute-start.4 = (bf16[128,1536]{1,0:T(8,128)(2,1)S(1)}, bf16[128,1536]{1,0:T(8,128)(2,1)S(1)}, u32[]{:S(2)}, u32[]{:S(2)}) collective-permute-start(bf16[128,1536]{1,0:T(8,128)(2,1)S(1)} %get-tuple-element.27.refs_0_), channel_id=1, source_target_pairs={{0,1},{1,0},{2,3},{3,2},{4,5},{5,4},{6,7},{7,6},{8,9},{9,8},{10,11... | collective-permute-start | bytes 1179656 | tf_op jit(solution)/shard_map/ppermute | solution.py:334
  16.5 9.8 %collective-permute-start.5 = (bf16[128,640]{1,0:T(8,128)(2,1)S(1)}, bf16[128,640]{1,0:T(8,128)(2,1)S(1)}, u32[]{:S(2)}, u32[]{:S(2)}) collective-permute-start(bf16[128,640]{1,0:T(8,128)(2,1)S(1)} %get-tuple-element.33), channel_id=1, source_target_pairs={{0,10},{2,8},{4,14},{6,12},{8,18},{10,16},{12,22},{14,20},{16,26},... | collective-permute-start | bytes 491528 | tf_op jit(solution)/shard_map/ppermute | solution.py:385
  19.1 9.9 %collective-permute-start.6 = (bf16[128,512]{1,0:T(8,128)(2,1)S(1)}, bf16[128,512]{1,0:T(8,128)(2,1)S(1)}, u32[]{:S(2)}, u32[]{:S(2)}) collective-permute-start(bf16[128,512]{1,0:T(8,128)(2,1)S(1)} %finish_rest.2), channel_id=1, source_target_pairs={{0,10},{2,8},{4,14},{6,12},{8,18},{10,16},{12,22},{14,20},{16,26},... | collective-permute-start | bytes 393224 | tf_op jit(solution)/shard_map/ppermute | solution.py:385
  21.2 9.2 %collective-permute-start.7 = (bf16[128,384]{1,0:T(8,128)(2,1)S(1)}, bf16[128,384]{1,0:T(8,128)(2,1)S(1)}, u32[]{:S(2)}, u32[]{:S(2)}) collective-permute-start(bf16[128,384]{1,0:T(8,128)(2,1)S(1)} %finish_rest.3), channel_id=1, source_target_pairs={{0,10},{2,8},{4,14},{6,12},{8,18},{10,16},{12,22},{14,20},{16,26},... | collective-permute-start | bytes 294920 | tf_op jit(solution)/shard_map/ppermute | solution.py:385

commit v10 on v8

--- a/solution.py
+++ b/solution.py
@@ -12,7 +12,7 @@
 MASKED = -1e30
 RAW = 5
 LOADS = 4
-PARTS = (5, 4, 3)
+PARTS = (6, 4, 2)
 F32 = jnp.float32
 BF16 = jnp.bfloat16
 VMEM = pl.BlockSpec(memory_space=pltpu.VMEM)

time: 31.2 us -> 31.2 us (level)
  transfers between devices with their start and end apart: 8 -> 8, of which waited for: 6 -> 5; matrix products, arithmetic and copies ran while one was open for 3% -> 3% of each run, Pallas kernels for 28% -> 28%
where the time goes in v10:
time: 31.2 us; the launch traced here: 31 us
  starting transfers between devices  11.8 us (38%)
  Pallas kernels  10.4 us (33%)
  waiting for transfers between devices  7.12 us (23%)
  local copies, waits for them, and re-layouts  1 us (3%)
  between operations  0.75 us (2%)
    pallas_call x7, Pallas kernels, call(): pl.pallas_call(kernel, out_shape=outs, in_specs=ins, out_specs=[VMEM] * l...  8.4 us
    ppermute x3, starting transfers between devices, body(): handed = [lax.ppermute(x, ('segment', 'frame'), onward) for x in finished]  6.49 us
    ppermute x3, waiting for transfers between devices, body(): handed = [lax.ppermute(x, ('segment', 'frame'), onward) for x in finished]  5.48 us
    ppermute x2, starting transfers between devices, from_partner(): return lax.ppermute(x, 'frame', swap_perm(frames))  3.47 us
    ppermute x2, starting transfers between devices, from_beyond(): return lax.ppermute(x, 'frame', beyond_perm(frames))  1.73 us
    ppermute x2, waiting for transfers between devices, from_beyond(): return lax.ppermute(x, 'frame', beyond_perm(frames))  1.52 us
    pallas_call x2, Pallas kernels, body(): pl.pallas_call(functools.partial(rest_kernel, start), out_shape=result, i...  1.3 us
    slice x1, local copies, waits for them, and re-layouts, body(): beyond = [from_beyond(own[:sent])] if far else []  0.99 us
  transfers between devices with their start and end apart: 8, of which 5 were waited for; matrix products, arithmetic and copies ran while one was open for 3% of the time, Pallas kernels for 28%

profile of v10, /device:TPU:0, one launch (start us, length us, event | category | flops | bytes accessed | tf_op | source)
XLA Modules:
  0.0 31.0 jit_solution(18078328812616115323)
XLA Ops:
  0.0 2.9 %collective-permute-start.1 = (bf16[128,1536]{1,0:T(8,128)(2,1)}, bf16[128,1536]{1,0:T(8,128)(2,1)S(1)}, u32[]{:S(2)}, u32[]{:S(2)}) collective-permute-start(bf16[128,1536]{1,0:T(8,128)(2,1)} %bitcast.13), channel_id=1, source_target_pairs={{0,2},{2,0},{4,6},{6,4},{1,3},{3,1},{5,7},{7,5},{8,10},{10,8},{12,... | collective-permute-start | bytes 1179656 | tf_op jit(solution)/shard_map/ppermute | solution.py:276
  2.9 1.0 %slice.4 = bf16[80,1536]{1,0:T(8,128)(2,1)S(1)} slice(bf16[128,1536]{1,0:T(8,128)(2,1)} %bitcast.14), slice={[0:80], [0:1536]} | slice | bytes 491520 | tf_op jit(solution)/shard_map/slice | solution.py:285
  3.9 1.6 %collective-permute-start.2 = (bf16[80,1536]{1,0:T(8,128)(2,1)S(1)}, bf16[80,1536]{1,0:T(8,128)(2,1)S(1)}, u32[]{:S(2)}, u32[]{:S(2)}) collective-permute-start(bf16[80,1536]{1,0:T(8,128)(2,1)S(1)} %slice.4), channel_id=1, source_target_pairs={{4,0},{6,2},{0,4},{2,6},{5,1},{7,3},{1,5},{3,7},{12,8},{14,10},{8,... | collective-permute-start | bytes 737288 | tf_op jit(solution)/shard_map/ppermute | solution.py:279
  5.5 0.5 %collective-permute-start = (s32[2,6]{1,0:T(2,128)}, s32[2,6]{1,0:T(2,128)S(1)}, u32[]{:S(2)}, u32[]{:S(2)}) collective-permute-start(s32[2,6]{1,0:T(2,128)} %bitcast.17), channel_id=1, source_target_pairs={{0,2},{2,0},{4,6},{6,4},{1,3},{3,1},{5,7},{7,5},{8,10},{10,8},{12,... | collective-permute-start | bytes 152 | tf_op jit(solution)/shard_map/ppermute | solution.py:276
  6.7 3.4 %own_pairs.1 = (f32[3,1536]{1,0:T(4,128)S(1)}, bf16[1536,768]{1,0:T(8,128)(2,1)S(1)}, bf16[1536,1536]{1,0:T(8,128)(2,1)S(1)}, bf16[128,1536]{1,0:T(8,128)(2,1)S(1)}, bf16[48,1536]{1,0:T(8,128)(2,1)S(1)}) custom-call(s32[1]{0:T(128)S(6)} %copy.11.domain_hbm, bf16[3,8,1536]{2,1,0:T(8,128)(2,1)} %bitcast.16, bf16[1536,2304]{1,0:T(8,128)(2,1)} %bitcast.12, ...), custom_call_target="tpu_custom_call" | custom-call | flops 1 | tf_op jit(solution)/shard_map/own_pairs/pallas_call | solution.py:249
  10.1 0.1 collective-permute-start.3
  10.2 1.2 %collective-permute-done.2.rows_ref = bf16[80,1536]{1,0:T(8,128)(2,1)S(1)} collective-permute-done((bf16[80,1536]{1,0:T(8,128)(2,1)S(1)}, bf16[80,1536]{1,0:T(8,128)(2,1)S(1)}, u32[]{:S(2)}, u32[]{:S(2)}) %collective-permute-start.2) | collective-permute-done | bytes 245792 | tf_op jit(solution)/shard_map/ppermute | solution.py:279
  11.4 0.0 copy-start
  11.4 1.1 %beyond_pairs.1.refs_0_ = bf16[80,1536]{1,0:T(8,128)(2,1)S(1)} custom-call(f32[3,1536]{1,0:T(4,128)S(1)} %get-tuple-element.19.modulate_ref, bf16[1536,1536]{1,0:T(8,128)(2,1)S(1)} %get-tuple-element.21.weight_ref, bf16[80,1536]{1,0:T(8,128)(2,1)S(1)} %collective-permute-done.2.rows_ref), custom_call_target="tpu_custom_call" | custom-call | flops 1 | tf_op jit(solution)/shard_map/beyond_pairs/pallas_call | solution.py:249
  12.6 0.0 collective-permute-done.1.rows_ref
  12.6 1.0 %pairs.1 = (bf16[128,1536]{1,0:T(8,128)(2,1)S(1)}, bf16[128,1536]{1,0:T(8,128)(2,1)S(1)}) custom-call(f32[3,1536]{1,0:T(4,128)S(1)} %get-tuple-element.19.modulate_ref, bf16[1536,1536]{1,0:T(8,128)(2,1)S(1)} %get-tuple-element.21.weight_ref, bf16[128,1536]{1,0:T(8,128)(2,1)S(1)} %collective-permute-done.1.rows_ref), custom_call_target="tpu_custom_call" | custom-call | flops 1 | tf_op jit(solution)/shard_map/pairs/pallas_call | solution.py:249
  13.6 0.1 collective-permute-start.4
  13.7 0.0 collective-permute-done.lists_ref
  13.7 0.0 copy-done
  13.7 1.2 %near_attention.1 = (bf16[128,768]{1,0:T(8,128)(2,1)S(1)}, f32[6,128]{1,0:T(8,128)S(1)}, f32[6,128]{1,0:T(8,128)S(1)}, f32[768,128]{1,0:T(8,128)S(1)}) custom-call(s32[2,6]{1,0:T(2,128)S(1)} %collective-permute-done.lists_ref, bf16[1536,768]{1,0:T(8,128)(2,1)S(1)} %get-tuple-element.23.q_weight_ref, bf16[768,1536]{1,0:T(8,128)(2,1)S(1)} %bitcast.8, ...), custom_call_target="tpu_custom_call" | custom-call | flops 10000000000 | tf_op jit(solution)/shard_map/near_attention/pallas_call | solution.py:249
  15.0 0.3 %collective-permute-done.3.refs_1_ = bf16[48,1536]{1,0:T(8,128)(2,1)S(1)} collective-permute-done((bf16[48,1536]{1,0:T(8,128)(2,1)S(1)}, bf16[48,1536]{1,0:T(8,128)(2,1)S(1)}, u32[]{:S(2)}, u32[]{:S(2)}) %collective-permute-start.3) | collective-permute-done | bytes 147488 | tf_op jit(solution)/shard_map/ppermute | solution.py:279
  15.3 0.1 collective-permute-done.4.refs_2_
  15.4 1.0 %finish.1 = (bf16[768,128]{1,0:T(8,128)(2,1)S(1)}, bf16[128,768]{1,0:T(8,128)(2,1)S(1)}) custom-call(s32[2,6]{1,0:T(2,128)S(1)} %collective-permute-done.lists_ref, f32[3,1536]{1,0:T(4,128)S(1)} %get-tuple-element.19.modulate_ref, bf16[768,1536]{1,0:T(8,128)(2,1)S(1)} %bitcast.9, bf16[128,1536]{1,0:T(8,128)(2,1)S(1)} %collective-permute-done.1.rows_ref, ...), custom_call_target="tpu_custom_call" | custom-call | flops 1 | tf_op jit(solution)/shard_map/finish/pallas_call | solution.py:249
  16.5 2.3 %collective-permute-start.5 = (bf16[128,768]{1,0:T(8,128)(2,1)S(1)}, bf16[128,768]{1,0:T(8,128)(2,1)S(1)}, u32[]{:S(2)}, u32[]{:S(2)}) collective-permute-start(bf16[128,768]{1,0:T(8,128)(2,1)S(1)} %get-tuple-element.31), channel_id=1, source_target_pairs={{0,10},{2,8},{4,14},{6,12},{8,18},{10,16},{12,22},{14,20},{16,26},... | collective-permute-start | bytes 589832 | tf_op jit(solution)/shard_map/ppermute | solution.py:384
  18.8 0.3 finish_rest.2
  19.1 1.8 %collective-permute-start.6 = (bf16[128,512]{1,0:T(8,128)(2,1)S(1)}, bf16[128,512]{1,0:T(8,128)(2,1)S(1)}, u32[]{:S(2)}, u32[]{:S(2)}) collective-permute-start(bf16[128,512]{1,0:T(8,128)(2,1)S(1)} %finish_rest.2), channel_id=1, source_target_pairs={{0,10},{2,8},{4,14},{6,12},{8,18},{10,16},{12,22},{14,20},{16,26},... | collective-permute-start | bytes 393224 | tf_op jit(solution)/shard_map/ppermute | solution.py:384
  20.9 0.3 finish_rest.3
  21.2 2.3 %collective-permute-start.7 = (bf16[128,256]{1,0:T(8,128)(2,1)S(1)}, bf16[128,256]{1,0:T(8,128)(2,1)S(1)}, u32[]{:S(2)}, u32[]{:S(2)}) collective-permute-start(bf16[128,256]{1,0:T(8,128)(2,1)S(1)} %finish_rest.3), channel_id=1, source_target_pairs={{0,10},{2,8},{4,14},{6,12},{8,18},{10,16},{12,22},{14,20},{16,26},... | collective-permute-start | bytes 196616 | tf_op jit(solution)/shard_map/ppermute | solution.py:384
  23.5 3.5 %collective-permute-done.5.part_ref = bf16[128,768]{1,0:T(8,128)(2,1)S(1)} collective-permute-done((bf16[128,768]{1,0:T(8,128)(2,1)S(1)}, bf16[128,768]{1,0:T(8,128)(2,1)S(1)}, u32[]{:S(2)}, u32[]{:S(2)}) %collective-permute-start.5) | collective-permute-done | bytes 196640 | tf_op jit(solution)/shard_map/ppermute | solution.py:384
  27.0 0.7 %first_columns.1._ = bf16[128,1536]{1,0:T(8,128)(2,1)} custom-call(bf16[128,768]{1,0:T(8,128)(2,1)S(1)} %collective-permute-done.5.part_ref), custom_call_target="tpu_custom_call" | custom-call | tf_op jit(solution)/shard_map/first_columns/pallas_call | solution.py:386
  27.7 2.0 %collective-permute-done.6.part_ref = bf16[128,512]{1,0:T(8,128)(2,1)S(1)} collective-permute-done((bf16[128,512]{1,0:T(8,128)(2,1)S(1)}, bf16[128,512]{1,0:T(8,128)(2,1)S(1)}, u32[]{:S(2)}, u32[]{:S(2)}) %collective-permute-start.6) | collective-permute-done | bytes 131104 | tf_op jit(solution)/shard_map/ppermute | solution.py:384
  29.7 0.7 %other_columns.2._ = bf16[128,1536]{1,0:T(8,128)(2,1)} custom-call(bf16[128,1536]{1,0:T(8,128)(2,1)} %first_columns.1._, bf16[128,512]{1,0:T(8,128)(2,1)S(1)} %collective-permute-done.6.part_ref), custom_call_target="tpu_custom_call", output_to_operand_aliasing={{}: (0, {})} | custom-call | tf_op jit(solution)/shard_map/other_columns/pallas_call | solution.py:396
  30.3 0.0 collective-permute-done.7.part_ref
  30.4 0.6 %other_columns.3 = bf16[128,1536]{1,0:T(8,128)(2,1)} custom-call(bf16[128,1536]{1,0:T(8,128)(2,1)} %other_columns.2._, bf16[128,256]{1,0:T(8,128)(2,1)S(1)} %collective-permute-done.7.part_ref), custom_call_target="tpu_custom_call", output_to_operand_aliasing={{}: (0, {})} | custom-call | tf_op jit(solution)/shard_map/other_columns/pallas_call | solution.py:396
Async XLA Ops:
  0.0 12.6 %collective-permute-start.1 = (bf16[128,1536]{1,0:T(8,128)(2,1)}, bf16[128,1536]{1,0:T(8,128)(2,1)S(1)}, u32[]{:S(2)}, u32[]{:S(2)}) collective-permute-start(bf16[128,1536]{1,0:T(8,128)(2,1)} %bitcast.13), channel_id=1, source_target_pairs={{0,2},{2,0},{4,6},{6,4},{1,3},{3,1},{5,7},{7,5},{8,10},{10,8},{12,... | collective-permute-start | bytes 1179656 | tf_op jit(solution)/shard_map/ppermute | solution.py:276
  3.9 7.5 %collective-permute-start.2 = (bf16[80,1536]{1,0:T(8,128)(2,1)S(1)}, bf16[80,1536]{1,0:T(8,128)(2,1)S(1)}, u32[]{:S(2)}, u32[]{:S(2)}) collective-permute-start(bf16[80,1536]{1,0:T(8,128)(2,1)S(1)} %slice.4), channel_id=1, source_target_pairs={{4,0},{6,2},{0,4},{2,6},{5,1},{7,3},{1,5},{3,7},{12,8},{14,10},{8,... | collective-permute-start | bytes 737288 | tf_op jit(solution)/shard_map/ppermute | solution.py:279
  5.5 8.2 %collective-permute-start = (s32[2,6]{1,0:T(2,128)}, s32[2,6]{1,0:T(2,128)S(1)}, u32[]{:S(2)}, u32[]{:S(2)}) collective-permute-start(s32[2,6]{1,0:T(2,128)} %bitcast.17), channel_id=1, source_target_pairs={{0,2},{2,0},{4,6},{6,4},{1,3},{3,1},{5,7},{7,5},{8,10},{10,8},{12,... | collective-permute-start | bytes 152 | tf_op jit(solution)/shard_map/ppermute | solution.py:276
  10.1 5.2 %collective-permute-start.3 = (bf16[48,1536]{1,0:T(8,128)(2,1)S(1)}, bf16[48,1536]{1,0:T(8,128)(2,1)S(1)}, u32[]{:S(2)}, u32[]{:S(2)}) collective-permute-start(bf16[48,1536]{1,0:T(8,128)(2,1)S(1)} %get-tuple-element.30), channel_id=1, source_target_pairs={{4,0},{6,2},{0,4},{2,6},{5,1},{7,3},{1,5},{3,7},{12,8},{14,10},{8,... | collective-permute-start | bytes 442376 | tf_op jit(solution)/shard_map/ppermute | solution.py:279
  11.4 2.3 %copy-start = (bf16[1,768,1536]{2,1,0:T(8,128)(2,1)S(1)}, bf16[1,768,1536]{2,1,0:T(8,128)(2,1)}, u32[]{:S(2)}) copy-start(bf16[1,768,1536]{2,1,0:T(8,128)(2,1)} %param.8) | copy-start | bytes 7077892
  13.6 1.8 %collective-permute-start.4 = (bf16[128,1536]{1,0:T(8,128)(2,1)S(1)}, bf16[128,1536]{1,0:T(8,128)(2,1)S(1)}, u32[]{:S(2)}, u32[]{:S(2)}) collective-permute-start(bf16[128,1536]{1,0:T(8,128)(2,1)S(1)} %get-tuple-element.25.refs_0_), channel_id=1, source_target_pairs={{0,1},{1,0},{2,3},{3,2},{4,5},{5,4},{6,7},{7,6},{8,9},{9,8},{10,11... | collective-permute-start | bytes 1179656 | tf_op jit(solution)/shard_map/ppermute | solution.py:333
  16.5 10.5 %collective-permute-start.5 = (bf16[128,768]{1,0:T(8,128)(2,1)S(1)}, bf16[128,768]{1,0:T(8,128)(2,1)S(1)}, u32[]{:S(2)}, u32[]{:S(2)}) collective-permute-start(bf16[128,768]{1,0:T(8,128)(2,1)S(1)} %get-tuple-element.31), channel_id=1, source_target_pairs={{0,10},{2,8},{4,14},{6,12},{8,18},{10,16},{12,22},{14,20},{16,26},... | collective-permute-start | bytes 589832 | tf_op jit(solution)/shard_map/ppermute | solution.py:384
  19.1 10.6 %collective-permute-start.6 = (bf16[128,512]{1,0:T(8,128)(2,1)S(1)}, bf16[128,512]{1,0:T(8,128)(2,1)S(1)}, u32[]{:S(2)}, u32[]{:S(2)}) collective-permute-start(bf16[128,512]{1,0:T(8,128)(2,1)S(1)} %finish_rest.2), channel_id=1, source_target_pairs={{0,10},{2,8},{4,14},{6,12},{8,18},{10,16},{12,22},{14,20},{16,26},... | collective-permute-start | bytes 393224 | tf_op jit(solution)/shard_map/ppermute | solution.py:384
  21.2 9.2 %collective-permute-start.7 = (bf16[128,256]{1,0:T(8,128)(2,1)S(1)}, bf16[128,256]{1,0:T(8,128)(2,1)S(1)}, u32[]{:S(2)}, u32[]{:S(2)}) collective-permute-start(bf16[128,256]{1,0:T(8,128)(2,1)S(1)} %finish_rest.3), channel_id=1, source_target_pairs={{0,10},{2,8},{4,14},{6,12},{8,18},{10,16},{12,22},{14,20},{16,26},... | collective-permute-start | bytes 196616 | tf_op jit(solution)/shard_map/ppermute | solution.py:384
